TPU v7x, 32 devices: a whole 2x2x4 slice. The times are simulated.
32 devices in a mesh: groups: 2 (over x), ctx: 16 (over z, y, core).
Axes of the slice: x: 2, y: 2, z: 4, core: 2. Of those that a mesh axis runs over, the one named last changes fastest.
Arguments:
- query_input: bfloat16 [32, 1536], P('groups'), parts along dimension 0, may hold values from -20 to 20
- query_gain: bfloat16 [1536], replicated, may hold values from 0.5 to 1.5
- nope_weight: bfloat16 [1536, 4096], P(None, 'ctx'), may hold values from -0.15625 to 0.15625
- rope_weight: bfloat16 [1536, 2048], P(None, 'ctx'), may hold values from -0.15625 to 0.15625
- key_up: bfloat16 [32, 128, 512], P('ctx'), may hold values from -0.5 to 0.5
- value_up: bfloat16 [32, 512, 128], P('ctx'), may hold values from -1 to 1
- out_weight: bfloat16 [4096, 7168], P('ctx'), may hold values from -0.09375 to 0.09375
- cache_latent: bfloat16 [4, 32768, 512], P('groups', 'ctx'), parts along dimension 0, may hold values from -8 to 8
- cache_rope: bfloat16 [4, 64, 32768], P('groups', None, 'ctx'), parts along dimension 0, may hold values from -256 to 256
- cached_length: int32 [4], P('groups'), parts along dimension 0, may hold values from 16384 to 32760, as said below
Outputs:
- attn_out: bfloat16 [32, 7168], P('groups'), parts along dimension 0
There are 2 independent parts, one for each index of `groups`. A program takes and returns all parts, laid end to end along the dimension named above; an argument that names none is the same for every part. Nothing has to cross between parts.
Inputs may be any that keep to these rules, and one draw needn't show every extreme that they name: `cached_length`: in every part one request has exactly 32760, so that its last new token sees the cache's last position.
All inputs are finite; a program needn't handle non-finite values.
Results may differ from a plain program's by a relative error of at most 0.012.
Values may be sent and summed in bfloat16 or wider, within the bound.
No kernel may reach another device: no remote copies, remote signals or barrier semaphores. Data moves between devices by JAX's collectives and lax.ppermute only.
A program may use at most 128 MiB of HBM per device.

v0:
```python
import math

import jax
import jax.numpy as jnp
from jax import lax
from jax.sharding import PartitionSpec as P

mscale_yarn = 1.0 + 0.1 * math.log(40.0)
masked_score = -1e30


def attend_heads(
    latent_query, rope_query, cache_latent, cache_rope, cached_length, positions, softmax_scale
):
    row_count, head_count, latent_width = latent_query.shape
    rope_width = rope_query.shape[2]
    requests = cache_latent.shape[0]
    stretch_rows = row_count // requests
    peak_list, sum_list, pool_list = ([], [], [])
    for request in range(requests):
        flat_latent = latent_query[request * stretch_rows : (request + 1) * stretch_rows].reshape(
            stretch_rows * head_count, latent_width
        )
        flat_rope = rope_query[request * stretch_rows : (request + 1) * stretch_rows].reshape(
            stretch_rows * head_count, rope_width
        )
        scores = jnp.einsum(
            "ql,pl->qp", flat_latent, cache_latent[request], preferred_element_type=jnp.float32
        )
        scores = (
            scores + jnp.dot(flat_rope, cache_rope[request], preferred_element_type=jnp.float32)
        ) * softmax_scale
        last_seen = (
            cached_length[request]
            + jnp.arange(stretch_rows * head_count, dtype=jnp.int32) // head_count
        )
        visible = positions[None, :] <= last_seen[:, None]
        scores = jnp.where(visible, scores, masked_score)
        block_peak = jnp.max(scores, axis=1)
        weights = jnp.where(visible, jnp.exp(scores - block_peak[:, None]), 0.0)
        block_sum = jnp.sum(weights, axis=1)
        block_pool = jnp.dot(
            weights.astype(jnp.bfloat16), cache_latent[request], preferred_element_type=jnp.float32
        )
        peak_list.append(block_peak.reshape(stretch_rows, head_count))
        sum_list.append(block_sum.reshape(stretch_rows, head_count))
        pool_list.append(block_pool.reshape(stretch_rows, head_count, latent_width))
    return (
        jnp.concatenate(peak_list, axis=0),
        jnp.concatenate(sum_list, axis=0),
        jnp.concatenate(pool_list, axis=0),
    )


def project_heads(pooled, weight_sum, value_up, out_weight):
    attended = (pooled / weight_sum[:, :, None]).astype(jnp.bfloat16)
    head_values = jnp.einsum(
        "rhl,hlv->rhv", attended, value_up, preferred_element_type=jnp.float32
    ).astype(jnp.bfloat16)
    return jnp.dot(
        head_values.reshape(head_values.shape[0], -1),
        out_weight,
        preferred_element_type=jnp.float32,
    )


def local(
    query_input,
    query_gain,
    nope_weight,
    rope_weight,
    key_up,
    value_up,
    out_weight,
    cache_latent,
    cache_rope,
    cached_length,
):
    head_local = key_up.shape[0]
    nope_width = key_up.shape[1]
    rope_width = rope_weight.shape[1] // head_local
    row_count = query_input.shape[0]
    key_count = cache_latent.shape[1]
    widened = query_input.astype(jnp.float32)
    normed = (
        widened
        * lax.rsqrt(jnp.mean(widened * widened, axis=-1, keepdims=True) + 1e-06)
        * query_gain.astype(jnp.float32)
    ).astype(jnp.bfloat16)
    query_nope = (
        jnp.dot(normed, nope_weight, preferred_element_type=jnp.float32)
        .astype(jnp.bfloat16)
        .reshape(row_count, head_local, nope_width)
    )
    query_rope = (
        jnp.dot(normed, rope_weight, preferred_element_type=jnp.float32)
        .astype(jnp.bfloat16)
        .reshape(row_count, head_local, rope_width)
    )
    query_latent = jnp.einsum(
        "rhn,hnl->rhl", query_nope, key_up, preferred_element_type=jnp.float32
    ).astype(jnp.bfloat16)
    softmax_scale = mscale_yarn * mscale_yarn / math.sqrt(nope_width + rope_width)
    positions = lax.axis_index("ctx") * key_count + jnp.arange(key_count, dtype=jnp.int32)
    every_latent, every_rope = (
        lax.all_gather(query_latent, "ctx", axis=1, tiled=True),
        lax.all_gather(query_rope, "ctx", axis=1, tiled=True),
    )
    block_peak, block_sum, block_pool = attend_heads(
        every_latent, every_rope, cache_latent, cache_rope, cached_length, positions, softmax_scale
    )
    pooled_in = lax.all_to_all(block_pool[None], "ctx", split_axis=2, concat_axis=0, tiled=True)
    peak_in = lax.all_to_all(block_peak[None], "ctx", split_axis=2, concat_axis=0, tiled=True)
    sum_in = lax.all_to_all(block_sum[None], "ctx", split_axis=2, concat_axis=0, tiled=True)
    row_top = jnp.max(peak_in, axis=0)
    factor = jnp.exp(peak_in - row_top[None])
    pooled = jnp.sum(pooled_in * factor[..., None], axis=0)
    weight_sum = jnp.sum(sum_in * factor, axis=0)
    partial_value = project_heads(pooled, weight_sum, value_up, out_weight)
    return lax.psum(partial_value, "ctx").astype(jnp.bfloat16)


def solution(mesh):
    placed = (
        P("groups", None),
        P(),
        P(None, "ctx"),
        P(None, "ctx"),
        P("ctx", None, None),
        P("ctx", None, None),
        P("ctx", None),
        P("groups", "ctx", None),
        P("groups", None, "ctx"),
        P("groups"),
    )
    return jax.shard_map(
        local, mesh=mesh, in_specs=placed, out_specs=P("groups", None), check_vma=False
    )
```

profile of v0, /device:TPU:0, one launch (start us, length us, event | category | flops | bytes accessed | tf_op | source)
XLA Modules:
  0.0 175.3 jit_solution(12115778293265833145)
XLA Ops:
  0.0 0.0 copy-start
  0.0 0.0 copy-start.4
  0.0 1.4 fusion.44
  1.4 0.7 convert_element_type.40
  2.1 0.9 fusion.28
  3.1 0.0 copy-done
  3.1 1.1 fusion.21
  4.1 1.1 fusion.20
  5.2 24.6 %all_gather.6 = bf16[16,32,512]{2,0,1:T(8,128)(2,1)S(1)} all-gather(bf16[16,2,512]{2,0,1:T(8,128)(2,1)S(1)} %fusion.20), channel_id=1, replica_groups=mesh['groups'=2,'ctx'=16] {'ctx'}, dimensions={1}, use_global_device_ids=true | all-gather | bytes 557056 | tf_op jit(solution)/shard_map/all_gather | solution.py:106
  29.8 0.1 copy.76
  29.9 0.0 copy-done.4
  29.9 0.0 copy-done.5
  29.9 0.2 convolution_convert_fusion.3
  30.2 0.1 reshape.79
  30.3 17.8 %all_gather.7 = bf16[16,32,64]{2,0,1:T(8,128)(2,1)S(1)} all-gather(bf16[16,2,64]{2,0,1:T(8,128)(2,1)S(1)} %copy.64), channel_id=1, replica_groups=mesh['groups'=2,'ctx'=16] {'ctx'}, dimensions={1}, use_global_device_ids=true | all-gather | bytes 69632 | tf_op jit(solution)/shard_map/all_gather | solution.py:107
  48.1 0.1 copy.75
  48.2 0.0 copy-start.1
  48.2 2.5 %fusion.6 = f32[256,2048]{1,0:T(8,128)S(1)} fusion(bf16[256,512]{1,0:T(8,128)(2,1)S(1)} %bitcast.80, bf16[2,2048,512]{2,1,0:T(8,128)(2,1)} %param.17), kind=kOutput, calls=%fused_computation.10 | convolution fusion | flops 536870912 | bytes 4456448 | tf_op jit(solution)/shard_map/ql,pl->qp/dot_general | solution.py:27
  50.7 0.3 copy-done.1
  51.0 0.7 fusion.10
  51.8 1.3 broadcast_add_fusion
  53.1 0.0 copy-done.3
  53.1 0.6 fusion.46
  53.8 0.6 fusion.45
  54.4 1.0 fusion.16
  55.4 0.1 reshape.85
  55.5 0.1 reshape.86
  55.6 0.7 copy.72
  56.3 3.5 %all-to-all-start.2 = ((f32[1,16,32]{1,0,2:T(1,128)}), f32[1,16,32]{1,0,2:T(1,128)S(1)}, u32[]{:S(2)}, u32[]{:S(2)}) async-start(f32[1,16,32]{1,0,2:T(1,128)} %copy.72), calls=%async_computation.2 | async-start | bytes 32768 | tf_op jit(solution)/shard_map/all_to_all | solution.py:114
  59.8 0.1 reshape.84
  59.9 0.1 reshape.83
  59.9 2.4 %fusion.4 = f32[8,32,512]{2,1,0:T(8,128)S(1)} fusion(bf16[8,32,2048]{2,1,0:T(8,128)(2,1)S(1)} %bitcast.79, bf16[2,2048,512]{2,1,0:T(8,128)(2,1)} %param.17), kind=kOutput, calls=%fused_computation.8 | convolution fusion | flops 536870912 | bytes 3670016 | tf_op jit(solution)/shard_map/dot_general | solution.py:42
  62.4 0.4 copy-done.2
  62.8 0.7 fusion.8
  63.5 0.7 copy.70
  64.2 2.1 %all-to-all-done.2 = f32[1,16,32]{1,0,2:T(1,128)S(1)} async-done(((f32[1,16,32]{1,0,2:T(1,128)}), f32[1,16,32]{1,0,2:T(1,128)S(1)}, u32[]{:S(2)}, u32[]{:S(2)}) %all-to-all-start.2) | async-done | bytes 2080 | tf_op jit(solution)/shard_map/all_to_all | solution.py:114
  66.2 3.9 %all-to-all-start.1 = ((f32[1,16,32]{1,0,2:T(1,128)}), f32[1,16,32]{1,0,2:T(1,128)S(1)}, u32[]{:S(2)}, u32[]{:S(2)}) async-start(f32[1,16,32]{1,0,2:T(1,128)} %copy.70), calls=%async_computation.1 | async-start | bytes 32768 | tf_op jit(solution)/shard_map/all_to_all | solution.py:113
  70.1 0.1 maximum_bitcast_fusion
  70.2 1.6 copy.68
  71.8 4.8 %all-to-all-done.1 = f32[1,16,32]{1,0,2:T(1,128)S(1)} async-done(((f32[1,16,32]{1,0,2:T(1,128)}), f32[1,16,32]{1,0,2:T(1,128)S(1)}, u32[]{:S(2)}, u32[]{:S(2)}) %all-to-all-start.1) | async-done | bytes 2080 | tf_op jit(solution)/shard_map/all_to_all | solution.py:113
  76.6 3.7 %all-to-all-start = ((f32[1,16,32,512]{3,1,0,2:T(8,128)}), f32[1,16,32,512]{3,1,0,2:T(8,128)S(1)}, u32[]{:S(2)}, u32[]{:S(2)}) async-start(f32[1,16,32,512]{3,1,0,2:T(8,128)} %copy.68), calls=%async_computation | async-start | bytes 2097152 | tf_op jit(solution)/shard_map/all_to_all | solution.py:112
  80.4 0.2 copy.71
  80.5 22.7 %all-to-all-done = f32[1,16,32,512]{3,1,0,2:T(8,128)S(1)} async-done(((f32[1,16,32,512]{3,1,0,2:T(8,128)}), f32[1,16,32,512]{3,1,0,2:T(8,128)S(1)}, u32[]{:S(2)}, u32[]{:S(2)}) %all-to-all-start) | async-done | bytes 1048608 | tf_op jit(solution)/shard_map/all_to_all | solution.py:112
  103.2 1.1 fusion.23
  104.3 0.0 copy-done.6
  104.3 0.2 fusion.22
  104.5 2.6 %fusion.36 = f32[16,7168]{1,0:T(8,128)S(1)} fusion(bf16[256,7168]{1,0:T(8,128)(2,1)} %param.16, bf16[2,2,8,128]{3,2,1,0:T(8,128)(2,1)S(1)} %fusion.22), kind=kOutput, calls=%fused_computation.48 | convolution fusion | flops 58720256 | bytes 4136960 | tf_op jit(solution)/shard_map/dot_general | solution.py:60
  107.1 68.1 %all-reduce.1 = bf16[16,7168]{1,0:T(8,128)(2,1)} all-reduce(f32[16,7168]{1,0:T(8,128)S(1)} %fusion.36), channel_id=1, replica_groups=mesh['groups'=2,'ctx'=16] {'ctx'}, use_global_device_ids=true, to_apply=%region_8.9 | all-reduce | flops 114688 | bytes 688128 | tf_op jit(solution)/shard_map/psum | solution.py:120
  (15 shorter events, 0.2 us)
Async XLA Ops:
  0.0 3.1 %copy-start = (bf16[1536,256]{1,0:T(8,128)(2,1)S(1)}, bf16[1536,256]{1,0:T(8,128)(2,1)}, u32[]{:S(2)}) copy-start(bf16[1536,256]{1,0:T(8,128)(2,1)} %param.12) | copy-start | bytes 2359300
  0.0 29.9 %copy-start.4 = (bf16[16,1536]{1,0:T(8,128)(2,1)S(1)}, bf16[16,1536]{1,0:T(8,128)(2,1)}, u32[]{:S(2)}) copy-start(bf16[16,1536]{1,0:T(8,128)(2,1)} %param.10) | copy-start | bytes 147460
  0.0 29.9 %copy-start.5 = (bf16[1536,128]{1,0:T(8,128)(2,1)S(1)}, bf16[1536,128]{1,0:T(8,128)(2,1)}, u32[]{:S(2)}) copy-start(bf16[1536,128]{1,0:T(8,128)(2,1)} %param.13) | copy-start | bytes 1179652
  48.2 2.8 %copy-start.1 = (bf16[2,2048,512]{2,1,0:T(8,128)(2,1)S(1)}, bf16[2,2048,512]{2,1,0:T(8,128)(2,1)}, u32[]{:S(2)}) copy-start(bf16[2,2048,512]{2,1,0:T(8,128)(2,1)} %param.17) | copy-start | bytes 12582916
  51.0 2.1 %copy-start.3 = (bf16[2,64,2048]{2,1,0:T(8,128)(2,1)S(1)}, bf16[2,64,2048]{2,1,0:T(8,128)(2,1)}, u32[]{:S(2)}) copy-start(bf16[2,64,2048]{2,1,0:T(8,128)(2,1)} %param.18) | copy-start | bytes 1572868
  56.3 10.0 %all-to-all-start.2 = ((f32[1,16,32]{1,0,2:T(1,128)}), f32[1,16,32]{1,0,2:T(1,128)S(1)}, u32[]{:S(2)}, u32[]{:S(2)}) async-start(f32[1,16,32]{1,0,2:T(1,128)} %copy.72), calls=%async_computation.2 | async-start | bytes 32768 | tf_op jit(solution)/shard_map/all_to_all | solution.py:114
  59.9 2.8 %copy-start.2 = (bf16[2,2048,512]{2,1,0:T(8,128)(2,1)S(1)}, bf16[2,2048,512]{2,1,0:T(8,128)(2,1)}, u32[]{:S(2)}) copy-start(bf16[2,2048,512]{2,1,0:T(8,128)(2,1)} %param.17) | copy-start | bytes 12582916
  66.2 10.4 %all-to-all-start.1 = ((f32[1,16,32]{1,0,2:T(1,128)}), f32[1,16,32]{1,0,2:T(1,128)S(1)}, u32[]{:S(2)}, u32[]{:S(2)}) async-start(f32[1,16,32]{1,0,2:T(1,128)} %copy.70), calls=%async_computation.1 | async-start | bytes 32768 | tf_op jit(solution)/shard_map/all_to_all | solution.py:113
  71.8 32.5 %copy-start.6 = (bf16[2,512,128]{2,1,0:T(8,128)(2,1)S(1)}, bf16[2,512,128]{2,1,0:T(8,128)(2,1)}, u32[]{:S(2)}) copy-start(bf16[2,512,128]{2,1,0:T(8,128)(2,1)} %param.15) | copy-start | bytes 786436
  76.6 26.6 %all-to-all-start = ((f32[1,16,32,512]{3,1,0,2:T(8,128)}), f32[1,16,32,512]{3,1,0,2:T(8,128)S(1)}, u32[]{:S(2)}, u32[]{:S(2)}) async-start(f32[1,16,32,512]{3,1,0,2:T(8,128)} %copy.68), calls=%async_computation | async-start | bytes 2097152 | tf_op jit(solution)/shard_map/all_to_all | solution.py:112
where the time goes:
time: 176 us; the launch traced here: 175 us
  blocking collectives  111 us (63%)
  waiting for transfers between devices  29.5 us (17%)
  matrix products  12.8 us (7%)
  starting transfers between devices  11 us (6%)
  local copies, waits for them, and re-layouts  5.92 us (3%)
  other arithmetic  5.27 us (3%)
    psum x1, blocking collectives, local(): return lax.psum(partial_value, 'ctx').astype(jnp.bfloat16)  68.1 us
    all_gather x1, blocking collectives, local(): lax.all_gather(query_latent, 'ctx', axis=1, tiled=True)  24.6 us
    all_to_all x1, waiting for transfers between devices, local(): lax.all_to_all(block_pool[None], 'ctx', split_axis=2, concat_axis=0, tile...  22.7 us
    all_gather x1, blocking collectives, local(): lax.all_gather(query_rope, 'ctx', axis=1, tiled=True)  17.8 us
    all_to_all x1, waiting for transfers between devices, local(): lax.all_to_all(block_peak[None], 'ctx', split_axis=2, concat_axis=0, tile...  4.8 us
    all_to_all x1, starting transfers between devices, local(): lax.all_to_all(block_peak[None], 'ctx', split_axis=2, concat_axis=0, tile...  3.88 us
    all_to_all x1, starting transfers between devices, local(): lax.all_to_all(block_pool[None], 'ctx', split_axis=2, concat_axis=0, tile...  3.65 us
  transfers between devices with their start and end apart: 3, of which 3 were waited for; matrix products, arithmetic and copies ran while one was open for 3% of the time, Pallas kernels for 0%

commit v1 on v0

v1 whole, which is shorter than its diff:
```python
import functools
import math

import jax
import jax.numpy as jnp
from jax import lax
from jax.experimental import pallas as pl
from jax.experimental.pallas import tpu as pltpu
from jax.sharding import PartitionSpec as P

mscale_yarn = 1.0 + 0.1 * math.log(40.0)
masked_score = -1e30
LOG2E = 1.4426950408889634
LANES = 128
F32 = jnp.float32
BF16 = jnp.bfloat16


def stage_list(count):
    stages, stride = [], 1
    while stride < count:
        left = count // stride
        radix = 2 if (stride < 4 or left < 4) else 4
        stages.append((stride, radix))
        stride *= radix
    return stages


def swap(x, count, mask):
    return lax.ppermute(x, "ctx", [(i, i ^ mask) for i in range(count)])


def call(body, outs, operands, *, flops=0, smem=(), name=None, limit=40 << 20):
    specs = [
        pl.BlockSpec(memory_space=pltpu.SMEM if i in smem else pltpu.VMEM)
        for i in range(len(operands))
    ]
    total = sum(o.size * o.dtype.itemsize for o in list(outs) + list(operands))
    return pl.pallas_call(
        body,
        out_shape=tuple(outs),
        in_specs=specs,
        out_specs=tuple(pl.BlockSpec(memory_space=pltpu.VMEM) for _ in outs),
        compiler_params=pltpu.CompilerParams(vmem_limit_bytes=limit),
        cost_estimate=pl.CostEstimate(flops=flops, bytes_accessed=total, transcendentals=0),
        name=name,
    )(*operands)


def spec(shape, dtype):
    return jax.ShapeDtypeStruct(shape, dtype)


def query_body(heads, reqs, x_ref, gain_ref, nope_ref, rope_ref, key_ref, out_ref):
    rows = x_ref.shape[0]
    stretch = rows // reqs
    nope_width, latent = key_ref.shape[1], key_ref.shape[2]
    rope_width = rope_ref.shape[1] // heads
    x = x_ref[...].astype(F32)
    mean = jnp.mean(x * x, axis=-1, keepdims=True)
    normed = (x * lax.rsqrt(mean + 1e-06) * gain_ref[...].astype(F32)).astype(BF16)
    nope = jnp.dot(normed, nope_ref[...], preferred_element_type=F32).astype(BF16)
    rope = jnp.dot(normed, rope_ref[...], preferred_element_type=F32)
    lat = [
        jnp.dot(
            nope[:, h * nope_width : (h + 1) * nope_width], key_ref[h], preferred_element_type=F32
        )
        for h in range(heads)
    ]
    ropes = []
    for b in range(reqs):
        part = slice(b * stretch, (b + 1) * stretch)
        rows_b = jnp.concatenate([lat[h][part] for h in range(heads)], axis=0)
        out_ref[:, b * latent : (b + 1) * latent] = rows_b.astype(BF16)
        ropes.append(
            jnp.concatenate(
                [rope[part, h * rope_width : (h + 1) * rope_width] for h in range(heads)], axis=0
            )
        )
    out_ref[:, reqs * latent :] = jnp.concatenate(ropes, axis=1).astype(BF16)


def pack_stats(columns):
    rows = columns[0].shape[0]
    lane = lax.broadcasted_iota(jnp.int32, (rows, LANES), 1)
    out = jnp.zeros((rows, LANES), F32)
    for b, column in enumerate(columns):
        high = column.astype(BF16).astype(F32)
        rest = column - high
        mid = rest.astype(BF16).astype(F32)
        low = rest - mid
        for k, term in enumerate((high, mid, low)):
            out = jnp.where(lane == 3 * b + k, term, out)
    return out


def read_stats(stats, b):
    return (stats[:, 3 * b : 3 * b + 1] + stats[:, 3 * b + 1 : 3 * b + 2]) + stats[
        :, 3 * b + 2 : 3 * b + 3
    ]


def merge(parts, reqs, latent):
    tops = []
    pooled = []
    for b in range(reqs):
        lse = [read_stats(p[:, reqs * latent :], b) for p in parts]
        top = functools.reduce(jnp.maximum, lse)
        weight = [jnp.exp(m - top) for m in lse]
        total = functools.reduce(jnp.add, weight)
        inverse = 1.0 / total
        value = functools.reduce(
            jnp.add,
            [p[:, b * latent : (b + 1) * latent] * (w * inverse) for p, w in zip(parts, weight)],
        )
        pooled.append(value)
        tops.append(top + jnp.log(total))
    return pooled, tops


def attend_body(
    n_q, reqs, latent, rope_width, stretch, scale, chunk, *refs
):
    length_ref, q_refs = refs[0], refs[1 : 1 + n_q]
    lat_ref, rope_ref = refs[1 + n_q], refs[2 + n_q]
    keep_ref, send_ref = refs[3 + n_q], refs[4 + n_q]
    q_s, s_s = refs[5 + n_q], refs[6 + n_q]
    rows = q_s.shape[0]
    half = rows // 2
    keys = lat_ref.shape[1]
    at = 0
    for q in q_refs:
        q_s[at : at + q.shape[0], :] = q[...]
        at += q.shape[0]
    first_key = lax.axis_index("ctx") * keys
    block = min(rows, 256)
    for r0 in range(0, rows, block):
        rs = slice(r0, r0 + block)
        stats = []
        for b in range(reqs):
            seen = (
                length_ref[b]
                - first_key
                + lax.broadcasted_iota(jnp.int32, (stretch, chunk), 0)
            )
            lane = lax.broadcasted_iota(jnp.int32, (stretch, chunk), 1)
            lhs = q_s[rs, b * latent : (b + 1) * latent]
            base = reqs * latent + b * rope_width
            lhs_rope = q_s[rs, base : base + rope_width]
            peak = None
            for k0 in range(0, keys, chunk):
                s = lax.dot_general(
                    lhs,
                    lat_ref[b, k0 : k0 + chunk, :],
                    (((1,), (1,)), ((), ())),
                    preferred_element_type=F32,
                ) + jnp.dot(
                    lhs_rope, rope_ref[b, :, k0 : k0 + chunk], preferred_element_type=F32
                )
                visible = (lane + k0) <= seen
                s = jnp.where(
                    visible[None], s.reshape(block // stretch, stretch, chunk), masked_score
                ).reshape(block, chunk)
                s_s[b, :, k0 : k0 + chunk] = s
                top = jnp.max(s, axis=1, keepdims=True)
                peak = top if peak is None else jnp.maximum(peak, top)
            total, pool = None, None
            for k0 in range(0, keys, chunk):
                w = jnp.exp2((s_s[b, :, k0 : k0 + chunk] - peak) * (scale * LOG2E))
                part = jnp.sum(w, axis=1, keepdims=True)
                term = jnp.dot(
                    w.astype(BF16), lat_ref[b, k0 : k0 + chunk, :], preferred_element_type=F32
                )
                total = part if total is None else total + part
                pool = term if pool is None else pool + term
            pool = pool * (1.0 / total)
            stats.append(peak * scale + jnp.log(total))
            cols = slice(b * latent, (b + 1) * latent)
            for lo in range(r0, r0 + block, min(block, half)):
                size = min(block, half)
                piece = pool[lo - r0 : lo - r0 + size]
                if lo < half:
                    keep_ref[lo : lo + size, cols] = piece
                else:
                    send_ref[lo - half : lo - half + size, cols] = piece.astype(BF16)
        packed = pack_stats(stats)
        for lo in range(r0, r0 + block, min(block, half)):
            size = min(block, half)
            piece = packed[lo - r0 : lo - r0 + size]
            if lo < half:
                keep_ref[lo : lo + size, reqs * latent :] = piece
            else:
                send_ref[lo - half : lo - half + size, reqs * latent :] = piece.astype(BF16)


def merge_body(n_in, reqs, latent, *refs):
    parts = [r[...].astype(F32) for r in refs[:n_in]]
    outs = refs[n_in:]
    pooled, tops = merge(parts, reqs, latent)
    packed = pack_stats(tops)
    size = outs[0].shape[0]
    for j, out in enumerate(outs):
        rows = slice(j * size, (j + 1) * size)
        for b in range(reqs):
            out[:, b * latent : (b + 1) * latent] = pooled[b][rows].astype(out.dtype)
        out[:, reqs * latent :] = packed[rows].astype(out.dtype)


def project_body(n_in, reqs, heads, latent, parts_out, *refs):
    parts = [r[...].astype(F32) for r in refs[:n_in]]
    value_ref, weight_ref = refs[n_in], refs[n_in + 1]
    keep_ref, send_ref = refs[n_in + 2], refs[n_in + 3]
    pooled, _ = merge(parts, reqs, latent)
    stretch = pooled[0].shape[0] // heads
    values = []
    for h in range(heads):
        rows = jnp.concatenate([p[h * stretch : (h + 1) * stretch] for p in pooled], axis=0)
        values.append(
            jnp.dot(rows.astype(BF16), value_ref[h], preferred_element_type=F32).astype(BF16)
        )
    hidden = jnp.concatenate(values, axis=1)
    mine = lax.rem(lax.axis_index("ctx"), parts_out)
    width = weight_ref.shape[1] // parts_out
    for e in range(parts_out):
        start = pl.multiple_of(jnp.bitwise_xor(mine, e) * width, LANES)
        out = jnp.dot(hidden, weight_ref[:, pl.ds(start, width)], preferred_element_type=F32)
        slot = slice((e // 2) * width, (e // 2 + 1) * width)
        if e % 2 == 0:
            keep_ref[:, slot] = out
        else:
            send_ref[:, slot] = out.astype(BF16)


def place_body(parts_out, *refs):
    pieces, out_ref = refs[:-1], refs[-1]
    mine = lax.rem(lax.axis_index("ctx"), parts_out)
    width = out_ref.shape[1] // parts_out
    e_order = (0, 2, 1, 3)
    at = 0
    for piece in pieces:
        for k in range(piece.shape[1] // width):
            start = pl.multiple_of(jnp.bitwise_xor(mine, e_order[at]) * width, LANES)
            out_ref[:, pl.ds(start, width)] = piece[:, k * width : (k + 1) * width]
            at += 1


def local(count, query_input, query_gain, nope_weight, rope_weight, key_up, value_up, out_weight,
          cache_latent, cache_rope, cached_length):
    heads, nope_width, latent = key_up.shape
    reqs = cache_latent.shape[0]
    rope_width = cache_rope.shape[1]
    rows = query_input.shape[0]
    stretch = rows // reqs
    own = heads * stretch
    width = reqs * latent + LANES
    stages = stage_list(count)
    scale = mscale_yarn * mscale_yarn / math.sqrt(nope_width + rope_width)

    (query,) = call(
        functools.partial(query_body, heads, reqs),
        [spec((own, width), BF16)],
        [query_input, query_gain[None], nope_weight, rope_weight, key_up],
        name="query",
    )
    held = query
    for stride, radix in reversed(stages[2:]):
        got = [swap(held, count, j * stride) for j in range(1, radix)]
        held = jnp.concatenate([held] + got, axis=0)
    beside = swap(held, count, stages[1][0])
    near = jnp.concatenate([held, beside], axis=0)
    far = swap(near, count, stages[0][0])

    half = near.shape[0]
    total = 2 * half
    block = min(total, 256)
    operands = [cached_length, near, far, cache_latent, cache_rope]
    keep, send = pl.pallas_call(
        functools.partial(attend_body, 2, reqs, latent, rope_width, stretch, scale, 512),
        out_shape=(spec((half, width), F32), spec((half, width), BF16)),
        in_specs=[pl.BlockSpec(memory_space=pltpu.SMEM)]
        + [pl.BlockSpec(memory_space=pltpu.VMEM)] * 4,
        out_specs=(pl.BlockSpec(memory_space=pltpu.VMEM),) * 2,
        scratch_shapes=[
            pltpu.VMEM((total, width), BF16),
            pltpu.VMEM((reqs, block, cache_latent.shape[1]), F32),
        ],
        compiler_params=pltpu.CompilerParams(vmem_limit_bytes=48 << 20),
        cost_estimate=pl.CostEstimate(
            flops=4 * total * cache_latent.shape[1] * latent * reqs,
            bytes_accessed=8 << 20,
            transcendentals=0,
        ),
        name="attend",
    )(*operands)

    got = [swap(send, count, stages[0][0])]
    for stride, radix in stages[1:]:
        size = keep.shape[0] // radix
        pieces = call(
            functools.partial(merge_body, 1 + len(got), reqs, latent),
            [spec((size, width), F32)] + [spec((size, width), BF16)] * (radix - 1),
            [keep] + got,
            name="merge",
        )
        keep = pieces[0]
        got = [swap(p, count, j * stride) for j, p in enumerate(pieces[1:], 1)]

    parts_out = 4
    model = out_weight.shape[1]
    quarter = model // parts_out
    keep, send = call(
        functools.partial(project_body, 1 + len(got), reqs, heads, latent, parts_out),
        [spec((rows, 2 * quarter), F32), spec((rows, 2 * quarter), BF16)],
        [keep] + got + [value_up, out_weight],
        name="project",
    )
    kept = keep + swap(send, count, stages[0][0]).astype(F32)
    kept = kept[:, :quarter] + swap(kept[:, quarter:].astype(BF16), count, stages[1][0]).astype(F32)
    for stride, radix in stages[2:]:
        mine = kept.astype(BF16)
        terms = [mine.astype(F32)] + [
            swap(mine, count, j * stride).astype(F32) for j in range(1, radix)
        ]
        while len(terms) > 1:
            terms = [terms[i] + terms[i + 1] for i in range(0, len(terms), 2)]
        kept = terms[0]
    done = kept.astype(BF16)
    both = jnp.concatenate([done, swap(done, count, stages[1][0])], axis=1)
    other = swap(both, count, stages[0][0])
    (out,) = call(
        functools.partial(place_body, parts_out),
        [spec((rows, model), BF16)],
        [both, other],
        name="place",
    )
    return out


def solution(mesh):
    placed = (
        P("groups", None),
        P(),
        P(None, "ctx"),
        P(None, "ctx"),
        P("ctx", None, None),
        P("ctx", None, None),
        P("ctx", None),
        P("groups", "ctx", None),
        P("groups", None, "ctx"),
        P("groups"),
    )
    return jax.shard_map(
        functools.partial(local, mesh.shape["ctx"]),
        mesh=mesh,
        in_specs=placed,
        out_specs=P("groups", None),
        check_vma=False,
    )
```

time: 176 us -> 67.3 us (0.38)
  blocking collectives: 111 us -> 0 us
  matrix products: 12.8 us -> 0 us
  starting transfers between devices: 11 us -> 21.4 us
  Pallas kernels: 0 us -> 6.9 us
  other arithmetic: 5.27 us -> 0.09 us
  local copies, waits for them, and re-layouts: 5.92 us -> 8.52 us
    psum x1 -> x0, blocking collectives: 68.1 us -> none  [local(): return lax.psum(partial_value, 'ctx').astype(jnp.bfloat16)]
    all_gather x2 -> x0, blocking collectives: 42.4 us -> none  [the longest x1 24.6 us: local(): lax.all_gather(query_latent, 'ctx', axis=1, tiled=True)]
    ppermute x0 -> x17, waiting for transfers between devices: none -> 29.9 us  [swap(): return lax.ppermute(x, 'ctx', [(i, i ^ mask) for i in range(count)])]
    all_to_all x3 -> x0, waiting for transfers between devices: 29.5 us -> none  [the longest x1 22.7 us: local(): lax.all_to_all(block_pool[None], 'ctx', split_axis=2, concat_axis=0, tile...]
    ppermute x0 -> x17, starting transfers between devices: none -> 21.4 us  [swap(): return lax.ppermute(x, 'ctx', [(i, i ^ mask) for i in range(count)])]
    dot_general x11 -> x0, matrix products: 12.8 us -> none  [the longest x2 3.21 us: attend_heads(): jnp.einsum('ql,pl->qp', flat_latent, cache_latent[request], preferred_ele...]
    all_to_all x3 -> x0, starting transfers between devices: 11 us -> none  [the longest x1 3.88 us: local(): lax.all_to_all(block_peak[None], 'ctx', split_axis=2, concat_axis=0, tile...]
    unnamed x16 -> x22, local copies, waits for them, and re-layouts: 0.88 us -> 7.8 us
  transfers between devices with their start and end apart: 3 -> 17, of which waited for: 3 -> 14; matrix products, arithmetic and copies ran while one was open for 3% -> 0% of each run, Pallas kernels for 0% -> 0%
where the time goes in v1:
time: 67.3 us; the launch traced here: 66.9 us
  waiting for transfers between devices  29.9 us (44%)
  starting transfers between devices  21.4 us (32%)
  local copies, waits for them, and re-layouts  8.52 us (13%)
  Pallas kernels  6.9 us (10%)
    ppermute x17, waiting for transfers between devices, swap(): return lax.ppermute(x, 'ctx', [(i, i ^ mask) for i in range(count)])  29.9 us
    ppermute x17, starting transfers between devices, swap(): return lax.ppermute(x, 'ctx', [(i, i ^ mask) for i in range(count)])  21.4 us
    unnamed x22, local copies, waits for them, and re-layouts  7.8 us
    pallas_call x1, Pallas kernels, local(): pl.pallas_call(functools.partial(attend_body, 2, reqs, latent, rope_width...  4.19 us
    pallas_call x5, Pallas kernels, call(): pl.pallas_call(body, out_shape=tuple(outs), in_specs=specs, out_specs=tup...  2.71 us
  transfers between devices with their start and end apart: 17, of which 14 were waited for; matrix products, arithmetic and copies ran while one was open for 0% of the time, Pallas kernels for 0%

profile of v1, /device:TPU:0, one launch (start us, length us, event | category | flops | bytes accessed | tf_op | source)
XLA Modules:
  0.0 66.9 jit_solution(6173942582113689793)
XLA Ops:
  0.0 0.7 %broadcast_in_dim.3.gain_ref = bf16[1,1536]{1,0:T(2,128)(2,1)S(1)} reshape(bf16[1536]{0:T(1024)(128)(2,1)} %param.11) | data formatting | bytes 6144 | tf_op jit(solution)/shard_map/broadcast_in_dim | solution.py:262
  0.7 1.1 %copy-done.1 = bf16[1536,256]{1,0:T(8,128)(2,1)S(1)} copy-done((bf16[1536,256]{1,0:T(8,128)(2,1)S(1)}, bf16[1536,256]{1,0:T(8,128)(2,1)}, u32[]{:S(2)}) %copy-start.1) | copy-done | bytes 786456
  1.8 1.0 %copy-done.2 = bf16[1536,128]{1,0:T(8,128)(2,1)S(1)} copy-done((bf16[1536,128]{1,0:T(8,128)(2,1)S(1)}, bf16[1536,128]{1,0:T(8,128)(2,1)}, u32[]{:S(2)}) %copy-start.2) | copy-done | bytes 393240
  2.8 0.9 %copy-done.4 = bf16[2,128,512]{2,1,0:T(8,128)(2,1)S(1)} copy-done((bf16[2,128,512]{2,1,0:T(8,128)(2,1)S(1)}, bf16[2,128,512]{2,1,0:T(8,128)(2,1)}, u32[]{:S(2)}) %copy-start.4) | copy-done | bytes 262168
  3.8 0.8 %copy-done.5 = bf16[16,1536]{1,0:T(8,128)(2,1)S(1)} copy-done((bf16[16,1536]{1,0:T(8,128)(2,1)S(1)}, bf16[16,1536]{1,0:T(8,128)(2,1)}, u32[]{:S(2)}) %copy-start.5) | copy-done | bytes 49176
  4.6 0.5 query.1
  5.1 5.1 %collective-permute-start.2 = (bf16[16,1152]{1,0:T(8,128)(2,1)S(1)}, bf16[16,1152]{1,0:T(8,128)(2,1)S(1)}, u32[]{:S(2)}, u32[]{:S(2)}) collective-permute-start(bf16[16,1152]{1,0:T(8,128)(2,1)S(1)} %query.1), channel_id=1, source_target_pairs={{0,12},{1,13},{2,14},{3,15},{4,8},{5,9},{6,10},{7,11},{8,4},{9,5},... | collective-permute-start | bytes 110600 | tf_op jit(solution)/shard_map/ppermute | solution.py:30
  10.2 0.0 collective-permute-start.1
  10.2 0.6 collective-permute-start
  10.9 1.3 %collective-permute-done.2 = bf16[16,1152]{1,0:T(8,128)(2,1)S(1)} collective-permute-done((bf16[16,1152]{1,0:T(8,128)(2,1)S(1)}, bf16[16,1152]{1,0:T(8,128)(2,1)S(1)}, u32[]{:S(2)}, u32[]{:S(2)}) %collective-permute-start.2) | collective-permute-done | bytes 36896 | tf_op jit(solution)/shard_map/ppermute | solution.py:30
  12.2 2.9 %collective-permute-done.1 = bf16[16,1152]{1,0:T(8,128)(2,1)S(1)} collective-permute-done((bf16[16,1152]{1,0:T(8,128)(2,1)S(1)}, bf16[16,1152]{1,0:T(8,128)(2,1)S(1)}, u32[]{:S(2)}, u32[]{:S(2)}) %collective-permute-start.1) | collective-permute-done | bytes 36896 | tf_op jit(solution)/shard_map/ppermute | solution.py:30
  15.1 0.0 collective-permute-done
  15.1 1.6 %collective-permute-start.3 = (bf16[64,1152]{1,0:T(8,128)(2,1)S(1)}, bf16[64,1152]{1,0:T(8,128)(2,1)S(1)}, u32[]{:S(2)}, u32[]{:S(2)}) collective-permute-start(bf16[64,1152]{1,0:T(8,128)(2,1)S(1)} %pad_maximum_fusion), channel_id=1, source_target_pairs={{0,2},{1,3},{2,0},{3,1},{4,6},{5,7},{6,4},{7,5},{8,10},{9,11},{10,... | collective-permute-start | bytes 442376 | tf_op jit(solution)/shard_map/ppermute | solution.py:30
  16.7 3.6 %collective-permute-done.3 = bf16[64,1152]{1,0:T(8,128)(2,1)S(1)} collective-permute-done((bf16[64,1152]{1,0:T(8,128)(2,1)S(1)}, bf16[64,1152]{1,0:T(8,128)(2,1)S(1)}, u32[]{:S(2)}, u32[]{:S(2)}) %collective-permute-start.3) | collective-permute-done | bytes 147488 | tf_op jit(solution)/shard_map/ppermute | solution.py:30
  20.3 0.0 copy-start
  20.3 0.0 copy-start.3
  20.3 0.1 collective-permute-start.4
  20.4 1.6 %collective-permute-done.4.refs_2_ = bf16[128,1152]{1,0:T(8,128)(2,1)S(1)} collective-permute-done((bf16[128,1152]{1,0:T(8,128)(2,1)S(1)}, bf16[128,1152]{1,0:T(8,128)(2,1)S(1)}, u32[]{:S(2)}, u32[]{:S(2)}) %collective-permute-start.4) | collective-permute-done | bytes 294944 | tf_op jit(solution)/shard_map/ppermute | solution.py:30
  22.0 2.2 %copy-done.6 = bf16[2,2048,512]{2,1,0:T(8,128)(2,1)S(1)} copy-done((bf16[2,2048,512]{2,1,0:T(8,128)(2,1)S(1)}, bf16[2,2048,512]{2,1,0:T(8,128)(2,1)}, u32[]{:S(2)}) %copy-start.6) | copy-done | bytes 4194328
  24.2 1.0 %copy-done.7 = bf16[2,64,2048]{2,1,0:T(8,128)(2,1)S(1)} copy-done((bf16[2,64,2048]{2,1,0:T(8,128)(2,1)S(1)}, bf16[2,64,2048]{2,1,0:T(8,128)(2,1)}, u32[]{:S(2)}) %copy-start.7) | copy-done | bytes 524312
  25.2 0.7 copy-done.8
  25.9 4.2 %attend.1 = (f32[128,1152]{1,0:T(8,128)S(1)}, bf16[128,1152]{1,0:T(8,128)(2,1)S(1)}) custom-call(s32[2]{0:T(128)S(1)} %copy-done.8, bf16[128,1152]{1,0:T(8,128)(2,1)S(1)} %constant_dynamic-update-slice_fusion.refs_1_, bf16[128,1152]{1,0:T(8,128)(2,1)S(1)} %collective-permute-done.4.refs_2_, bf16[2,2048,512]{2,1,0:T(8,128)(2,1)S(1)} %copy-done.6, ...), custom_call_target="tpu_custom_call" | custom-call | flops 2147483648 | bytes 8388608 | tf_op jit(solution)/shard_map/attend/pallas_call | solution.py:277
  30.1 0.2 collective-permute-start.5
  30.3 1.4 %collective-permute-done.5.refs_1_ = bf16[128,1152]{1,0:T(8,128)(2,1)S(1)} collective-permute-done((bf16[128,1152]{1,0:T(8,128)(2,1)S(1)}, bf16[128,1152]{1,0:T(8,128)(2,1)S(1)}, u32[]{:S(2)}, u32[]{:S(2)}) %collective-permute-start.5) | collective-permute-done | bytes 294944 | tf_op jit(solution)/shard_map/ppermute | solution.py:30
  31.7 0.3 merge.2
  32.1 1.6 %collective-permute-start.6 = (bf16[64,1152]{1,0:T(8,128)(2,1)S(1)}, bf16[64,1152]{1,0:T(8,128)(2,1)S(1)}, u32[]{:S(2)}, u32[]{:S(2)}) collective-permute-start(bf16[64,1152]{1,0:T(8,128)(2,1)S(1)} %get-tuple-element.18), channel_id=1, source_target_pairs={{0,2},{1,3},{2,0},{3,1},{4,6},{5,7},{6,4},{7,5},{8,10},{9,11},{10,... | collective-permute-start | bytes 442376 | tf_op jit(solution)/shard_map/ppermute | solution.py:30
  33.7 4.4 %collective-permute-done.6.refs_1_ = bf16[64,1152]{1,0:T(8,128)(2,1)S(1)} collective-permute-done((bf16[64,1152]{1,0:T(8,128)(2,1)S(1)}, bf16[64,1152]{1,0:T(8,128)(2,1)S(1)}, u32[]{:S(2)}, u32[]{:S(2)}) %collective-permute-start.6) | collective-permute-done | bytes 147488 | tf_op jit(solution)/shard_map/ppermute | solution.py:30
  38.0 0.2 merge.3
  38.3 0.1 collective-permute-start.7
  38.4 2.1 %collective-permute-start.8 = (bf16[16,1152]{1,0:T(8,128)(2,1)S(1)}, bf16[16,1152]{1,0:T(8,128)(2,1)S(1)}, u32[]{:S(2)}, u32[]{:S(2)}) collective-permute-start(bf16[16,1152]{1,0:T(8,128)(2,1)S(1)} %get-tuple-element.21), channel_id=1, source_target_pairs={{0,8},{1,9},{2,10},{3,11},{4,12},{5,13},{6,14},{7,15},{8,0},{9,1},... | collective-permute-start | bytes 110600 | tf_op jit(solution)/shard_map/ppermute | solution.py:30
  40.5 2.3 %collective-permute-start.9 = (bf16[16,1152]{1,0:T(8,128)(2,1)S(1)}, bf16[16,1152]{1,0:T(8,128)(2,1)S(1)}, u32[]{:S(2)}, u32[]{:S(2)}) collective-permute-start(bf16[16,1152]{1,0:T(8,128)(2,1)S(1)} %get-tuple-element.22), channel_id=1, source_target_pairs={{0,12},{1,13},{2,14},{3,15},{4,8},{5,9},{6,10},{7,11},{8,4},{9,5},... | collective-permute-start | bytes 110600 | tf_op jit(solution)/shard_map/ppermute | solution.py:30
  42.8 0.0 collective-permute-done.7.refs_1_
  42.8 0.7 collective-permute-done.8.refs_2_
  43.4 2.8 %collective-permute-done.9.refs_3_ = bf16[16,1152]{1,0:T(8,128)(2,1)S(1)} collective-permute-done((bf16[16,1152]{1,0:T(8,128)(2,1)S(1)}, bf16[16,1152]{1,0:T(8,128)(2,1)S(1)}, u32[]{:S(2)}, u32[]{:S(2)}) %collective-permute-start.9) | collective-permute-done | bytes 36896 | tf_op jit(solution)/shard_map/ppermute | solution.py:30
  46.2 0.9 %project.1 = (f32[16,3584]{1,0:T(8,128)S(1)}, bf16[16,3584]{1,0:T(8,128)(2,1)S(1)}) custom-call(f32[16,1152]{1,0:T(8,128)S(1)} %get-tuple-element.19.refs_0_, bf16[16,1152]{1,0:T(8,128)(2,1)S(1)} %collective-permute-done.7.refs_1_, bf16[16,1152]{1,0:T(8,128)(2,1)S(1)} %collective-permute-done.8.refs_2_, bf16[16,1152]{1,0:T(8,128)(2,1)S(1)} %collective-permute-done.9.refs_3_, ...), custom_call_target="tpu_custom_call" | custom-call | bytes 4460544 | tf_op jit(solution)/shard_map/project/pallas_call | solution.py:39
  47.1 0.0 collective-permute-start.10
  47.1 1.3 %collective-permute-done.10 = bf16[16,3584]{1,0:T(8,128)(2,1)S(1)} collective-permute-done((bf16[16,3584]{1,0:T(8,128)(2,1)S(1)}, bf16[16,3584]{1,0:T(8,128)(2,1)S(1)}, u32[]{:S(2)}, u32[]{:S(2)}) %collective-permute-start.10) | collective-permute-done | bytes 114720 | tf_op jit(solution)/shard_map/ppermute | solution.py:30
  48.5 1.6 %collective-permute-start.11 = (bf16[16,1792]{1,0:T(8,128)(2,1)S(1)}, bf16[16,1792]{1,0:T(8,128)(2,1)S(1)}, u32[]{:S(2)}, u32[]{:S(2)}) collective-permute-start(bf16[16,1792]{1,0:T(8,128)(2,1)S(1)} %slice.15), channel_id=1, source_target_pairs={{0,2},{1,3},{2,0},{3,1},{4,6},{5,7},{6,4},{7,5},{8,10},{9,11},{10,... | collective-permute-start | bytes 172040 | tf_op jit(solution)/shard_map/ppermute | solution.py:30
  50.1 2.7 %collective-permute-done.11 = bf16[16,1792]{1,0:T(8,128)(2,1)S(1)} collective-permute-done((bf16[16,1792]{1,0:T(8,128)(2,1)S(1)}, bf16[16,1792]{1,0:T(8,128)(2,1)S(1)}, u32[]{:S(2)}, u32[]{:S(2)}) %collective-permute-start.11) | collective-permute-done | bytes 57376 | tf_op jit(solution)/shard_map/ppermute | solution.py:30
  52.7 2.4 %collective-permute-start.14 = (bf16[16,1792]{1,0:T(8,128)(2,1)S(1)}, bf16[16,1792]{1,0:T(8,128)(2,1)S(1)}, u32[]{:S(2)}, u32[]{:S(2)}) collective-permute-start(bf16[16,1792]{1,0:T(8,128)(2,1)S(1)} %fusion), channel_id=1, source_target_pairs={{0,12},{1,13},{2,14},{3,15},{4,8},{5,9},{6,10},{7,11},{8,4},{9,5},... | collective-permute-start | bytes 172040 | tf_op jit(solution)/shard_map/ppermute | solution.py:30
  55.1 2.1 %collective-permute-start.12 = (bf16[16,1792]{1,0:T(8,128)(2,1)S(1)}, bf16[16,1792]{1,0:T(8,128)(2,1)S(1)}, u32[]{:S(2)}, u32[]{:S(2)}) collective-permute-start(bf16[16,1792]{1,0:T(8,128)(2,1)S(1)} %fusion), channel_id=1, source_target_pairs={{0,4},{1,5},{2,6},{3,7},{4,0},{5,1},{6,2},{7,3},{8,12},{9,13},{10,... | collective-permute-start | bytes 172040 | tf_op jit(solution)/shard_map/ppermute | solution.py:30
  57.2 1.9 %collective-permute-done.14 = bf16[16,1792]{1,0:T(8,128)(2,1)S(1)} collective-permute-done((bf16[16,1792]{1,0:T(8,128)(2,1)S(1)}, bf16[16,1792]{1,0:T(8,128)(2,1)S(1)}, u32[]{:S(2)}, u32[]{:S(2)}) %collective-permute-start.14) | collective-permute-done | bytes 57376 | tf_op jit(solution)/shard_map/ppermute | solution.py:30
  59.1 1.5 %collective-permute-done.13 = bf16[16,1792]{1,0:T(8,128)(2,1)S(1)} collective-permute-done((bf16[16,1792]{1,0:T(8,128)(2,1)S(1)}, bf16[16,1792]{1,0:T(8,128)(2,1)S(1)}, u32[]{:S(2)}, u32[]{:S(2)}) %collective-permute-start.13) | collective-permute-done | bytes 57376 | tf_op jit(solution)/shard_map/ppermute | solution.py:30
  60.6 1.6 %collective-permute-start.15 = (bf16[16,1792]{1,0:T(8,128)(2,1)S(1)}, bf16[16,1792]{1,0:T(8,128)(2,1)S(1)}, u32[]{:S(2)}, u32[]{:S(2)}) collective-permute-start(bf16[16,1792]{1,0:T(8,128)(2,1)S(1)} %add_convert_fusion), channel_id=1, source_target_pairs={{0,2},{1,3},{2,0},{3,1},{4,6},{5,7},{6,4},{7,5},{8,10},{9,11},{10,... | collective-permute-start | bytes 172040 | tf_op jit(solution)/shard_map/ppermute | solution.py:30
  62.2 2.7 %collective-permute-done.15 = bf16[16,1792]{1,0:T(8,128)(2,1)S(1)} collective-permute-done((bf16[16,1792]{1,0:T(8,128)(2,1)S(1)}, bf16[16,1792]{1,0:T(8,128)(2,1)S(1)}, u32[]{:S(2)}, u32[]{:S(2)}) %collective-permute-start.15) | collective-permute-done | bytes 57376 | tf_op jit(solution)/shard_map/ppermute | solution.py:30
  64.8 0.1 collective-permute-start.16
  64.9 1.3 %collective-permute-done.16.refs_1_ = bf16[16,3584]{1,0:T(8,128)(2,1)S(1)} collective-permute-done((bf16[16,3584]{1,0:T(8,128)(2,1)S(1)}, bf16[16,3584]{1,0:T(8,128)(2,1)S(1)}, u32[]{:S(2)}, u32[]{:S(2)}) %collective-permute-start.16) | collective-permute-done | bytes 114720 | tf_op jit(solution)/shard_map/ppermute | solution.py:30
  66.2 0.7 %place.1 = bf16[16,7168]{1,0:T(8,128)(2,1)} custom-call(bf16[16,3584]{1,0:T(8,128)(2,1)S(1)} %pad_maximum_fusion.1.refs_0_, bf16[16,3584]{1,0:T(8,128)(2,1)S(1)} %collective-permute-done.16.refs_1_), custom_call_target="tpu_custom_call" | custom-call | bytes 458752 | tf_op jit(solution)/shard_map/place/pallas_call | solution.py:39
  (22 shorter events, 0.2 us)
Async XLA Ops:
  0.7 1.1 %copy-start.1 = (bf16[1536,256]{1,0:T(8,128)(2,1)S(1)}, bf16[1536,256]{1,0:T(8,128)(2,1)}, u32[]{:S(2)}) copy-start(bf16[1536,256]{1,0:T(8,128)(2,1)} %nope_ref.1) | copy-start | bytes 2359300
  1.8 1.0 %copy-start.2 = (bf16[1536,128]{1,0:T(8,128)(2,1)S(1)}, bf16[1536,128]{1,0:T(8,128)(2,1)}, u32[]{:S(2)}) copy-start(bf16[1536,128]{1,0:T(8,128)(2,1)} %rope_ref.1) | copy-start | bytes 1179652
  2.8 0.9 %copy-start.4 = (bf16[2,128,512]{2,1,0:T(8,128)(2,1)S(1)}, bf16[2,128,512]{2,1,0:T(8,128)(2,1)}, u32[]{:S(2)}) copy-start(bf16[2,128,512]{2,1,0:T(8,128)(2,1)} %key_ref.1) | copy-start | bytes 786436
  3.8 0.8 %copy-start.5 = (bf16[16,1536]{1,0:T(8,128)(2,1)S(1)}, bf16[16,1536]{1,0:T(8,128)(2,1)}, u32[]{:S(2)}) copy-start(bf16[16,1536]{1,0:T(8,128)(2,1)} %x_ref.1) | copy-start | bytes 147460
  5.1 7.0 %collective-permute-start.2 = (bf16[16,1152]{1,0:T(8,128)(2,1)S(1)}, bf16[16,1152]{1,0:T(8,128)(2,1)S(1)}, u32[]{:S(2)}, u32[]{:S(2)}) collective-permute-start(bf16[16,1152]{1,0:T(8,128)(2,1)S(1)} %query.1), channel_id=1, source_target_pairs={{0,12},{1,13},{2,14},{3,15},{4,8},{5,9},{6,10},{7,11},{8,4},{9,5},... | collective-permute-start | bytes 110600 | tf_op jit(solution)/shard_map/ppermute | solution.py:30
  10.2 4.9 %collective-permute-start.1 = (bf16[16,1152]{1,0:T(8,128)(2,1)S(1)}, bf16[16,1152]{1,0:T(8,128)(2,1)S(1)}, u32[]{:S(2)}, u32[]{:S(2)}) collective-permute-start(bf16[16,1152]{1,0:T(8,128)(2,1)S(1)} %query.1), channel_id=1, source_target_pairs={{0,8},{1,9},{2,10},{3,11},{4,12},{5,13},{6,14},{7,15},{8,0},{9,1},... | collective-permute-start | bytes 110600 | tf_op jit(solution)/shard_map/ppermute | solution.py:30
  10.2 4.9 %collective-permute-start = (bf16[16,1152]{1,0:T(8,128)(2,1)S(1)}, bf16[16,1152]{1,0:T(8,128)(2,1)S(1)}, u32[]{:S(2)}, u32[]{:S(2)}) collective-permute-start(bf16[16,1152]{1,0:T(8,128)(2,1)S(1)} %query.1), channel_id=1, source_target_pairs={{0,4},{1,5},{2,6},{3,7},{4,0},{5,1},{6,2},{7,3},{8,12},{9,13},{10,... | collective-permute-start | bytes 110600 | tf_op jit(solution)/shard_map/ppermute | solution.py:30
  15.1 5.2 %collective-permute-start.3 = (bf16[64,1152]{1,0:T(8,128)(2,1)S(1)}, bf16[64,1152]{1,0:T(8,128)(2,1)S(1)}, u32[]{:S(2)}, u32[]{:S(2)}) collective-permute-start(bf16[64,1152]{1,0:T(8,128)(2,1)S(1)} %pad_maximum_fusion), channel_id=1, source_target_pairs={{0,2},{1,3},{2,0},{3,1},{4,6},{5,7},{6,4},{7,5},{8,10},{9,11},{10,... | collective-permute-start | bytes 442376 | tf_op jit(solution)/shard_map/ppermute | solution.py:30
  20.3 25.9 %copy-start = (bf16[256,7168]{1,0:T(8,128)(2,1)S(1)}, bf16[256,7168]{1,0:T(8,128)(2,1)}, u32[]{:S(2)}) copy-start(bf16[256,7168]{1,0:T(8,128)(2,1)} %refs_5_.1) | copy-start | bytes 11010052
  20.3 25.9 %copy-start.3 = (bf16[2,512,128]{2,1,0:T(8,128)(2,1)S(1)}, bf16[2,512,128]{2,1,0:T(8,128)(2,1)}, u32[]{:S(2)}) copy-start(bf16[2,512,128]{2,1,0:T(8,128)(2,1)} %refs_4_.3) | copy-start | bytes 786436
  20.3 1.6 %collective-permute-start.4 = (bf16[128,1152]{1,0:T(8,128)(2,1)S(1)}, bf16[128,1152]{1,0:T(8,128)(2,1)S(1)}, u32[]{:S(2)}, u32[]{:S(2)}) collective-permute-start(bf16[128,1152]{1,0:T(8,128)(2,1)S(1)} %constant_dynamic-update-slice_fusion.refs_1_), channel_id=1, source_target_pairs={{0,1},{1,0},{2,3},{3,2},{4,5},{5,4},{6,7},{7,6},{8,9},{9,8},{10,11... | collective-permute-start | bytes 884744 | tf_op jit(solution)/shard_map/ppermute | solution.py:30
  22.0 2.2 %copy-start.6 = (bf16[2,2048,512]{2,1,0:T(8,128)(2,1)S(1)}, bf16[2,2048,512]{2,1,0:T(8,128)(2,1)}, u32[]{:S(2)}) copy-start(bf16[2,2048,512]{2,1,0:T(8,128)(2,1)} %refs_3_.1) | copy-start | bytes 12582916
  24.2 1.0 %copy-start.7 = (bf16[2,64,2048]{2,1,0:T(8,128)(2,1)S(1)}, bf16[2,64,2048]{2,1,0:T(8,128)(2,1)}, u32[]{:S(2)}) copy-start(bf16[2,64,2048]{2,1,0:T(8,128)(2,1)} %refs_4_.2) | copy-start | bytes 1572868
  25.2 0.7 copy-start.8
  30.1 1.6 %collective-permute-start.5 = (bf16[128,1152]{1,0:T(8,128)(2,1)S(1)}, bf16[128,1152]{1,0:T(8,128)(2,1)S(1)}, u32[]{:S(2)}, u32[]{:S(2)}) collective-permute-start(bf16[128,1152]{1,0:T(8,128)(2,1)S(1)} %get-tuple-element.16), channel_id=1, source_target_pairs={{0,1},{1,0},{2,3},{3,2},{4,5},{5,4},{6,7},{7,6},{8,9},{9,8},{10,11... | collective-permute-start | bytes 884744 | tf_op jit(solution)/shard_map/ppermute | solution.py:30
  32.1 6.0 %collective-permute-start.6 = (bf16[64,1152]{1,0:T(8,128)(2,1)S(1)}, bf16[64,1152]{1,0:T(8,128)(2,1)S(1)}, u32[]{:S(2)}, u32[]{:S(2)}) collective-permute-start(bf16[64,1152]{1,0:T(8,128)(2,1)S(1)} %get-tuple-element.18), channel_id=1, source_target_pairs={{0,2},{1,3},{2,0},{3,1},{4,6},{5,7},{6,4},{7,5},{8,10},{9,11},{10,... | collective-permute-start | bytes 442376 | tf_op jit(solution)/shard_map/ppermute | solution.py:30
  38.3 4.5 %collective-permute-start.7 = (bf16[16,1152]{1,0:T(8,128)(2,1)S(1)}, bf16[16,1152]{1,0:T(8,128)(2,1)S(1)}, u32[]{:S(2)}, u32[]{:S(2)}) collective-permute-start(bf16[16,1152]{1,0:T(8,128)(2,1)S(1)} %get-tuple-element.20), channel_id=1, source_target_pairs={{0,4},{1,5},{2,6},{3,7},{4,0},{5,1},{6,2},{7,3},{8,12},{9,13},{10,... | collective-permute-start | bytes 110600 | tf_op jit(solution)/shard_map/ppermute | solution.py:30
  38.4 5.0 %collective-permute-start.8 = (bf16[16,1152]{1,0:T(8,128)(2,1)S(1)}, bf16[16,1152]{1,0:T(8,128)(2,1)S(1)}, u32[]{:S(2)}, u32[]{:S(2)}) collective-permute-start(bf16[16,1152]{1,0:T(8,128)(2,1)S(1)} %get-tuple-element.21), channel_id=1, source_target_pairs={{0,8},{1,9},{2,10},{3,11},{4,12},{5,13},{6,14},{7,15},{8,0},{9,1},... | collective-permute-start | bytes 110600 | tf_op jit(solution)/shard_map/ppermute | solution.py:30
  40.5 5.8 %collective-permute-start.9 = (bf16[16,1152]{1,0:T(8,128)(2,1)S(1)}, bf16[16,1152]{1,0:T(8,128)(2,1)S(1)}, u32[]{:S(2)}, u32[]{:S(2)}) collective-permute-start(bf16[16,1152]{1,0:T(8,128)(2,1)S(1)} %get-tuple-element.22), channel_id=1, source_target_pairs={{0,12},{1,13},{2,14},{3,15},{4,8},{5,9},{6,10},{7,11},{8,4},{9,5},... | collective-permute-start | bytes 110600 | tf_op jit(solution)/shard_map/ppermute | solution.py:30
  47.1 1.4 %collective-permute-start.10 = (bf16[16,3584]{1,0:T(8,128)(2,1)S(1)}, bf16[16,3584]{1,0:T(8,128)(2,1)S(1)}, u32[]{:S(2)}, u32[]{:S(2)}) collective-permute-start(bf16[16,3584]{1,0:T(8,128)(2,1)S(1)} %get-tuple-element.24), channel_id=1, source_target_pairs={{0,1},{1,0},{2,3},{3,2},{4,5},{5,4},{6,7},{7,6},{8,9},{9,8},{10,11... | collective-permute-start | bytes 344072 | tf_op jit(solution)/shard_map/ppermute | solution.py:30
  48.5 4.2 %collective-permute-start.11 = (bf16[16,1792]{1,0:T(8,128)(2,1)S(1)}, bf16[16,1792]{1,0:T(8,128)(2,1)S(1)}, u32[]{:S(2)}, u32[]{:S(2)}) collective-permute-start(bf16[16,1792]{1,0:T(8,128)(2,1)S(1)} %slice.15), channel_id=1, source_target_pairs={{0,2},{1,3},{2,0},{3,1},{4,6},{5,7},{6,4},{7,5},{8,10},{9,11},{10,... | collective-permute-start | bytes 172040 | tf_op jit(solution)/shard_map/ppermute | solution.py:30
  52.7 6.3 %collective-permute-start.14 = (bf16[16,1792]{1,0:T(8,128)(2,1)S(1)}, bf16[16,1792]{1,0:T(8,128)(2,1)S(1)}, u32[]{:S(2)}, u32[]{:S(2)}) collective-permute-start(bf16[16,1792]{1,0:T(8,128)(2,1)S(1)} %fusion), channel_id=1, source_target_pairs={{0,12},{1,13},{2,14},{3,15},{4,8},{5,9},{6,10},{7,11},{8,4},{9,5},... | collective-permute-start | bytes 172040 | tf_op jit(solution)/shard_map/ppermute | solution.py:30
  55.1 5.4 %collective-permute-start.13 = (bf16[16,1792]{1,0:T(8,128)(2,1)S(1)}, bf16[16,1792]{1,0:T(8,128)(2,1)S(1)}, u32[]{:S(2)}, u32[]{:S(2)}) collective-permute-start(bf16[16,1792]{1,0:T(8,128)(2,1)S(1)} %fusion), channel_id=1, source_target_pairs={{0,8},{1,9},{2,10},{3,11},{4,12},{5,13},{6,14},{7,15},{8,0},{9,1},... | collective-permute-start | bytes 172040 | tf_op jit(solution)/shard_map/ppermute | solution.py:30
  55.1 5.4 %collective-permute-start.12 = (bf16[16,1792]{1,0:T(8,128)(2,1)S(1)}, bf16[16,1792]{1,0:T(8,128)(2,1)S(1)}, u32[]{:S(2)}, u32[]{:S(2)}) collective-permute-start(bf16[16,1792]{1,0:T(8,128)(2,1)S(1)} %fusion), channel_id=1, source_target_pairs={{0,4},{1,5},{2,6},{3,7},{4,0},{5,1},{6,2},{7,3},{8,12},{9,13},{10,... | collective-permute-start | bytes 172040 | tf_op jit(solution)/shard_map/ppermute | solution.py:30
  60.6 4.2 %collective-permute-start.15 = (bf16[16,1792]{1,0:T(8,128)(2,1)S(1)}, bf16[16,1792]{1,0:T(8,128)(2,1)S(1)}, u32[]{:S(2)}, u32[]{:S(2)}) collective-permute-start(bf16[16,1792]{1,0:T(8,128)(2,1)S(1)} %add_convert_fusion), channel_id=1, source_target_pairs={{0,2},{1,3},{2,0},{3,1},{4,6},{5,7},{6,4},{7,5},{8,10},{9,11},{10,... | collective-permute-start | bytes 172040 | tf_op jit(solution)/shard_map/ppermute | solution.py:30
  64.8 1.4 %collective-permute-start.16 = (bf16[16,3584]{1,0:T(8,128)(2,1)S(1)}, bf16[16,3584]{1,0:T(8,128)(2,1)S(1)}, u32[]{:S(2)}, u32[]{:S(2)}) collective-permute-start(bf16[16,3584]{1,0:T(8,128)(2,1)S(1)} %pad_maximum_fusion.1.refs_0_), channel_id=1, source_target_pairs={{0,1},{1,0},{2,3},{3,2},{4,5},{5,4},{6,7},{7,6},{8,9},{9,8},{10,11... | collective-permute-start | bytes 344072 | tf_op jit(solution)/shard_map/ppermute | solution.py:30

commit v2 on v1

--- a/solution.py
+++ b/solution.py
@@ -51,16 +51,31 @@
     return jax.ShapeDtypeStruct(shape, dtype)
 
 
-def query_body(heads, reqs, x_ref, gain_ref, nope_ref, rope_ref, key_ref, out_ref):
+def query_body(heads, reqs, *refs):
+    sources, out_ref, (x_ref, gain_ref, nope_ref, rope_ref, key_ref), sems = (
+        refs[:5], refs[5], refs[6:11], refs[11]
+    )
+    copies = [
+        pltpu.make_async_copy(source, held, sems.at[i])
+        for i, (source, held) in enumerate(zip(sources, refs[6:11]))
+    ]
+    for copy in copies:
+        copy.start()
     rows = x_ref.shape[0]
     stretch = rows // reqs
     nope_width, latent = key_ref.shape[1], key_ref.shape[2]
     rope_width = rope_ref.shape[1] // heads
+    copies[0].wait()
+    copies[1].wait()
     x = x_ref[...].astype(F32)
     mean = jnp.mean(x * x, axis=-1, keepdims=True)
-    normed = (x * lax.rsqrt(mean + 1e-06) * gain_ref[...].astype(F32)).astype(BF16)
+    gain = gain_ref[...].astype(F32).reshape(1, -1)
+    normed = (x * lax.rsqrt(mean + 1e-06) * gain).astype(BF16)
+    copies[2].wait()
     nope = jnp.dot(normed, nope_ref[...], preferred_element_type=F32).astype(BF16)
+    copies[3].wait()
     rope = jnp.dot(normed, rope_ref[...], preferred_element_type=F32)
+    copies[4].wait()
     lat = [
         jnp.dot(
             nope[:, h * nope_width : (h + 1) * nope_width], key_ref[h], preferred_element_type=F32
@@ -231,8 +246,16 @@
             send_ref[:, slot] = out.astype(BF16)
 
 
+def join_body(*refs):
+    at = 0
+    for r in refs[:-1]:
+        refs[-1][at : at + r.shape[0], :] = r[...]
+        at += r.shape[0]
+
+
 def place_body(parts_out, *refs):
-    pieces, out_ref = refs[:-1], refs[-1]
+    pieces, out_ref, sems = refs[:-2], refs[-2], refs[-1]
+    copies = []
     mine = lax.rem(lax.axis_index("ctx"), parts_out)
     width = out_ref.shape[1] // parts_out
     e_order = (0, 2, 1, 3)
@@ -240,8 +263,17 @@
     for piece in pieces:
         for k in range(piece.shape[1] // width):
             start = pl.multiple_of(jnp.bitwise_xor(mine, e_order[at]) * width, LANES)
-            out_ref[:, pl.ds(start, width)] = piece[:, k * width : (k + 1) * width]
+            copies.append(
+                pltpu.make_async_copy(
+                    piece.at[:, pl.ds(k * width, width)],
+                    out_ref.at[:, pl.ds(start, width)],
+                    sems.at[at],
+                )
+            )
+            copies[-1].start()
             at += 1
+    for copy in copies:
+        copy.wait()
 
 
 def local(count, query_input, query_gain, nope_weight, rope_weight, key_up, value_up, out_weight,
@@ -256,16 +288,31 @@
     stages = stage_list(count)
     scale = mscale_yarn * mscale_yarn / math.sqrt(nope_width + rope_width)
 
-    (query,) = call(
+    sources = [query_input, query_gain, nope_weight, rope_weight, key_up]
+    query = pl.pallas_call(
         functools.partial(query_body, heads, reqs),
-        [spec((own, width), BF16)],
-        [query_input, query_gain[None], nope_weight, rope_weight, key_up],
+        out_shape=spec((own, width), BF16),
+        in_specs=[pl.BlockSpec(memory_space=pl.ANY)] * len(sources),
+        out_specs=pl.BlockSpec(memory_space=pltpu.VMEM),
+        scratch_shapes=[pltpu.VMEM(a.shape, a.dtype) for a in sources]
+        + [pltpu.SemaphoreType.DMA((len(sources),))],
+        compiler_params=pltpu.CompilerParams(vmem_limit_bytes=24 << 20),
+        cost_estimate=pl.CostEstimate(flops=1 << 24, bytes_accessed=1 << 21, transcendentals=0),
         name="query",
-    )
+    )(*sources)
+    join_flops = 4 << 30
     held = query
     for stride, radix in reversed(stages[2:]):
         got = [swap(held, count, j * stride) for j in range(1, radix)]
-        held = jnp.concatenate([held] + got, axis=0)
+        parts = [held] + got
+        (held,) = call(
+            join_body,
+            [spec((radix * held.shape[0], width), BF16)],
+            parts,
+            flops=join_flops,
+            limit=16 << 20,
+            name="join",
+        )
     beside = swap(held, count, stages[1][0])
     near = jnp.concatenate([held, beside], axis=0)
     far = swap(near, count, stages[0][0])
@@ -303,7 +350,7 @@
             name="merge",
         )
         keep = pieces[0]
-        got = [swap(p, count, j * stride) for j, p in enumerate(pieces[1:], 1)]
+        got = [swap(pieces[j], count, j * stride) for j in reversed(range(1, radix))]
 
     parts_out = 4
     model = out_weight.shape[1]
@@ -327,13 +374,15 @@
     done = kept.astype(BF16)
     both = jnp.concatenate([done, swap(done, count, stages[1][0])], axis=1)
     other = swap(both, count, stages[0][0])
-    (out,) = call(
+    return pl.pallas_call(
         functools.partial(place_body, parts_out),
-        [spec((rows, model), BF16)],
-        [both, other],
+        out_shape=spec((rows, model), BF16),
+        in_specs=[pl.BlockSpec(memory_space=pltpu.VMEM)] * 2,
+        out_specs=pl.BlockSpec(memory_space=pl.ANY),
+        scratch_shapes=[pltpu.SemaphoreType.DMA((parts_out,))],
+        compiler_params=pltpu.CompilerParams(vmem_limit_bytes=16 << 20),
         name="place",
-    )
-    return out
+    )(both, other)
 
 
 def solution(mesh):

time: 67.3 us -> 63.1 us (0.938)
  local copies, waits for them, and re-layouts: 8.52 us -> 4.6 us
  waiting for transfers between devices: 29.9 us -> 29 us
    unnamed x22 -> x20, local copies, waits for them, and re-layouts: 7.8 us -> 4.59 us
    pallas_call x0 -> x2, Pallas kernels: none -> 1.88 us  [the longest x1 1.16 us: local(): pl.pallas_call(functools.partial(query_body, heads, reqs), out_shape=spec...]
    pallas_call x5 -> x4, Pallas kernels: 2.71 us -> 1.47 us  [call(): pl.pallas_call(body, out_shape=tuple(outs), in_specs=specs, out_specs=tup...]
    ppermute x17, waiting for transfers between devices: 29.9 us -> 29 us  [swap(): return lax.ppermute(x, 'ctx', [(i, i ^ mask) for i in range(count)])]
    broadcast_in_dim x1 -> x0, local copies, waits for them, and re-layouts: 0.69 us -> none  [local(): query_gain[None]]
  transfers between devices with their start and end apart: 17 -> 17, of which waited for: 14 -> 15; matrix products, arithmetic and copies ran while one was open for 0% -> 0% of each run, Pallas kernels for 0% -> 0%
where the time goes in v2:
time: 63.1 us; the launch traced here: 62.8 us
  waiting for transfers between devices  29 us (46%)
  starting transfers between devices  21.4 us (34%)
  Pallas kernels  7.55 us (12%)
  local copies, waits for them, and re-layouts  4.6 us (7%)
    ppermute x17, waiting for transfers between devices, swap(): return lax.ppermute(x, 'ctx', [(i, i ^ mask) for i in range(count)])  29 us
    ppermute x17, starting transfers between devices, swap(): return lax.ppermute(x, 'ctx', [(i, i ^ mask) for i in range(count)])  21.4 us
    unnamed x20, local copies, waits for them, and re-layouts  4.59 us
    pallas_call x1, Pallas kernels, local(): pl.pallas_call(functools.partial(attend_body, 2, reqs, latent, rope_width...  4.2 us
    pallas_call x4, Pallas kernels, call(): pl.pallas_call(body, out_shape=tuple(outs), in_specs=specs, out_specs=tup...  1.47 us
  transfers between devices with their start and end apart: 17, of which 15 were waited for; matrix products, arithmetic and copies ran while one was open for 0% of the time, Pallas kernels for 0%

profile of v2, /device:TPU:0, one launch (start us, length us, event | category | flops | bytes accessed | tf_op | source)
XLA Modules:
  0.0 62.8 jit_solution(2864511039535720623)
XLA Ops:
  0.0 1.1 %copy-done.1 = bf16[1536,256]{1,0:T(8,128)(2,1)S(1)} copy-done((bf16[1536,256]{1,0:T(8,128)(2,1)S(1)}, bf16[1536,256]{1,0:T(8,128)(2,1)}, u32[]{:S(2)}) %copy-start.1) | copy-done | bytes 786456
  1.1 1.0 %copy-done.2 = bf16[1536,128]{1,0:T(8,128)(2,1)S(1)} copy-done((bf16[1536,128]{1,0:T(8,128)(2,1)S(1)}, bf16[1536,128]{1,0:T(8,128)(2,1)}, u32[]{:S(2)}) %copy-start.2) | copy-done | bytes 393240
  2.1 0.9 %copy-done.4 = bf16[2,128,512]{2,1,0:T(8,128)(2,1)S(1)} copy-done((bf16[2,128,512]{2,1,0:T(8,128)(2,1)S(1)}, bf16[2,128,512]{2,1,0:T(8,128)(2,1)}, u32[]{:S(2)}) %copy-start.4) | copy-done | bytes 262168
  3.1 0.8 %copy-done.5 = bf16[16,1536]{1,0:T(8,128)(2,1)S(1)} copy-done((bf16[16,1536]{1,0:T(8,128)(2,1)S(1)}, bf16[16,1536]{1,0:T(8,128)(2,1)}, u32[]{:S(2)}) %copy-start.5) | copy-done | bytes 49176
  3.9 0.7 %copy-done.6 = bf16[1536]{0:T(1024)(128)(2,1)S(1)} copy-done((bf16[1536]{0:T(1024)(128)(2,1)S(1)}, bf16[1536]{0:T(1024)(128)(2,1)}, u32[]{:S(2)}) %copy-start.6) | copy-done | bytes 3096
  4.6 1.2 %query.1.refs_0_ = bf16[16,1152]{1,0:T(8,128)(2,1)S(1)} custom-call(bf16[16,1536]{1,0:T(8,128)(2,1)S(1)} %copy-done.5, bf16[1536]{0:T(1024)(128)(2,1)S(1)} %copy-done.6, bf16[1536,256]{1,0:T(8,128)(2,1)S(1)} %copy-done.1, bf16[1536,128]{1,0:T(8,128)(2,1)S(1)} %copy-done.2, bf16[2,128,512]{2,1,0:T(8,128)(2,1)S(1)} %copy-done.4), custom_call_target="tpu_custom_call" | custom-call | flops 16777216 | bytes 2097152 | tf_op jit(solution)/shard_map/query/pallas_call | solution.py:292
  5.7 0.0 copy-start.7
  5.8 0.0 copy-start.8
  5.8 0.0 copy-start.9
  5.8 5.1 %collective-permute-start.2 = (bf16[16,1152]{1,0:T(8,128)(2,1)S(1)}, bf16[16,1152]{1,0:T(8,128)(2,1)S(1)}, u32[]{:S(2)}, u32[]{:S(2)}) collective-permute-start(bf16[16,1152]{1,0:T(8,128)(2,1)S(1)} %query.1.refs_0_), channel_id=1, source_target_pairs={{0,12},{1,13},{2,14},{3,15},{4,8},{5,9},{6,10},{7,11},{8,4},{9,5},... | collective-permute-start | bytes 110600 | tf_op jit(solution)/shard_map/ppermute | solution.py:30
  10.9 0.0 collective-permute-start.1
  10.9 0.6 %collective-permute-start = (bf16[16,1152]{1,0:T(8,128)(2,1)S(1)}, bf16[16,1152]{1,0:T(8,128)(2,1)S(1)}, u32[]{:S(2)}, u32[]{:S(2)}) collective-permute-start(bf16[16,1152]{1,0:T(8,128)(2,1)S(1)} %query.1.refs_0_), channel_id=1, source_target_pairs={{0,4},{1,5},{2,6},{3,7},{4,0},{5,1},{6,2},{7,3},{8,12},{9,13},{10,... | collective-permute-start | bytes 110600 | tf_op jit(solution)/shard_map/ppermute | solution.py:30
  11.5 1.3 %collective-permute-done.2.refs_3_ = bf16[16,1152]{1,0:T(8,128)(2,1)S(1)} collective-permute-done((bf16[16,1152]{1,0:T(8,128)(2,1)S(1)}, bf16[16,1152]{1,0:T(8,128)(2,1)S(1)}, u32[]{:S(2)}, u32[]{:S(2)}) %collective-permute-start.2) | collective-permute-done | bytes 36896 | tf_op jit(solution)/shard_map/ppermute | solution.py:30
  12.8 2.9 %collective-permute-done.1.refs_2_ = bf16[16,1152]{1,0:T(8,128)(2,1)S(1)} collective-permute-done((bf16[16,1152]{1,0:T(8,128)(2,1)S(1)}, bf16[16,1152]{1,0:T(8,128)(2,1)S(1)}, u32[]{:S(2)}, u32[]{:S(2)}) %collective-permute-start.1) | collective-permute-done | bytes 36896 | tf_op jit(solution)/shard_map/ppermute | solution.py:30
  15.8 1.6 %collective-permute-start.3 = (bf16[64,1152]{1,0:T(8,128)(2,1)S(1)}, bf16[64,1152]{1,0:T(8,128)(2,1)S(1)}, u32[]{:S(2)}, u32[]{:S(2)}) collective-permute-start(bf16[64,1152]{1,0:T(8,128)(2,1)S(1)} %join.1), channel_id=1, source_target_pairs={{0,2},{1,3},{2,0},{3,1},{4,6},{5,7},{6,4},{7,5},{8,10},{9,11},{10,... | collective-permute-start | bytes 442376 | tf_op jit(solution)/shard_map/ppermute | solution.py:30
  17.4 3.6 %collective-permute-done.3 = bf16[64,1152]{1,0:T(8,128)(2,1)S(1)} collective-permute-done((bf16[64,1152]{1,0:T(8,128)(2,1)S(1)}, bf16[64,1152]{1,0:T(8,128)(2,1)S(1)}, u32[]{:S(2)}, u32[]{:S(2)}) %collective-permute-start.3) | collective-permute-done | bytes 147488 | tf_op jit(solution)/shard_map/ppermute | solution.py:30
  21.0 0.0 copy-start
  21.0 0.0 copy-start.3
  21.0 0.1 collective-permute-start.4
  21.1 1.6 %collective-permute-done.4.refs_2_ = bf16[128,1152]{1,0:T(8,128)(2,1)S(1)} collective-permute-done((bf16[128,1152]{1,0:T(8,128)(2,1)S(1)}, bf16[128,1152]{1,0:T(8,128)(2,1)S(1)}, u32[]{:S(2)}, u32[]{:S(2)}) %collective-permute-start.4) | collective-permute-done | bytes 294944 | tf_op jit(solution)/shard_map/ppermute | solution.py:30
  22.7 4.2 %attend.1 = (f32[128,1152]{1,0:T(8,128)S(1)}, bf16[128,1152]{1,0:T(8,128)(2,1)S(1)}) custom-call(s32[2]{0:T(128)S(1)} %copy-done.9, bf16[128,1152]{1,0:T(8,128)(2,1)S(1)} %pad_maximum_fusion.refs_1_, bf16[128,1152]{1,0:T(8,128)(2,1)S(1)} %collective-permute-done.4.refs_2_, bf16[2,2048,512]{2,1,0:T(8,128)(2,1)S(1)} %copy-done.7, ...), custom_call_target="tpu_custom_call" | custom-call | flops 2147483648 | bytes 8388608 | tf_op jit(solution)/shard_map/attend/pallas_call | solution.py:324
  26.9 0.2 collective-permute-start.5
  27.1 1.5 %collective-permute-done.5.refs_1_ = bf16[128,1152]{1,0:T(8,128)(2,1)S(1)} collective-permute-done((bf16[128,1152]{1,0:T(8,128)(2,1)S(1)}, bf16[128,1152]{1,0:T(8,128)(2,1)S(1)}, u32[]{:S(2)}, u32[]{:S(2)}) %collective-permute-start.5) | collective-permute-done | bytes 294944 | tf_op jit(solution)/shard_map/ppermute | solution.py:30
  28.5 0.3 merge.2
  28.9 1.6 %collective-permute-start.6 = (bf16[64,1152]{1,0:T(8,128)(2,1)S(1)}, bf16[64,1152]{1,0:T(8,128)(2,1)S(1)}, u32[]{:S(2)}, u32[]{:S(2)}) collective-permute-start(bf16[64,1152]{1,0:T(8,128)(2,1)S(1)} %get-tuple-element.18), channel_id=1, source_target_pairs={{0,2},{1,3},{2,0},{3,1},{4,6},{5,7},{6,4},{7,5},{8,10},{9,11},{10,... | collective-permute-start | bytes 442376 | tf_op jit(solution)/shard_map/ppermute | solution.py:30
  30.5 4.4 %collective-permute-done.6.refs_1_ = bf16[64,1152]{1,0:T(8,128)(2,1)S(1)} collective-permute-done((bf16[64,1152]{1,0:T(8,128)(2,1)S(1)}, bf16[64,1152]{1,0:T(8,128)(2,1)S(1)}, u32[]{:S(2)}, u32[]{:S(2)}) %collective-permute-start.6) | collective-permute-done | bytes 147488 | tf_op jit(solution)/shard_map/ppermute | solution.py:30
  34.9 0.2 merge.3
  35.1 1.5 %collective-permute-start.7 = (bf16[16,1152]{1,0:T(8,128)(2,1)S(1)}, bf16[16,1152]{1,0:T(8,128)(2,1)S(1)}, u32[]{:S(2)}, u32[]{:S(2)}) collective-permute-start(bf16[16,1152]{1,0:T(8,128)(2,1)S(1)} %get-tuple-element.20), channel_id=1, source_target_pairs={{0,12},{1,13},{2,14},{3,15},{4,8},{5,9},{6,10},{7,11},{8,4},{9,5},... | collective-permute-start | bytes 110600 | tf_op jit(solution)/shard_map/ppermute | solution.py:30
  36.6 0.6 %collective-permute-start.8 = (bf16[16,1152]{1,0:T(8,128)(2,1)S(1)}, bf16[16,1152]{1,0:T(8,128)(2,1)S(1)}, u32[]{:S(2)}, u32[]{:S(2)}) collective-permute-start(bf16[16,1152]{1,0:T(8,128)(2,1)S(1)} %get-tuple-element.21), channel_id=1, source_target_pairs={{0,8},{1,9},{2,10},{3,11},{4,12},{5,13},{6,14},{7,15},{8,0},{9,1},... | collective-permute-start | bytes 110600 | tf_op jit(solution)/shard_map/ppermute | solution.py:30
  37.3 2.3 %collective-permute-start.9 = (bf16[16,1152]{1,0:T(8,128)(2,1)S(1)}, bf16[16,1152]{1,0:T(8,128)(2,1)S(1)}, u32[]{:S(2)}, u32[]{:S(2)}) collective-permute-start(bf16[16,1152]{1,0:T(8,128)(2,1)S(1)} %get-tuple-element.22), channel_id=1, source_target_pairs={{0,4},{1,5},{2,6},{3,7},{4,0},{5,1},{6,2},{7,3},{8,12},{9,13},{10,... | collective-permute-start | bytes 110600 | tf_op jit(solution)/shard_map/ppermute | solution.py:30
  39.6 1.6 %collective-permute-done.7.refs_1_ = bf16[16,1152]{1,0:T(8,128)(2,1)S(1)} collective-permute-done((bf16[16,1152]{1,0:T(8,128)(2,1)S(1)}, bf16[16,1152]{1,0:T(8,128)(2,1)S(1)}, u32[]{:S(2)}, u32[]{:S(2)}) %collective-permute-start.7) | collective-permute-done | bytes 36896 | tf_op jit(solution)/shard_map/ppermute | solution.py:30
  41.1 0.4 collective-permute-done.8.refs_2_
  41.6 0.4 collective-permute-done.9.refs_3_
  41.9 0.9 %project.1 = (f32[16,3584]{1,0:T(8,128)S(1)}, bf16[16,3584]{1,0:T(8,128)(2,1)S(1)}) custom-call(f32[16,1152]{1,0:T(8,128)S(1)} %get-tuple-element.19.refs_0_, bf16[16,1152]{1,0:T(8,128)(2,1)S(1)} %collective-permute-done.7.refs_1_, bf16[16,1152]{1,0:T(8,128)(2,1)S(1)} %collective-permute-done.8.refs_2_, bf16[16,1152]{1,0:T(8,128)(2,1)S(1)} %collective-permute-done.9.refs_3_, ...), custom_call_target="tpu_custom_call" | custom-call | bytes 4460544 | tf_op jit(solution)/shard_map/project/pallas_call | solution.py:39
  42.8 0.0 collective-permute-start.10
  42.8 1.3 %collective-permute-done.10 = bf16[16,3584]{1,0:T(8,128)(2,1)S(1)} collective-permute-done((bf16[16,3584]{1,0:T(8,128)(2,1)S(1)}, bf16[16,3584]{1,0:T(8,128)(2,1)S(1)}, u32[]{:S(2)}, u32[]{:S(2)}) %collective-permute-start.10) | collective-permute-done | bytes 114720 | tf_op jit(solution)/shard_map/ppermute | solution.py:30
  44.2 1.6 %collective-permute-start.11 = (bf16[16,1792]{1,0:T(8,128)(2,1)S(1)}, bf16[16,1792]{1,0:T(8,128)(2,1)S(1)}, u32[]{:S(2)}, u32[]{:S(2)}) collective-permute-start(bf16[16,1792]{1,0:T(8,128)(2,1)S(1)} %slice.15), channel_id=1, source_target_pairs={{0,2},{1,3},{2,0},{3,1},{4,6},{5,7},{6,4},{7,5},{8,10},{9,11},{10,... | collective-permute-start | bytes 172040 | tf_op jit(solution)/shard_map/ppermute | solution.py:30
  45.8 2.7 %collective-permute-done.11 = bf16[16,1792]{1,0:T(8,128)(2,1)S(1)} collective-permute-done((bf16[16,1792]{1,0:T(8,128)(2,1)S(1)}, bf16[16,1792]{1,0:T(8,128)(2,1)S(1)}, u32[]{:S(2)}, u32[]{:S(2)}) %collective-permute-start.11) | collective-permute-done | bytes 57376 | tf_op jit(solution)/shard_map/ppermute | solution.py:30
  48.5 2.4 %collective-permute-start.14 = (bf16[16,1792]{1,0:T(8,128)(2,1)S(1)}, bf16[16,1792]{1,0:T(8,128)(2,1)S(1)}, u32[]{:S(2)}, u32[]{:S(2)}) collective-permute-start(bf16[16,1792]{1,0:T(8,128)(2,1)S(1)} %fusion), channel_id=1, source_target_pairs={{0,12},{1,13},{2,14},{3,15},{4,8},{5,9},{6,10},{7,11},{8,4},{9,5},... | collective-permute-start | bytes 172040 | tf_op jit(solution)/shard_map/ppermute | solution.py:30
  50.8 0.7 %collective-permute-start.13 = (bf16[16,1792]{1,0:T(8,128)(2,1)S(1)}, bf16[16,1792]{1,0:T(8,128)(2,1)S(1)}, u32[]{:S(2)}, u32[]{:S(2)}) collective-permute-start(bf16[16,1792]{1,0:T(8,128)(2,1)S(1)} %fusion), channel_id=1, source_target_pairs={{0,8},{1,9},{2,10},{3,11},{4,12},{5,13},{6,14},{7,15},{8,0},{9,1},... | collective-permute-start | bytes 172040 | tf_op jit(solution)/shard_map/ppermute | solution.py:30
  51.6 1.3 %collective-permute-start.12 = (bf16[16,1792]{1,0:T(8,128)(2,1)S(1)}, bf16[16,1792]{1,0:T(8,128)(2,1)S(1)}, u32[]{:S(2)}, u32[]{:S(2)}) collective-permute-start(bf16[16,1792]{1,0:T(8,128)(2,1)S(1)} %fusion), channel_id=1, source_target_pairs={{0,4},{1,5},{2,6},{3,7},{4,0},{5,1},{6,2},{7,3},{8,12},{9,13},{10,... | collective-permute-start | bytes 172040 | tf_op jit(solution)/shard_map/ppermute | solution.py:30
  52.9 1.9 %collective-permute-done.14 = bf16[16,1792]{1,0:T(8,128)(2,1)S(1)} collective-permute-done((bf16[16,1792]{1,0:T(8,128)(2,1)S(1)}, bf16[16,1792]{1,0:T(8,128)(2,1)S(1)}, u32[]{:S(2)}, u32[]{:S(2)}) %collective-permute-start.14) | collective-permute-done | bytes 57376 | tf_op jit(solution)/shard_map/ppermute | solution.py:30
  54.8 1.5 %collective-permute-done.13 = bf16[16,1792]{1,0:T(8,128)(2,1)S(1)} collective-permute-done((bf16[16,1792]{1,0:T(8,128)(2,1)S(1)}, bf16[16,1792]{1,0:T(8,128)(2,1)S(1)}, u32[]{:S(2)}, u32[]{:S(2)}) %collective-permute-start.13) | collective-permute-done | bytes 57376 | tf_op jit(solution)/shard_map/ppermute | solution.py:30
  56.4 1.6 %collective-permute-start.15 = (bf16[16,1792]{1,0:T(8,128)(2,1)S(1)}, bf16[16,1792]{1,0:T(8,128)(2,1)S(1)}, u32[]{:S(2)}, u32[]{:S(2)}) collective-permute-start(bf16[16,1792]{1,0:T(8,128)(2,1)S(1)} %add_convert_fusion), channel_id=1, source_target_pairs={{0,2},{1,3},{2,0},{3,1},{4,6},{5,7},{6,4},{7,5},{8,10},{9,11},{10,... | collective-permute-start | bytes 172040 | tf_op jit(solution)/shard_map/ppermute | solution.py:30
  58.0 2.7 %collective-permute-done.15 = bf16[16,1792]{1,0:T(8,128)(2,1)S(1)} collective-permute-done((bf16[16,1792]{1,0:T(8,128)(2,1)S(1)}, bf16[16,1792]{1,0:T(8,128)(2,1)S(1)}, u32[]{:S(2)}, u32[]{:S(2)}) %collective-permute-start.15) | collective-permute-done | bytes 57376 | tf_op jit(solution)/shard_map/ppermute | solution.py:30
  60.7 0.1 collective-permute-start.16
  60.7 1.3 %collective-permute-done.16.refs_1_ = bf16[16,3584]{1,0:T(8,128)(2,1)S(1)} collective-permute-done((bf16[16,3584]{1,0:T(8,128)(2,1)S(1)}, bf16[16,3584]{1,0:T(8,128)(2,1)S(1)}, u32[]{:S(2)}, u32[]{:S(2)}) %collective-permute-start.16) | collective-permute-done | bytes 114720 | tf_op jit(solution)/shard_map/ppermute | solution.py:30
  62.1 0.7 %place.1 = bf16[16,7168]{1,0:T(8,128)(2,1)} custom-call(bf16[16,3584]{1,0:T(8,128)(2,1)S(1)} %pad_maximum_fusion.1.refs_0_, bf16[16,3584]{1,0:T(8,128)(2,1)S(1)} %collective-permute-done.16.refs_1_), custom_call_target="tpu_custom_call" | custom-call | tf_op jit(solution)/shard_map/place/pallas_call | solution.py:377
  (19 shorter events, 0.2 us)
Async XLA Ops:
  0.0 1.1 %copy-start.1 = (bf16[1536,256]{1,0:T(8,128)(2,1)S(1)}, bf16[1536,256]{1,0:T(8,128)(2,1)}, u32[]{:S(2)}) copy-start(bf16[1536,256]{1,0:T(8,128)(2,1)} %refs_2_.1) | copy-start | bytes 2359300
  1.1 1.0 %copy-start.2 = (bf16[1536,128]{1,0:T(8,128)(2,1)S(1)}, bf16[1536,128]{1,0:T(8,128)(2,1)}, u32[]{:S(2)}) copy-start(bf16[1536,128]{1,0:T(8,128)(2,1)} %refs_3_.2) | copy-start | bytes 1179652
  2.1 0.9 %copy-start.4 = (bf16[2,128,512]{2,1,0:T(8,128)(2,1)S(1)}, bf16[2,128,512]{2,1,0:T(8,128)(2,1)}, u32[]{:S(2)}) copy-start(bf16[2,128,512]{2,1,0:T(8,128)(2,1)} %refs_4_.3) | copy-start | bytes 786436
  3.1 0.8 %copy-start.5 = (bf16[16,1536]{1,0:T(8,128)(2,1)S(1)}, bf16[16,1536]{1,0:T(8,128)(2,1)}, u32[]{:S(2)}) copy-start(bf16[16,1536]{1,0:T(8,128)(2,1)} %refs_0_.2) | copy-start | bytes 147460
  3.9 0.7 %copy-start.6 = (bf16[1536]{0:T(1024)(128)(2,1)S(1)}, bf16[1536]{0:T(1024)(128)(2,1)}, u32[]{:S(2)}) copy-start(bf16[1536]{0:T(1024)(128)(2,1)} %refs_1_.1) | copy-start | bytes 9220
  5.7 16.9 %copy-start.7 = (bf16[2,2048,512]{2,1,0:T(8,128)(2,1)S(1)}, bf16[2,2048,512]{2,1,0:T(8,128)(2,1)}, u32[]{:S(2)}) copy-start(bf16[2,2048,512]{2,1,0:T(8,128)(2,1)} %refs_3_.3) | copy-start | bytes 12582916
  5.8 16.9 %copy-start.8 = (bf16[2,64,2048]{2,1,0:T(8,128)(2,1)S(1)}, bf16[2,64,2048]{2,1,0:T(8,128)(2,1)}, u32[]{:S(2)}) copy-start(bf16[2,64,2048]{2,1,0:T(8,128)(2,1)} %refs_4_.4) | copy-start | bytes 1572868
  5.8 16.9 %copy-start.9 = (s32[2]{0:T(128)S(1)}, s32[2]{0:T(128)}, u32[]{:S(2)}) copy-start(s32[2]{0:T(128)} %refs_0_.3) | copy-start | bytes 28
  5.8 7.1 %collective-permute-start.2 = (bf16[16,1152]{1,0:T(8,128)(2,1)S(1)}, bf16[16,1152]{1,0:T(8,128)(2,1)S(1)}, u32[]{:S(2)}, u32[]{:S(2)}) collective-permute-start(bf16[16,1152]{1,0:T(8,128)(2,1)S(1)} %query.1.refs_0_), channel_id=1, source_target_pairs={{0,12},{1,13},{2,14},{3,15},{4,8},{5,9},{6,10},{7,11},{8,4},{9,5},... | collective-permute-start | bytes 110600 | tf_op jit(solution)/shard_map/ppermute | solution.py:30
  10.9 4.9 %collective-permute-start.1 = (bf16[16,1152]{1,0:T(8,128)(2,1)S(1)}, bf16[16,1152]{1,0:T(8,128)(2,1)S(1)}, u32[]{:S(2)}, u32[]{:S(2)}) collective-permute-start(bf16[16,1152]{1,0:T(8,128)(2,1)S(1)} %query.1.refs_0_), channel_id=1, source_target_pairs={{0,8},{1,9},{2,10},{3,11},{4,12},{5,13},{6,14},{7,15},{8,0},{9,1},... | collective-permute-start | bytes 110600 | tf_op jit(solution)/shard_map/ppermute | solution.py:30
  10.9 4.9 %collective-permute-start = (bf16[16,1152]{1,0:T(8,128)(2,1)S(1)}, bf16[16,1152]{1,0:T(8,128)(2,1)S(1)}, u32[]{:S(2)}, u32[]{:S(2)}) collective-permute-start(bf16[16,1152]{1,0:T(8,128)(2,1)S(1)} %query.1.refs_0_), channel_id=1, source_target_pairs={{0,4},{1,5},{2,6},{3,7},{4,0},{5,1},{6,2},{7,3},{8,12},{9,13},{10,... | collective-permute-start | bytes 110600 | tf_op jit(solution)/shard_map/ppermute | solution.py:30
  15.8 5.2 %collective-permute-start.3 = (bf16[64,1152]{1,0:T(8,128)(2,1)S(1)}, bf16[64,1152]{1,0:T(8,128)(2,1)S(1)}, u32[]{:S(2)}, u32[]{:S(2)}) collective-permute-start(bf16[64,1152]{1,0:T(8,128)(2,1)S(1)} %join.1), channel_id=1, source_target_pairs={{0,2},{1,3},{2,0},{3,1},{4,6},{5,7},{6,4},{7,5},{8,10},{9,11},{10,... | collective-permute-start | bytes 442376 | tf_op jit(solution)/shard_map/ppermute | solution.py:30
  21.0 20.9 %copy-start = (bf16[256,7168]{1,0:T(8,128)(2,1)S(1)}, bf16[256,7168]{1,0:T(8,128)(2,1)}, u32[]{:S(2)}) copy-start(bf16[256,7168]{1,0:T(8,128)(2,1)} %refs_5_.1) | copy-start | bytes 11010052
  21.0 20.9 %copy-start.3 = (bf16[2,512,128]{2,1,0:T(8,128)(2,1)S(1)}, bf16[2,512,128]{2,1,0:T(8,128)(2,1)}, u32[]{:S(2)}) copy-start(bf16[2,512,128]{2,1,0:T(8,128)(2,1)} %refs_4_.5) | copy-start | bytes 786436
  21.0 1.6 %collective-permute-start.4 = (bf16[128,1152]{1,0:T(8,128)(2,1)S(1)}, bf16[128,1152]{1,0:T(8,128)(2,1)S(1)}, u32[]{:S(2)}, u32[]{:S(2)}) collective-permute-start(bf16[128,1152]{1,0:T(8,128)(2,1)S(1)} %pad_maximum_fusion.refs_1_), channel_id=1, source_target_pairs={{0,1},{1,0},{2,3},{3,2},{4,5},{5,4},{6,7},{7,6},{8,9},{9,8},{10,11... | collective-permute-start | bytes 884744 | tf_op jit(solution)/shard_map/ppermute | solution.py:30
  26.9 1.6 %collective-permute-start.5 = (bf16[128,1152]{1,0:T(8,128)(2,1)S(1)}, bf16[128,1152]{1,0:T(8,128)(2,1)S(1)}, u32[]{:S(2)}, u32[]{:S(2)}) collective-permute-start(bf16[128,1152]{1,0:T(8,128)(2,1)S(1)} %get-tuple-element.16), channel_id=1, source_target_pairs={{0,1},{1,0},{2,3},{3,2},{4,5},{5,4},{6,7},{7,6},{8,9},{9,8},{10,11... | collective-permute-start | bytes 884744 | tf_op jit(solution)/shard_map/ppermute | solution.py:30
  28.9 6.0 %collective-permute-start.6 = (bf16[64,1152]{1,0:T(8,128)(2,1)S(1)}, bf16[64,1152]{1,0:T(8,128)(2,1)S(1)}, u32[]{:S(2)}, u32[]{:S(2)}) collective-permute-start(bf16[64,1152]{1,0:T(8,128)(2,1)S(1)} %get-tuple-element.18), channel_id=1, source_target_pairs={{0,2},{1,3},{2,0},{3,1},{4,6},{5,7},{6,4},{7,5},{8,10},{9,11},{10,... | collective-permute-start | bytes 442376 | tf_op jit(solution)/shard_map/ppermute | solution.py:30
  35.1 6.0 %collective-permute-start.7 = (bf16[16,1152]{1,0:T(8,128)(2,1)S(1)}, bf16[16,1152]{1,0:T(8,128)(2,1)S(1)}, u32[]{:S(2)}, u32[]{:S(2)}) collective-permute-start(bf16[16,1152]{1,0:T(8,128)(2,1)S(1)} %get-tuple-element.20), channel_id=1, source_target_pairs={{0,12},{1,13},{2,14},{3,15},{4,8},{5,9},{6,10},{7,11},{8,4},{9,5},... | collective-permute-start | bytes 110600 | tf_op jit(solution)/shard_map/ppermute | solution.py:30
  36.6 4.9 %collective-permute-start.8 = (bf16[16,1152]{1,0:T(8,128)(2,1)S(1)}, bf16[16,1152]{1,0:T(8,128)(2,1)S(1)}, u32[]{:S(2)}, u32[]{:S(2)}) collective-permute-start(bf16[16,1152]{1,0:T(8,128)(2,1)S(1)} %get-tuple-element.21), channel_id=1, source_target_pairs={{0,8},{1,9},{2,10},{3,11},{4,12},{5,13},{6,14},{7,15},{8,0},{9,1},... | collective-permute-start | bytes 110600 | tf_op jit(solution)/shard_map/ppermute | solution.py:30
  37.3 4.6 %collective-permute-start.9 = (bf16[16,1152]{1,0:T(8,128)(2,1)S(1)}, bf16[16,1152]{1,0:T(8,128)(2,1)S(1)}, u32[]{:S(2)}, u32[]{:S(2)}) collective-permute-start(bf16[16,1152]{1,0:T(8,128)(2,1)S(1)} %get-tuple-element.22), channel_id=1, source_target_pairs={{0,4},{1,5},{2,6},{3,7},{4,0},{5,1},{6,2},{7,3},{8,12},{9,13},{10,... | collective-permute-start | bytes 110600 | tf_op jit(solution)/shard_map/ppermute | solution.py:30
  42.8 1.4 %collective-permute-start.10 = (bf16[16,3584]{1,0:T(8,128)(2,1)S(1)}, bf16[16,3584]{1,0:T(8,128)(2,1)S(1)}, u32[]{:S(2)}, u32[]{:S(2)}) collective-permute-start(bf16[16,3584]{1,0:T(8,128)(2,1)S(1)} %get-tuple-element.24), channel_id=1, source_target_pairs={{0,1},{1,0},{2,3},{3,2},{4,5},{5,4},{6,7},{7,6},{8,9},{9,8},{10,11... | collective-permute-start | bytes 344072 | tf_op jit(solution)/shard_map/ppermute | solution.py:30
  44.2 4.2 %collective-permute-start.11 = (bf16[16,1792]{1,0:T(8,128)(2,1)S(1)}, bf16[16,1792]{1,0:T(8,128)(2,1)S(1)}, u32[]{:S(2)}, u32[]{:S(2)}) collective-permute-start(bf16[16,1792]{1,0:T(8,128)(2,1)S(1)} %slice.15), channel_id=1, source_target_pairs={{0,2},{1,3},{2,0},{3,1},{4,6},{5,7},{6,4},{7,5},{8,10},{9,11},{10,... | collective-permute-start | bytes 172040 | tf_op jit(solution)/shard_map/ppermute | solution.py:30
  48.5 6.4 %collective-permute-start.14 = (bf16[16,1792]{1,0:T(8,128)(2,1)S(1)}, bf16[16,1792]{1,0:T(8,128)(2,1)S(1)}, u32[]{:S(2)}, u32[]{:S(2)}) collective-permute-start(bf16[16,1792]{1,0:T(8,128)(2,1)S(1)} %fusion), channel_id=1, source_target_pairs={{0,12},{1,13},{2,14},{3,15},{4,8},{5,9},{6,10},{7,11},{8,4},{9,5},... | collective-permute-start | bytes 172040 | tf_op jit(solution)/shard_map/ppermute | solution.py:30
  50.8 5.5 %collective-permute-start.13 = (bf16[16,1792]{1,0:T(8,128)(2,1)S(1)}, bf16[16,1792]{1,0:T(8,128)(2,1)S(1)}, u32[]{:S(2)}, u32[]{:S(2)}) collective-permute-start(bf16[16,1792]{1,0:T(8,128)(2,1)S(1)} %fusion), channel_id=1, source_target_pairs={{0,8},{1,9},{2,10},{3,11},{4,12},{5,13},{6,14},{7,15},{8,0},{9,1},... | collective-permute-start | bytes 172040 | tf_op jit(solution)/shard_map/ppermute | solution.py:30
  51.6 4.8 %collective-permute-start.12 = (bf16[16,1792]{1,0:T(8,128)(2,1)S(1)}, bf16[16,1792]{1,0:T(8,128)(2,1)S(1)}, u32[]{:S(2)}, u32[]{:S(2)}) collective-permute-start(bf16[16,1792]{1,0:T(8,128)(2,1)S(1)} %fusion), channel_id=1, source_target_pairs={{0,4},{1,5},{2,6},{3,7},{4,0},{5,1},{6,2},{7,3},{8,12},{9,13},{10,... | collective-permute-start | bytes 172040 | tf_op jit(solution)/shard_map/ppermute | solution.py:30
  56.4 4.2 %collective-permute-start.15 = (bf16[16,1792]{1,0:T(8,128)(2,1)S(1)}, bf16[16,1792]{1,0:T(8,128)(2,1)S(1)}, u32[]{:S(2)}, u32[]{:S(2)}) collective-permute-start(bf16[16,1792]{1,0:T(8,128)(2,1)S(1)} %add_convert_fusion), channel_id=1, source_target_pairs={{0,2},{1,3},{2,0},{3,1},{4,6},{5,7},{6,4},{7,5},{8,10},{9,11},{10,... | collective-permute-start | bytes 172040 | tf_op jit(solution)/shard_map/ppermute | solution.py:30
  60.7 1.4 %collective-permute-start.16 = (bf16[16,3584]{1,0:T(8,128)(2,1)S(1)}, bf16[16,3584]{1,0:T(8,128)(2,1)S(1)}, u32[]{:S(2)}, u32[]{:S(2)}) collective-permute-start(bf16[16,3584]{1,0:T(8,128)(2,1)S(1)} %pad_maximum_fusion.1.refs_0_), channel_id=1, source_target_pairs={{0,1},{1,0},{2,3},{3,2},{4,5},{5,4},{6,7},{7,6},{8,9},{9,8},{10,11... | collective-permute-start | bytes 344072 | tf_op jit(solution)/shard_map/ppermute | solution.py:30

commit v3 on v2

--- a/solution.py
+++ b/solution.py
@@ -51,31 +51,24 @@
     return jax.ShapeDtypeStruct(shape, dtype)
 
 
-def query_body(heads, reqs, *refs):
-    sources, out_ref, (x_ref, gain_ref, nope_ref, rope_ref, key_ref), sems = (
-        refs[:5], refs[5], refs[6:11], refs[11]
-    )
-    copies = [
-        pltpu.make_async_copy(source, held, sems.at[i])
-        for i, (source, held) in enumerate(zip(sources, refs[6:11]))
-    ]
-    for copy in copies:
-        copy.start()
+def table_body(keys, table_ref):
+    table_ref[...] = (
+        lax.axis_index("ctx") * keys
+        + lax.broadcasted_iota(jnp.int32, table_ref.shape, 1)
+        - lax.broadcasted_iota(jnp.int32, table_ref.shape, 0)
+    )
+
+
+def query_body(heads, reqs, x_ref, gain_ref, nope_ref, rope_ref, key_ref, table_ref, out_ref):
     rows = x_ref.shape[0]
     stretch = rows // reqs
     nope_width, latent = key_ref.shape[1], key_ref.shape[2]
     rope_width = rope_ref.shape[1] // heads
-    copies[0].wait()
-    copies[1].wait()
     x = x_ref[...].astype(F32)
     mean = jnp.mean(x * x, axis=-1, keepdims=True)
-    gain = gain_ref[...].astype(F32).reshape(1, -1)
-    normed = (x * lax.rsqrt(mean + 1e-06) * gain).astype(BF16)
-    copies[2].wait()
+    normed = (x * lax.rsqrt(mean + 1e-06) * gain_ref[...].astype(F32).reshape(1, -1)).astype(BF16)
     nope = jnp.dot(normed, nope_ref[...], preferred_element_type=F32).astype(BF16)
-    copies[3].wait()
     rope = jnp.dot(normed, rope_ref[...], preferred_element_type=F32)
-    copies[4].wait()
     lat = [
         jnp.dot(
             nope[:, h * nope_width : (h + 1) * nope_width], key_ref[h], preferred_element_type=F32
@@ -136,10 +129,11 @@
 def attend_body(
     n_q, reqs, latent, rope_width, stretch, scale, chunk, *refs
 ):
-    length_ref, q_refs = refs[0], refs[1 : 1 + n_q]
-    lat_ref, rope_ref = refs[1 + n_q], refs[2 + n_q]
-    keep_ref, send_ref = refs[3 + n_q], refs[4 + n_q]
-    q_s, s_s = refs[5 + n_q], refs[6 + n_q]
+    length_ref, table_ref, refs = refs[0], refs[1], refs[2:]
+    q_refs = refs[:n_q]
+    lat_ref, rope_ref = refs[n_q], refs[1 + n_q]
+    keep_ref, send_ref = refs[2 + n_q], refs[3 + n_q]
+    q_s, s_s = refs[4 + n_q], refs[5 + n_q]
     rows = q_s.shape[0]
     half = rows // 2
     keys = lat_ref.shape[1]
@@ -147,18 +141,12 @@
     for q in q_refs:
         q_s[at : at + q.shape[0], :] = q[...]
         at += q.shape[0]
-    first_key = lax.axis_index("ctx") * keys
     block = min(rows, 256)
     for r0 in range(0, rows, block):
         rs = slice(r0, r0 + block)
         stats = []
         for b in range(reqs):
-            seen = (
-                length_ref[b]
-                - first_key
-                + lax.broadcasted_iota(jnp.int32, (stretch, chunk), 0)
-            )
-            lane = lax.broadcasted_iota(jnp.int32, (stretch, chunk), 1)
+            seen = length_ref[b]
             lhs = q_s[rs, b * latent : (b + 1) * latent]
             base = reqs * latent + b * rope_width
             lhs_rope = q_s[rs, base : base + rope_width]
@@ -172,7 +160,7 @@
                 ) + jnp.dot(
                     lhs_rope, rope_ref[b, :, k0 : k0 + chunk], preferred_element_type=F32
                 )
-                visible = (lane + k0) <= seen
+                visible = table_ref[...] + k0 <= seen
                 s = jnp.where(
                     visible[None], s.reshape(block // stretch, stretch, chunk), masked_score
                 ).reshape(block, chunk)
@@ -288,18 +276,22 @@
     stages = stage_list(count)
     scale = mscale_yarn * mscale_yarn / math.sqrt(nope_width + rope_width)
 
-    sources = [query_input, query_gain, nope_weight, rope_weight, key_up]
-    query = pl.pallas_call(
+    chunk = 512
+    (table,) = call(
+        functools.partial(table_body, cache_latent.shape[1]),
+        [spec((stretch, chunk), jnp.int32)],
+        [],
+        flops=2 << 30,
+        limit=16 << 20,
+        name="table",
+    )
+    (query,) = call(
         functools.partial(query_body, heads, reqs),
-        out_shape=spec((own, width), BF16),
-        in_specs=[pl.BlockSpec(memory_space=pl.ANY)] * len(sources),
-        out_specs=pl.BlockSpec(memory_space=pltpu.VMEM),
-        scratch_shapes=[pltpu.VMEM(a.shape, a.dtype) for a in sources]
-        + [pltpu.SemaphoreType.DMA((len(sources),))],
-        compiler_params=pltpu.CompilerParams(vmem_limit_bytes=24 << 20),
-        cost_estimate=pl.CostEstimate(flops=1 << 24, bytes_accessed=1 << 21, transcendentals=0),
+        [spec((own, width), BF16)],
+        [query_input, query_gain, nope_weight, rope_weight, key_up, table],
+        limit=16 << 20,
         name="query",
-    )(*sources)
+    )
     join_flops = 4 << 30
     held = query
     for stride, radix in reversed(stages[2:]):
@@ -320,12 +312,12 @@
     half = near.shape[0]
     total = 2 * half
     block = min(total, 256)
-    operands = [cached_length, near, far, cache_latent, cache_rope]
+    operands = [cached_length, table, near, far, cache_latent, cache_rope]
     keep, send = pl.pallas_call(
-        functools.partial(attend_body, 2, reqs, latent, rope_width, stretch, scale, 512),
+        functools.partial(attend_body, 2, reqs, latent, rope_width, stretch, scale, chunk),
         out_shape=(spec((half, width), F32), spec((half, width), BF16)),
         in_specs=[pl.BlockSpec(memory_space=pltpu.SMEM)]
-        + [pl.BlockSpec(memory_space=pltpu.VMEM)] * 4,
+        + [pl.BlockSpec(memory_space=pltpu.VMEM)] * 5,
         out_specs=(pl.BlockSpec(memory_space=pltpu.VMEM),) * 2,
         scratch_shapes=[
             pltpu.VMEM((total, width), BF16),

time: 63.1 us -> 59.1 us (0.937)
  local copies, waits for them, and re-layouts: 4.6 us -> 1.35 us
    unnamed x20, local copies, waits for them, and re-layouts: 4.59 us -> 1.34 us
    pallas_call x1 -> x0, Pallas kernels: 1.16 us -> none  [local(): pl.pallas_call(functools.partial(query_body, heads, reqs), out_shape=spec...]
    pallas_call x4 -> x6, Pallas kernels: 1.47 us -> 2.02 us  [call(): pl.pallas_call(body, out_shape=tuple(outs), in_specs=specs, out_specs=tup...]
where the time goes in v3:
time: 59.1 us; the launch traced here: 58.9 us
  waiting for transfers between devices  29 us (49%)
  starting transfers between devices  21.4 us (36%)
  Pallas kernels  6.94 us (12%)
  local copies, waits for them, and re-layouts  1.35 us (2%)
    ppermute x17, waiting for transfers between devices, swap(): return lax.ppermute(x, 'ctx', [(i, i ^ mask) for i in range(count)])  29 us
    ppermute x17, starting transfers between devices, swap(): return lax.ppermute(x, 'ctx', [(i, i ^ mask) for i in range(count)])  21.4 us
    pallas_call x1, Pallas kernels, local(): pl.pallas_call(functools.partial(attend_body, 2, reqs, latent, rope_width...  4.2 us
    pallas_call x6, Pallas kernels, call(): pl.pallas_call(body, out_shape=tuple(outs), in_specs=specs, out_specs=tup...  2.02 us
    unnamed x20, local copies, waits for them, and re-layouts  1.34 us
  transfers between devices with their start and end apart: 17, of which 15 were waited for; matrix products, arithmetic and copies ran while one was open for 0% of the time, Pallas kernels for 0%

profile of v3, /device:TPU:0, one launch (start us, length us, event | category | flops | bytes accessed | tf_op | source)
XLA Modules:
  0.0 58.9 jit_solution(9965069963948457210)
XLA Ops:
  0.0 0.9 %copy-done.4 = bf16[2,128,512]{2,1,0:T(8,128)(2,1)S(1)} copy-done((bf16[2,128,512]{2,1,0:T(8,128)(2,1)S(1)}, bf16[2,128,512]{2,1,0:T(8,128)(2,1)}, u32[]{:S(2)}) %copy-start.4) | copy-done | bytes 262168
  1.0 0.1 copy-done.2
  1.1 0.3 copy-done.1
  1.3 0.0 copy-done.6
  1.3 0.0 copy-done.5
  1.3 0.5 query.1.refs_0_
  1.9 0.0 copy-start.9
  1.9 5.1 %collective-permute-start.2 = (bf16[16,1152]{1,0:T(8,128)(2,1)S(1)}, bf16[16,1152]{1,0:T(8,128)(2,1)S(1)}, u32[]{:S(2)}, u32[]{:S(2)}) collective-permute-start(bf16[16,1152]{1,0:T(8,128)(2,1)S(1)} %query.1.refs_0_), channel_id=1, source_target_pairs={{0,12},{1,13},{2,14},{3,15},{4,8},{5,9},{6,10},{7,11},{8,4},{9,5},... | collective-permute-start | bytes 110600 | tf_op jit(solution)/shard_map/ppermute | solution.py:30
  7.0 0.0 collective-permute-start.1
  7.0 0.6 %collective-permute-start = (bf16[16,1152]{1,0:T(8,128)(2,1)S(1)}, bf16[16,1152]{1,0:T(8,128)(2,1)S(1)}, u32[]{:S(2)}, u32[]{:S(2)}) collective-permute-start(bf16[16,1152]{1,0:T(8,128)(2,1)S(1)} %query.1.refs_0_), channel_id=1, source_target_pairs={{0,4},{1,5},{2,6},{3,7},{4,0},{5,1},{6,2},{7,3},{8,12},{9,13},{10,... | collective-permute-start | bytes 110600 | tf_op jit(solution)/shard_map/ppermute | solution.py:30
  7.7 1.3 %collective-permute-done.2.refs_3_ = bf16[16,1152]{1,0:T(8,128)(2,1)S(1)} collective-permute-done((bf16[16,1152]{1,0:T(8,128)(2,1)S(1)}, bf16[16,1152]{1,0:T(8,128)(2,1)S(1)}, u32[]{:S(2)}, u32[]{:S(2)}) %collective-permute-start.2) | collective-permute-done | bytes 36896 | tf_op jit(solution)/shard_map/ppermute | solution.py:30
  9.0 2.9 %collective-permute-done.1.refs_2_ = bf16[16,1152]{1,0:T(8,128)(2,1)S(1)} collective-permute-done((bf16[16,1152]{1,0:T(8,128)(2,1)S(1)}, bf16[16,1152]{1,0:T(8,128)(2,1)S(1)}, u32[]{:S(2)}, u32[]{:S(2)}) %collective-permute-start.1) | collective-permute-done | bytes 36896 | tf_op jit(solution)/shard_map/ppermute | solution.py:30
  11.9 0.0 collective-permute-done.refs_1_
  11.9 1.6 %collective-permute-start.3 = (bf16[64,1152]{1,0:T(8,128)(2,1)S(1)}, bf16[64,1152]{1,0:T(8,128)(2,1)S(1)}, u32[]{:S(2)}, u32[]{:S(2)}) collective-permute-start(bf16[64,1152]{1,0:T(8,128)(2,1)S(1)} %join.1), channel_id=1, source_target_pairs={{0,2},{1,3},{2,0},{3,1},{4,6},{5,7},{6,4},{7,5},{8,10},{9,11},{10,... | collective-permute-start | bytes 442376 | tf_op jit(solution)/shard_map/ppermute | solution.py:30
  13.5 3.6 %collective-permute-done.3 = bf16[64,1152]{1,0:T(8,128)(2,1)S(1)} collective-permute-done((bf16[64,1152]{1,0:T(8,128)(2,1)S(1)}, bf16[64,1152]{1,0:T(8,128)(2,1)S(1)}, u32[]{:S(2)}, u32[]{:S(2)}) %collective-permute-start.3) | collective-permute-done | bytes 147488 | tf_op jit(solution)/shard_map/ppermute | solution.py:30
  17.1 0.0 copy-start
  17.1 0.0 copy-start.3
  17.2 0.1 collective-permute-start.4
  17.2 1.6 %collective-permute-done.4.refs_3_ = bf16[128,1152]{1,0:T(8,128)(2,1)S(1)} collective-permute-done((bf16[128,1152]{1,0:T(8,128)(2,1)S(1)}, bf16[128,1152]{1,0:T(8,128)(2,1)S(1)}, u32[]{:S(2)}, u32[]{:S(2)}) %collective-permute-start.4) | collective-permute-done | bytes 294944 | tf_op jit(solution)/shard_map/ppermute | solution.py:30
  18.8 4.2 %attend.1 = (f32[128,1152]{1,0:T(8,128)S(1)}, bf16[128,1152]{1,0:T(8,128)(2,1)S(1)}) custom-call(s32[2]{0:T(128)S(1)} %copy-done.9, s32[8,512]{1,0:T(8,128)S(1)} %table.1.table_ref.refs_1_, bf16[128,1152]{1,0:T(8,128)(2,1)S(1)} %pad_maximum_fusion.refs_2_, bf16[128,1152]{1,0:T(8,128)(2,1)S(1)} %collective-permute-done.4.refs_3_, ...), custom_call_target="tpu_custom_call" | custom-call | flops 2147483648 | bytes 8388608 | tf_op jit(solution)/shard_map/attend/pallas_call | solution.py:316
  23.0 0.2 collective-permute-start.5
  23.2 1.4 %collective-permute-done.5.refs_1_ = bf16[128,1152]{1,0:T(8,128)(2,1)S(1)} collective-permute-done((bf16[128,1152]{1,0:T(8,128)(2,1)S(1)}, bf16[128,1152]{1,0:T(8,128)(2,1)S(1)}, u32[]{:S(2)}, u32[]{:S(2)}) %collective-permute-start.5) | collective-permute-done | bytes 294944 | tf_op jit(solution)/shard_map/ppermute | solution.py:30
  24.7 0.3 merge.2
  25.0 1.6 %collective-permute-start.6 = (bf16[64,1152]{1,0:T(8,128)(2,1)S(1)}, bf16[64,1152]{1,0:T(8,128)(2,1)S(1)}, u32[]{:S(2)}, u32[]{:S(2)}) collective-permute-start(bf16[64,1152]{1,0:T(8,128)(2,1)S(1)} %get-tuple-element.18), channel_id=1, source_target_pairs={{0,2},{1,3},{2,0},{3,1},{4,6},{5,7},{6,4},{7,5},{8,10},{9,11},{10,... | collective-permute-start | bytes 442376 | tf_op jit(solution)/shard_map/ppermute | solution.py:30
  26.6 4.4 %collective-permute-done.6.refs_1_ = bf16[64,1152]{1,0:T(8,128)(2,1)S(1)} collective-permute-done((bf16[64,1152]{1,0:T(8,128)(2,1)S(1)}, bf16[64,1152]{1,0:T(8,128)(2,1)S(1)}, u32[]{:S(2)}, u32[]{:S(2)}) %collective-permute-start.6) | collective-permute-done | bytes 147488 | tf_op jit(solution)/shard_map/ppermute | solution.py:30
  31.0 0.2 merge.3
  31.2 1.5 %collective-permute-start.7 = (bf16[16,1152]{1,0:T(8,128)(2,1)S(1)}, bf16[16,1152]{1,0:T(8,128)(2,1)S(1)}, u32[]{:S(2)}, u32[]{:S(2)}) collective-permute-start(bf16[16,1152]{1,0:T(8,128)(2,1)S(1)} %get-tuple-element.20), channel_id=1, source_target_pairs={{0,12},{1,13},{2,14},{3,15},{4,8},{5,9},{6,10},{7,11},{8,4},{9,5},... | collective-permute-start | bytes 110600 | tf_op jit(solution)/shard_map/ppermute | solution.py:30
  32.8 0.6 %collective-permute-start.8 = (bf16[16,1152]{1,0:T(8,128)(2,1)S(1)}, bf16[16,1152]{1,0:T(8,128)(2,1)S(1)}, u32[]{:S(2)}, u32[]{:S(2)}) collective-permute-start(bf16[16,1152]{1,0:T(8,128)(2,1)S(1)} %get-tuple-element.21), channel_id=1, source_target_pairs={{0,8},{1,9},{2,10},{3,11},{4,12},{5,13},{6,14},{7,15},{8,0},{9,1},... | collective-permute-start | bytes 110600 | tf_op jit(solution)/shard_map/ppermute | solution.py:30
  33.4 2.3 %collective-permute-start.9 = (bf16[16,1152]{1,0:T(8,128)(2,1)S(1)}, bf16[16,1152]{1,0:T(8,128)(2,1)S(1)}, u32[]{:S(2)}, u32[]{:S(2)}) collective-permute-start(bf16[16,1152]{1,0:T(8,128)(2,1)S(1)} %get-tuple-element.22), channel_id=1, source_target_pairs={{0,4},{1,5},{2,6},{3,7},{4,0},{5,1},{6,2},{7,3},{8,12},{9,13},{10,... | collective-permute-start | bytes 110600 | tf_op jit(solution)/shard_map/ppermute | solution.py:30
  35.7 1.6 %collective-permute-done.7.refs_1_ = bf16[16,1152]{1,0:T(8,128)(2,1)S(1)} collective-permute-done((bf16[16,1152]{1,0:T(8,128)(2,1)S(1)}, bf16[16,1152]{1,0:T(8,128)(2,1)S(1)}, u32[]{:S(2)}, u32[]{:S(2)}) %collective-permute-start.7) | collective-permute-done | bytes 36896 | tf_op jit(solution)/shard_map/ppermute | solution.py:30
  37.3 0.4 collective-permute-done.8.refs_2_
  37.7 0.4 collective-permute-done.9.refs_3_
  38.1 0.9 %project.1 = (f32[16,3584]{1,0:T(8,128)S(1)}, bf16[16,3584]{1,0:T(8,128)(2,1)S(1)}) custom-call(f32[16,1152]{1,0:T(8,128)S(1)} %get-tuple-element.19.refs_0_, bf16[16,1152]{1,0:T(8,128)(2,1)S(1)} %collective-permute-done.7.refs_1_, bf16[16,1152]{1,0:T(8,128)(2,1)S(1)} %collective-permute-done.8.refs_2_, bf16[16,1152]{1,0:T(8,128)(2,1)S(1)} %collective-permute-done.9.refs_3_, ...), custom_call_target="tpu_custom_call" | custom-call | bytes 4460544 | tf_op jit(solution)/shard_map/project/pallas_call | solution.py:39
  38.9 0.0 collective-permute-start.10
  39.0 1.3 %collective-permute-done.10 = bf16[16,3584]{1,0:T(8,128)(2,1)S(1)} collective-permute-done((bf16[16,3584]{1,0:T(8,128)(2,1)S(1)}, bf16[16,3584]{1,0:T(8,128)(2,1)S(1)}, u32[]{:S(2)}, u32[]{:S(2)}) %collective-permute-start.10) | collective-permute-done | bytes 114720 | tf_op jit(solution)/shard_map/ppermute | solution.py:30
  40.3 1.6 %collective-permute-start.11 = (bf16[16,1792]{1,0:T(8,128)(2,1)S(1)}, bf16[16,1792]{1,0:T(8,128)(2,1)S(1)}, u32[]{:S(2)}, u32[]{:S(2)}) collective-permute-start(bf16[16,1792]{1,0:T(8,128)(2,1)S(1)} %slice.15), channel_id=1, source_target_pairs={{0,2},{1,3},{2,0},{3,1},{4,6},{5,7},{6,4},{7,5},{8,10},{9,11},{10,... | collective-permute-start | bytes 172040 | tf_op jit(solution)/shard_map/ppermute | solution.py:30
  41.9 2.7 %collective-permute-done.11 = bf16[16,1792]{1,0:T(8,128)(2,1)S(1)} collective-permute-done((bf16[16,1792]{1,0:T(8,128)(2,1)S(1)}, bf16[16,1792]{1,0:T(8,128)(2,1)S(1)}, u32[]{:S(2)}, u32[]{:S(2)}) %collective-permute-start.11) | collective-permute-done | bytes 57376 | tf_op jit(solution)/shard_map/ppermute | solution.py:30
  44.6 2.4 %collective-permute-start.14 = (bf16[16,1792]{1,0:T(8,128)(2,1)S(1)}, bf16[16,1792]{1,0:T(8,128)(2,1)S(1)}, u32[]{:S(2)}, u32[]{:S(2)}) collective-permute-start(bf16[16,1792]{1,0:T(8,128)(2,1)S(1)} %fusion), channel_id=1, source_target_pairs={{0,12},{1,13},{2,14},{3,15},{4,8},{5,9},{6,10},{7,11},{8,4},{9,5},... | collective-permute-start | bytes 172040 | tf_op jit(solution)/shard_map/ppermute | solution.py:30
  47.0 0.7 %collective-permute-start.13 = (bf16[16,1792]{1,0:T(8,128)(2,1)S(1)}, bf16[16,1792]{1,0:T(8,128)(2,1)S(1)}, u32[]{:S(2)}, u32[]{:S(2)}) collective-permute-start(bf16[16,1792]{1,0:T(8,128)(2,1)S(1)} %fusion), channel_id=1, source_target_pairs={{0,8},{1,9},{2,10},{3,11},{4,12},{5,13},{6,14},{7,15},{8,0},{9,1},... | collective-permute-start | bytes 172040 | tf_op jit(solution)/shard_map/ppermute | solution.py:30
  47.7 1.3 %collective-permute-start.12 = (bf16[16,1792]{1,0:T(8,128)(2,1)S(1)}, bf16[16,1792]{1,0:T(8,128)(2,1)S(1)}, u32[]{:S(2)}, u32[]{:S(2)}) collective-permute-start(bf16[16,1792]{1,0:T(8,128)(2,1)S(1)} %fusion), channel_id=1, source_target_pairs={{0,4},{1,5},{2,6},{3,7},{4,0},{5,1},{6,2},{7,3},{8,12},{9,13},{10,... | collective-permute-start | bytes 172040 | tf_op jit(solution)/shard_map/ppermute | solution.py:30
  49.1 1.9 %collective-permute-done.14 = bf16[16,1792]{1,0:T(8,128)(2,1)S(1)} collective-permute-done((bf16[16,1792]{1,0:T(8,128)(2,1)S(1)}, bf16[16,1792]{1,0:T(8,128)(2,1)S(1)}, u32[]{:S(2)}, u32[]{:S(2)}) %collective-permute-start.14) | collective-permute-done | bytes 57376 | tf_op jit(solution)/shard_map/ppermute | solution.py:30
  51.0 1.5 %collective-permute-done.13 = bf16[16,1792]{1,0:T(8,128)(2,1)S(1)} collective-permute-done((bf16[16,1792]{1,0:T(8,128)(2,1)S(1)}, bf16[16,1792]{1,0:T(8,128)(2,1)S(1)}, u32[]{:S(2)}, u32[]{:S(2)}) %collective-permute-start.13) | collective-permute-done | bytes 57376 | tf_op jit(solution)/shard_map/ppermute | solution.py:30
  52.5 0.0 collective-permute-done.12
  52.6 1.6 %collective-permute-start.15 = (bf16[16,1792]{1,0:T(8,128)(2,1)S(1)}, bf16[16,1792]{1,0:T(8,128)(2,1)S(1)}, u32[]{:S(2)}, u32[]{:S(2)}) collective-permute-start(bf16[16,1792]{1,0:T(8,128)(2,1)S(1)} %add_convert_fusion), channel_id=1, source_target_pairs={{0,2},{1,3},{2,0},{3,1},{4,6},{5,7},{6,4},{7,5},{8,10},{9,11},{10,... | collective-permute-start | bytes 172040 | tf_op jit(solution)/shard_map/ppermute | solution.py:30
  54.1 2.7 %collective-permute-done.15 = bf16[16,1792]{1,0:T(8,128)(2,1)S(1)} collective-permute-done((bf16[16,1792]{1,0:T(8,128)(2,1)S(1)}, bf16[16,1792]{1,0:T(8,128)(2,1)S(1)}, u32[]{:S(2)}, u32[]{:S(2)}) %collective-permute-start.15) | collective-permute-done | bytes 57376 | tf_op jit(solution)/shard_map/ppermute | solution.py:30
  56.8 0.1 collective-permute-start.16
  56.9 1.3 %collective-permute-done.16.refs_1_ = bf16[16,3584]{1,0:T(8,128)(2,1)S(1)} collective-permute-done((bf16[16,3584]{1,0:T(8,128)(2,1)S(1)}, bf16[16,3584]{1,0:T(8,128)(2,1)S(1)}, u32[]{:S(2)}, u32[]{:S(2)}) %collective-permute-start.16) | collective-permute-done | bytes 114720 | tf_op jit(solution)/shard_map/ppermute | solution.py:30
  58.2 0.7 %place.1 = bf16[16,7168]{1,0:T(8,128)(2,1)} custom-call(bf16[16,3584]{1,0:T(8,128)(2,1)S(1)} %pad_maximum_fusion.1.refs_0_, bf16[16,3584]{1,0:T(8,128)(2,1)S(1)} %collective-permute-done.16.refs_1_), custom_call_target="tpu_custom_call" | custom-call | tf_op jit(solution)/shard_map/place/pallas_call | solution.py:369
  (20 shorter events, 0.2 us)
Async XLA Ops:
  0.0 0.9 %copy-start.4 = (bf16[2,128,512]{2,1,0:T(8,128)(2,1)S(1)}, bf16[2,128,512]{2,1,0:T(8,128)(2,1)}, u32[]{:S(2)}) copy-start(bf16[2,128,512]{2,1,0:T(8,128)(2,1)} %key_ref.1) | copy-start | bytes 786436
  0.0 1.1 %copy-start.2 = (bf16[1536,128]{1,0:T(8,128)(2,1)S(1)}, bf16[1536,128]{1,0:T(8,128)(2,1)}, u32[]{:S(2)}) copy-start(bf16[1536,128]{1,0:T(8,128)(2,1)} %rope_ref.1) | copy-start | bytes 1179652
  0.0 1.3 %copy-start.1 = (bf16[1536,256]{1,0:T(8,128)(2,1)S(1)}, bf16[1536,256]{1,0:T(8,128)(2,1)}, u32[]{:S(2)}) copy-start(bf16[1536,256]{1,0:T(8,128)(2,1)} %nope_ref.1) | copy-start | bytes 2359300
  0.0 1.3 %copy-start.6 = (bf16[1536]{0:T(1024)(128)(2,1)S(1)}, bf16[1536]{0:T(1024)(128)(2,1)}, u32[]{:S(2)}) copy-start(bf16[1536]{0:T(1024)(128)(2,1)} %gain_ref.1) | copy-start | bytes 9220
  0.0 1.3 %copy-start.5 = (bf16[16,1536]{1,0:T(8,128)(2,1)S(1)}, bf16[16,1536]{1,0:T(8,128)(2,1)}, u32[]{:S(2)}) copy-start(bf16[16,1536]{1,0:T(8,128)(2,1)} %x_ref.1) | copy-start | bytes 147460
  1.9 16.9 %copy-start.7 = (bf16[2,2048,512]{2,1,0:T(8,128)(2,1)S(1)}, bf16[2,2048,512]{2,1,0:T(8,128)(2,1)}, u32[]{:S(2)}) copy-start(bf16[2,2048,512]{2,1,0:T(8,128)(2,1)} %refs_4_.2) | copy-start | bytes 12582916
  1.9 16.9 %copy-start.8 = (bf16[2,64,2048]{2,1,0:T(8,128)(2,1)S(1)}, bf16[2,64,2048]{2,1,0:T(8,128)(2,1)}, u32[]{:S(2)}) copy-start(bf16[2,64,2048]{2,1,0:T(8,128)(2,1)} %refs_5_.2) | copy-start | bytes 1572868
  1.9 16.9 %copy-start.9 = (s32[2]{0:T(128)S(1)}, s32[2]{0:T(128)}, u32[]{:S(2)}) copy-start(s32[2]{0:T(128)} %refs_0_.1) | copy-start | bytes 28
  1.9 7.1 %collective-permute-start.2 = (bf16[16,1152]{1,0:T(8,128)(2,1)S(1)}, bf16[16,1152]{1,0:T(8,128)(2,1)S(1)}, u32[]{:S(2)}, u32[]{:S(2)}) collective-permute-start(bf16[16,1152]{1,0:T(8,128)(2,1)S(1)} %query.1.refs_0_), channel_id=1, source_target_pairs={{0,12},{1,13},{2,14},{3,15},{4,8},{5,9},{6,10},{7,11},{8,4},{9,5},... | collective-permute-start | bytes 110600 | tf_op jit(solution)/shard_map/ppermute | solution.py:30
  7.0 4.9 %collective-permute-start.1 = (bf16[16,1152]{1,0:T(8,128)(2,1)S(1)}, bf16[16,1152]{1,0:T(8,128)(2,1)S(1)}, u32[]{:S(2)}, u32[]{:S(2)}) collective-permute-start(bf16[16,1152]{1,0:T(8,128)(2,1)S(1)} %query.1.refs_0_), channel_id=1, source_target_pairs={{0,8},{1,9},{2,10},{3,11},{4,12},{5,13},{6,14},{7,15},{8,0},{9,1},... | collective-permute-start | bytes 110600 | tf_op jit(solution)/shard_map/ppermute | solution.py:30
  7.0 4.9 %collective-permute-start = (bf16[16,1152]{1,0:T(8,128)(2,1)S(1)}, bf16[16,1152]{1,0:T(8,128)(2,1)S(1)}, u32[]{:S(2)}, u32[]{:S(2)}) collective-permute-start(bf16[16,1152]{1,0:T(8,128)(2,1)S(1)} %query.1.refs_0_), channel_id=1, source_target_pairs={{0,4},{1,5},{2,6},{3,7},{4,0},{5,1},{6,2},{7,3},{8,12},{9,13},{10,... | collective-permute-start | bytes 110600 | tf_op jit(solution)/shard_map/ppermute | solution.py:30
  11.9 5.2 %collective-permute-start.3 = (bf16[64,1152]{1,0:T(8,128)(2,1)S(1)}, bf16[64,1152]{1,0:T(8,128)(2,1)S(1)}, u32[]{:S(2)}, u32[]{:S(2)}) collective-permute-start(bf16[64,1152]{1,0:T(8,128)(2,1)S(1)} %join.1), channel_id=1, source_target_pairs={{0,2},{1,3},{2,0},{3,1},{4,6},{5,7},{6,4},{7,5},{8,10},{9,11},{10,... | collective-permute-start | bytes 442376 | tf_op jit(solution)/shard_map/ppermute | solution.py:30
  17.1 20.9 %copy-start = (bf16[256,7168]{1,0:T(8,128)(2,1)S(1)}, bf16[256,7168]{1,0:T(8,128)(2,1)}, u32[]{:S(2)}) copy-start(bf16[256,7168]{1,0:T(8,128)(2,1)} %refs_5_.3) | copy-start | bytes 11010052
  17.1 20.9 %copy-start.3 = (bf16[2,512,128]{2,1,0:T(8,128)(2,1)S(1)}, bf16[2,512,128]{2,1,0:T(8,128)(2,1)}, u32[]{:S(2)}) copy-start(bf16[2,512,128]{2,1,0:T(8,128)(2,1)} %refs_4_.3) | copy-start | bytes 786436
  17.2 1.6 %collective-permute-start.4 = (bf16[128,1152]{1,0:T(8,128)(2,1)S(1)}, bf16[128,1152]{1,0:T(8,128)(2,1)S(1)}, u32[]{:S(2)}, u32[]{:S(2)}) collective-permute-start(bf16[128,1152]{1,0:T(8,128)(2,1)S(1)} %pad_maximum_fusion.refs_2_), channel_id=1, source_target_pairs={{0,1},{1,0},{2,3},{3,2},{4,5},{5,4},{6,7},{7,6},{8,9},{9,8},{10,11... | collective-permute-start | bytes 884744 | tf_op jit(solution)/shard_map/ppermute | solution.py:30
  23.0 1.6 %collective-permute-start.5 = (bf16[128,1152]{1,0:T(8,128)(2,1)S(1)}, bf16[128,1152]{1,0:T(8,128)(2,1)S(1)}, u32[]{:S(2)}, u32[]{:S(2)}) collective-permute-start(bf16[128,1152]{1,0:T(8,128)(2,1)S(1)} %get-tuple-element.16), channel_id=1, source_target_pairs={{0,1},{1,0},{2,3},{3,2},{4,5},{5,4},{6,7},{7,6},{8,9},{9,8},{10,11... | collective-permute-start | bytes 884744 | tf_op jit(solution)/shard_map/ppermute | solution.py:30
  25.0 6.0 %collective-permute-start.6 = (bf16[64,1152]{1,0:T(8,128)(2,1)S(1)}, bf16[64,1152]{1,0:T(8,128)(2,1)S(1)}, u32[]{:S(2)}, u32[]{:S(2)}) collective-permute-start(bf16[64,1152]{1,0:T(8,128)(2,1)S(1)} %get-tuple-element.18), channel_id=1, source_target_pairs={{0,2},{1,3},{2,0},{3,1},{4,6},{5,7},{6,4},{7,5},{8,10},{9,11},{10,... | collective-permute-start | bytes 442376 | tf_op jit(solution)/shard_map/ppermute | solution.py:30
  31.2 6.0 %collective-permute-start.7 = (bf16[16,1152]{1,0:T(8,128)(2,1)S(1)}, bf16[16,1152]{1,0:T(8,128)(2,1)S(1)}, u32[]{:S(2)}, u32[]{:S(2)}) collective-permute-start(bf16[16,1152]{1,0:T(8,128)(2,1)S(1)} %get-tuple-element.20), channel_id=1, source_target_pairs={{0,12},{1,13},{2,14},{3,15},{4,8},{5,9},{6,10},{7,11},{8,4},{9,5},... | collective-permute-start | bytes 110600 | tf_op jit(solution)/shard_map/ppermute | solution.py:30
  32.8 4.9 %collective-permute-start.8 = (bf16[16,1152]{1,0:T(8,128)(2,1)S(1)}, bf16[16,1152]{1,0:T(8,128)(2,1)S(1)}, u32[]{:S(2)}, u32[]{:S(2)}) collective-permute-start(bf16[16,1152]{1,0:T(8,128)(2,1)S(1)} %get-tuple-element.21), channel_id=1, source_target_pairs={{0,8},{1,9},{2,10},{3,11},{4,12},{5,13},{6,14},{7,15},{8,0},{9,1},... | collective-permute-start | bytes 110600 | tf_op jit(solution)/shard_map/ppermute | solution.py:30
  33.4 4.7 %collective-permute-start.9 = (bf16[16,1152]{1,0:T(8,128)(2,1)S(1)}, bf16[16,1152]{1,0:T(8,128)(2,1)S(1)}, u32[]{:S(2)}, u32[]{:S(2)}) collective-permute-start(bf16[16,1152]{1,0:T(8,128)(2,1)S(1)} %get-tuple-element.22), channel_id=1, source_target_pairs={{0,4},{1,5},{2,6},{3,7},{4,0},{5,1},{6,2},{7,3},{8,12},{9,13},{10,... | collective-permute-start | bytes 110600 | tf_op jit(solution)/shard_map/ppermute | solution.py:30
  38.9 1.4 %collective-permute-start.10 = (bf16[16,3584]{1,0:T(8,128)(2,1)S(1)}, bf16[16,3584]{1,0:T(8,128)(2,1)S(1)}, u32[]{:S(2)}, u32[]{:S(2)}) collective-permute-start(bf16[16,3584]{1,0:T(8,128)(2,1)S(1)} %get-tuple-element.24), channel_id=1, source_target_pairs={{0,1},{1,0},{2,3},{3,2},{4,5},{5,4},{6,7},{7,6},{8,9},{9,8},{10,11... | collective-permute-start | bytes 344072 | tf_op jit(solution)/shard_map/ppermute | solution.py:30
  40.3 4.2 %collective-permute-start.11 = (bf16[16,1792]{1,0:T(8,128)(2,1)S(1)}, bf16[16,1792]{1,0:T(8,128)(2,1)S(1)}, u32[]{:S(2)}, u32[]{:S(2)}) collective-permute-start(bf16[16,1792]{1,0:T(8,128)(2,1)S(1)} %slice.15), channel_id=1, source_target_pairs={{0,2},{1,3},{2,0},{3,1},{4,6},{5,7},{6,4},{7,5},{8,10},{9,11},{10,... | collective-permute-start | bytes 172040 | tf_op jit(solution)/shard_map/ppermute | solution.py:30
  44.6 6.4 %collective-permute-start.14 = (bf16[16,1792]{1,0:T(8,128)(2,1)S(1)}, bf16[16,1792]{1,0:T(8,128)(2,1)S(1)}, u32[]{:S(2)}, u32[]{:S(2)}) collective-permute-start(bf16[16,1792]{1,0:T(8,128)(2,1)S(1)} %fusion), channel_id=1, source_target_pairs={{0,12},{1,13},{2,14},{3,15},{4,8},{5,9},{6,10},{7,11},{8,4},{9,5},... | collective-permute-start | bytes 172040 | tf_op jit(solution)/shard_map/ppermute | solution.py:30
  47.0 5.5 %collective-permute-start.13 = (bf16[16,1792]{1,0:T(8,128)(2,1)S(1)}, bf16[16,1792]{1,0:T(8,128)(2,1)S(1)}, u32[]{:S(2)}, u32[]{:S(2)}) collective-permute-start(bf16[16,1792]{1,0:T(8,128)(2,1)S(1)} %fusion), channel_id=1, source_target_pairs={{0,8},{1,9},{2,10},{3,11},{4,12},{5,13},{6,14},{7,15},{8,0},{9,1},... | collective-permute-start | bytes 172040 | tf_op jit(solution)/shard_map/ppermute | solution.py:30
  47.7 4.8 %collective-permute-start.12 = (bf16[16,1792]{1,0:T(8,128)(2,1)S(1)}, bf16[16,1792]{1,0:T(8,128)(2,1)S(1)}, u32[]{:S(2)}, u32[]{:S(2)}) collective-permute-start(bf16[16,1792]{1,0:T(8,128)(2,1)S(1)} %fusion), channel_id=1, source_target_pairs={{0,4},{1,5},{2,6},{3,7},{4,0},{5,1},{6,2},{7,3},{8,12},{9,13},{10,... | collective-permute-start | bytes 172040 | tf_op jit(solution)/shard_map/ppermute | solution.py:30
  52.6 4.2 %collective-permute-start.15 = (bf16[16,1792]{1,0:T(8,128)(2,1)S(1)}, bf16[16,1792]{1,0:T(8,128)(2,1)S(1)}, u32[]{:S(2)}, u32[]{:S(2)}) collective-permute-start(bf16[16,1792]{1,0:T(8,128)(2,1)S(1)} %add_convert_fusion), channel_id=1, source_target_pairs={{0,2},{1,3},{2,0},{3,1},{4,6},{5,7},{6,4},{7,5},{8,10},{9,11},{10,... | collective-permute-start | bytes 172040 | tf_op jit(solution)/shard_map/ppermute | solution.py:30
  56.8 1.4 %collective-permute-start.16 = (bf16[16,3584]{1,0:T(8,128)(2,1)S(1)}, bf16[16,3584]{1,0:T(8,128)(2,1)S(1)}, u32[]{:S(2)}, u32[]{:S(2)}) collective-permute-start(bf16[16,3584]{1,0:T(8,128)(2,1)S(1)} %pad_maximum_fusion.1.refs_0_), channel_id=1, source_target_pairs={{0,1},{1,0},{2,3},{3,2},{4,5},{5,4},{6,7},{7,6},{8,9},{9,8},{10,11... | collective-permute-start | bytes 344072 | tf_op jit(solution)/shard_map/ppermute | solution.py:30

commit v4 on v3

--- a/solution.py
+++ b/solution.py
@@ -24,6 +24,14 @@
         stages.append((stride, radix))
         stride *= radix
     return stages
+
+
+def hop(j, stride):
+    return j * stride + (1 if j > 1 else 0)
+
+
+def beside_rel(e):
+    return (e & 1) ^ (3 if e & 2 else 0)
 
 
 def swap(x, count, mask):
@@ -133,7 +141,7 @@
     q_refs = refs[:n_q]
     lat_ref, rope_ref = refs[n_q], refs[1 + n_q]
     keep_ref, send_ref = refs[2 + n_q], refs[3 + n_q]
-    q_s, s_s = refs[4 + n_q], refs[5 + n_q]
+    q_s, s_s, w_s = refs[4 + n_q :]
     rows = q_s.shape[0]
     half = rows // 2
     keys = lat_ref.shape[1]
@@ -144,7 +152,7 @@
     block = min(rows, 256)
     for r0 in range(0, rows, block):
         rs = slice(r0, r0 + block)
-        stats = []
+        stats, peaks = [], []
         for b in range(reqs):
             seen = length_ref[b]
             lhs = q_s[rs, b * latent : (b + 1) * latent]
@@ -167,15 +175,16 @@
                 s_s[b, :, k0 : k0 + chunk] = s
                 top = jnp.max(s, axis=1, keepdims=True)
                 peak = top if peak is None else jnp.maximum(peak, top)
-            total, pool = None, None
+            peaks.append(peak)
+        for b in range(reqs):
+            peak = peaks[b]
+            total = None
             for k0 in range(0, keys, chunk):
                 w = jnp.exp2((s_s[b, :, k0 : k0 + chunk] - peak) * (scale * LOG2E))
                 part = jnp.sum(w, axis=1, keepdims=True)
-                term = jnp.dot(
-                    w.astype(BF16), lat_ref[b, k0 : k0 + chunk, :], preferred_element_type=F32
-                )
                 total = part if total is None else total + part
-                pool = term if pool is None else pool + term
+                w_s[b, :, k0 : k0 + chunk] = w.astype(BF16)
+            pool = jnp.dot(w_s[b], lat_ref[b], preferred_element_type=F32)
             pool = pool * (1.0 / total)
             stats.append(peak * scale + jnp.log(total))
             cols = slice(b * latent, (b + 1) * latent)
@@ -225,7 +234,7 @@
     mine = lax.rem(lax.axis_index("ctx"), parts_out)
     width = weight_ref.shape[1] // parts_out
     for e in range(parts_out):
-        start = pl.multiple_of(jnp.bitwise_xor(mine, e) * width, LANES)
+        start = pl.multiple_of(jnp.bitwise_xor(mine, beside_rel(e)) * width, LANES)
         out = jnp.dot(hidden, weight_ref[:, pl.ds(start, width)], preferred_element_type=F32)
         slot = slice((e // 2) * width, (e // 2 + 1) * width)
         if e % 2 == 0:
@@ -250,7 +259,7 @@
     at = 0
     for piece in pieces:
         for k in range(piece.shape[1] // width):
-            start = pl.multiple_of(jnp.bitwise_xor(mine, e_order[at]) * width, LANES)
+            start = pl.multiple_of(jnp.bitwise_xor(mine, beside_rel(e_order[at])) * width, LANES)
             copies.append(
                 pltpu.make_async_copy(
                     piece.at[:, pl.ds(k * width, width)],
@@ -276,7 +285,7 @@
     stages = stage_list(count)
     scale = mscale_yarn * mscale_yarn / math.sqrt(nope_width + rope_width)
 
-    chunk = 512
+    chunk = 256
     (table,) = call(
         functools.partial(table_body, cache_latent.shape[1]),
         [spec((stretch, chunk), jnp.int32)],
@@ -295,7 +304,7 @@
     join_flops = 4 << 30
     held = query
     for stride, radix in reversed(stages[2:]):
-        got = [swap(held, count, j * stride) for j in range(1, radix)]
+        got = [swap(held, count, hop(j, stride)) for j in range(1, radix)]
         parts = [held] + got
         (held,) = call(
             join_body,
@@ -322,6 +331,7 @@
         scratch_shapes=[
             pltpu.VMEM((total, width), BF16),
             pltpu.VMEM((reqs, block, cache_latent.shape[1]), F32),
+            pltpu.VMEM((reqs, block, cache_latent.shape[1]), BF16),
         ],
         compiler_params=pltpu.CompilerParams(vmem_limit_bytes=48 << 20),
         cost_estimate=pl.CostEstimate(
@@ -342,7 +352,7 @@
             name="merge",
         )
         keep = pieces[0]
-        got = [swap(pieces[j], count, j * stride) for j in reversed(range(1, radix))]
+        got = [swap(pieces[j], count, hop(j, stride)) for j in reversed(range(1, radix))]
 
     parts_out = 4
     model = out_weight.shape[1]
@@ -354,7 +364,7 @@
         name="project",
     )
     kept = keep + swap(send, count, stages[0][0]).astype(F32)
-    kept = kept[:, :quarter] + swap(kept[:, quarter:].astype(BF16), count, stages[1][0]).astype(F32)
+    kept = kept[:, :quarter] + swap(kept[:, quarter:].astype(BF16), count, beside_rel(2)).astype(F32)
     for stride, radix in stages[2:]:
         mine = kept.astype(BF16)
         terms = [mine.astype(F32)] + [
@@ -364,7 +374,7 @@
             terms = [terms[i] + terms[i + 1] for i in range(0, len(terms), 2)]
         kept = terms[0]
     done = kept.astype(BF16)
-    both = jnp.concatenate([done, swap(done, count, stages[1][0])], axis=1)
+    both = jnp.concatenate([done, swap(done, count, beside_rel(2))], axis=1)
     other = swap(both, count, stages[0][0])
     return pl.pallas_call(
         functools.partial(place_body, parts_out),

time: 59.1 us -> 59.3 us (level)
  waiting for transfers between devices: 29 us -> 31.4 us
  starting transfers between devices: 21.4 us -> 19.6 us
    ppermute x17, waiting for transfers between devices: 29 us -> 31.4 us  [swap(): return lax.ppermute(x, 'ctx', [(i, i ^ mask) for i in range(count)])]
    ppermute x17, starting transfers between devices: 21.4 us -> 19.6 us  [swap(): return lax.ppermute(x, 'ctx', [(i, i ^ mask) for i in range(count)])]
where the time goes in v4:
time: 59.3 us; the launch traced here: 59.2 us
  waiting for transfers between devices  31.4 us (53%)
  starting transfers between devices  19.6 us (33%)
  Pallas kernels  6.61 us (11%)
  local copies, waits for them, and re-layouts  1.35 us (2%)
    ppermute x17, waiting for transfers between devices, swap(): return lax.ppermute(x, 'ctx', [(i, i ^ mask) for i in range(count)])  31.4 us
    ppermute x17, starting transfers between devices, swap(): return lax.ppermute(x, 'ctx', [(i, i ^ mask) for i in range(count)])  19.6 us
    pallas_call x1, Pallas kernels, local(): pl.pallas_call(functools.partial(attend_body, 2, reqs, latent, rope_width...  3.88 us
    pallas_call x6, Pallas kernels, call(): pl.pallas_call(body, out_shape=tuple(outs), in_specs=specs, out_specs=tup...  2.03 us
    unnamed x20, local copies, waits for them, and re-layouts  1.34 us
  transfers between devices with their start and end apart: 17, of which 15 were waited for; matrix products, arithmetic and copies ran while one was open for 0% of the time, Pallas kernels for 0%

profile of v4, /device:TPU:0, one launch (start us, length us, event | category | flops | bytes accessed | tf_op | source)
XLA Modules:
  0.0 59.2 jit_solution(9114549445401259412)
XLA Ops:
  0.0 0.9 %copy-done.4 = bf16[2,128,512]{2,1,0:T(8,128)(2,1)S(1)} copy-done((bf16[2,128,512]{2,1,0:T(8,128)(2,1)S(1)}, bf16[2,128,512]{2,1,0:T(8,128)(2,1)}, u32[]{:S(2)}) %copy-start.4) | copy-done | bytes 262168
  1.0 0.1 copy-done.2
  1.1 0.3 copy-done.1
  1.3 0.0 copy-done.6
  1.3 0.0 copy-done.5
  1.3 0.5 query.1.refs_0_
  1.9 0.0 copy-start.9
  1.9 4.6 %collective-permute-start.2 = (bf16[16,1152]{1,0:T(8,128)(2,1)S(1)}, bf16[16,1152]{1,0:T(8,128)(2,1)S(1)}, u32[]{:S(2)}, u32[]{:S(2)}) collective-permute-start(bf16[16,1152]{1,0:T(8,128)(2,1)S(1)} %query.1.refs_0_), channel_id=1, source_target_pairs={{0,13},{1,12},{2,15},{3,14},{4,9},{5,8},{6,11},{7,10},{8,5},{9,4},... | collective-permute-start | bytes 110600 | tf_op jit(solution)/shard_map/ppermute | solution.py:38
  6.5 0.0 collective-permute-start.1
  6.5 0.6 %collective-permute-start = (bf16[16,1152]{1,0:T(8,128)(2,1)S(1)}, bf16[16,1152]{1,0:T(8,128)(2,1)S(1)}, u32[]{:S(2)}, u32[]{:S(2)}) collective-permute-start(bf16[16,1152]{1,0:T(8,128)(2,1)S(1)} %query.1.refs_0_), channel_id=1, source_target_pairs={{0,4},{1,5},{2,6},{3,7},{4,0},{5,1},{6,2},{7,3},{8,12},{9,13},{10,... | collective-permute-start | bytes 110600 | tf_op jit(solution)/shard_map/ppermute | solution.py:38
  7.1 1.2 %collective-permute-done.2.refs_3_ = bf16[16,1152]{1,0:T(8,128)(2,1)S(1)} collective-permute-done((bf16[16,1152]{1,0:T(8,128)(2,1)S(1)}, bf16[16,1152]{1,0:T(8,128)(2,1)S(1)}, u32[]{:S(2)}, u32[]{:S(2)}) %collective-permute-start.2) | collective-permute-done | bytes 36896 | tf_op jit(solution)/shard_map/ppermute | solution.py:38
  8.3 2.7 %collective-permute-done.1.refs_2_ = bf16[16,1152]{1,0:T(8,128)(2,1)S(1)} collective-permute-done((bf16[16,1152]{1,0:T(8,128)(2,1)S(1)}, bf16[16,1152]{1,0:T(8,128)(2,1)S(1)}, u32[]{:S(2)}, u32[]{:S(2)}) %collective-permute-start.1) | collective-permute-done | bytes 36896 | tf_op jit(solution)/shard_map/ppermute | solution.py:38
  11.0 0.0 collective-permute-done.refs_1_
  11.0 1.6 %collective-permute-start.3 = (bf16[64,1152]{1,0:T(8,128)(2,1)S(1)}, bf16[64,1152]{1,0:T(8,128)(2,1)S(1)}, u32[]{:S(2)}, u32[]{:S(2)}) collective-permute-start(bf16[64,1152]{1,0:T(8,128)(2,1)S(1)} %join.1), channel_id=1, source_target_pairs={{0,2},{1,3},{2,0},{3,1},{4,6},{5,7},{6,4},{7,5},{8,10},{9,11},{10,... | collective-permute-start | bytes 442376 | tf_op jit(solution)/shard_map/ppermute | solution.py:38
  12.6 4.7 %collective-permute-done.3 = bf16[64,1152]{1,0:T(8,128)(2,1)S(1)} collective-permute-done((bf16[64,1152]{1,0:T(8,128)(2,1)S(1)}, bf16[64,1152]{1,0:T(8,128)(2,1)S(1)}, u32[]{:S(2)}, u32[]{:S(2)}) %collective-permute-start.3) | collective-permute-done | bytes 147488 | tf_op jit(solution)/shard_map/ppermute | solution.py:38
  17.3 0.0 copy-start
  17.3 0.0 copy-start.3
  17.3 0.1 collective-permute-start.4
  17.4 1.6 %collective-permute-done.4.refs_3_ = bf16[128,1152]{1,0:T(8,128)(2,1)S(1)} collective-permute-done((bf16[128,1152]{1,0:T(8,128)(2,1)S(1)}, bf16[128,1152]{1,0:T(8,128)(2,1)S(1)}, u32[]{:S(2)}, u32[]{:S(2)}) %collective-permute-start.4) | collective-permute-done | bytes 294944 | tf_op jit(solution)/shard_map/ppermute | solution.py:38
  19.0 3.9 %attend.1 = (f32[128,1152]{1,0:T(8,128)S(1)}, bf16[128,1152]{1,0:T(8,128)(2,1)S(1)}) custom-call(s32[2]{0:T(128)S(1)} %copy-done.9, s32[8,256]{1,0:T(8,128)S(1)} %table.1.table_ref.refs_1_, bf16[128,1152]{1,0:T(8,128)(2,1)S(1)} %pad_maximum_fusion.refs_2_, bf16[128,1152]{1,0:T(8,128)(2,1)S(1)} %collective-permute-done.4.refs_3_, ...), custom_call_target="tpu_custom_call" | custom-call | flops 2147483648 | bytes 8388608 | tf_op jit(solution)/shard_map/attend/pallas_call | solution.py:325
  22.9 0.2 collective-permute-start.5
  23.0 1.5 %collective-permute-done.5.refs_1_ = bf16[128,1152]{1,0:T(8,128)(2,1)S(1)} collective-permute-done((bf16[128,1152]{1,0:T(8,128)(2,1)S(1)}, bf16[128,1152]{1,0:T(8,128)(2,1)S(1)}, u32[]{:S(2)}, u32[]{:S(2)}) %collective-permute-start.5) | collective-permute-done | bytes 294944 | tf_op jit(solution)/shard_map/ppermute | solution.py:38
  24.5 0.4 merge.2
  24.9 1.6 %collective-permute-start.6 = (bf16[64,1152]{1,0:T(8,128)(2,1)S(1)}, bf16[64,1152]{1,0:T(8,128)(2,1)S(1)}, u32[]{:S(2)}, u32[]{:S(2)}) collective-permute-start(bf16[64,1152]{1,0:T(8,128)(2,1)S(1)} %get-tuple-element.18), channel_id=1, source_target_pairs={{0,2},{1,3},{2,0},{3,1},{4,6},{5,7},{6,4},{7,5},{8,10},{9,11},{10,... | collective-permute-start | bytes 442376 | tf_op jit(solution)/shard_map/ppermute | solution.py:38
  26.4 4.4 %collective-permute-done.6.refs_1_ = bf16[64,1152]{1,0:T(8,128)(2,1)S(1)} collective-permute-done((bf16[64,1152]{1,0:T(8,128)(2,1)S(1)}, bf16[64,1152]{1,0:T(8,128)(2,1)S(1)}, u32[]{:S(2)}, u32[]{:S(2)}) %collective-permute-start.6) | collective-permute-done | bytes 147488 | tf_op jit(solution)/shard_map/ppermute | solution.py:38
  30.8 0.2 merge.3
  31.1 1.0 %collective-permute-start.7 = (bf16[16,1152]{1,0:T(8,128)(2,1)S(1)}, bf16[16,1152]{1,0:T(8,128)(2,1)S(1)}, u32[]{:S(2)}, u32[]{:S(2)}) collective-permute-start(bf16[16,1152]{1,0:T(8,128)(2,1)S(1)} %get-tuple-element.20), channel_id=1, source_target_pairs={{0,13},{1,12},{2,15},{3,14},{4,9},{5,8},{6,11},{7,10},{8,5},{9,4},... | collective-permute-start | bytes 110600 | tf_op jit(solution)/shard_map/ppermute | solution.py:38
  32.0 1.3 %collective-permute-start.8 = (bf16[16,1152]{1,0:T(8,128)(2,1)S(1)}, bf16[16,1152]{1,0:T(8,128)(2,1)S(1)}, u32[]{:S(2)}, u32[]{:S(2)}) collective-permute-start(bf16[16,1152]{1,0:T(8,128)(2,1)S(1)} %get-tuple-element.21), channel_id=1, source_target_pairs={{0,9},{1,8},{2,11},{3,10},{4,13},{5,12},{6,15},{7,14},{8,1},{9,0},... | collective-permute-start | bytes 110600 | tf_op jit(solution)/shard_map/ppermute | solution.py:38
  33.4 1.9 %collective-permute-start.9 = (bf16[16,1152]{1,0:T(8,128)(2,1)S(1)}, bf16[16,1152]{1,0:T(8,128)(2,1)S(1)}, u32[]{:S(2)}, u32[]{:S(2)}) collective-permute-start(bf16[16,1152]{1,0:T(8,128)(2,1)S(1)} %get-tuple-element.22), channel_id=1, source_target_pairs={{0,4},{1,5},{2,6},{3,7},{4,0},{5,1},{6,2},{7,3},{8,12},{9,13},{10,... | collective-permute-start | bytes 110600 | tf_op jit(solution)/shard_map/ppermute | solution.py:38
  35.2 1.2 %collective-permute-done.7.refs_1_ = bf16[16,1152]{1,0:T(8,128)(2,1)S(1)} collective-permute-done((bf16[16,1152]{1,0:T(8,128)(2,1)S(1)}, bf16[16,1152]{1,0:T(8,128)(2,1)S(1)}, u32[]{:S(2)}, u32[]{:S(2)}) %collective-permute-start.7) | collective-permute-done | bytes 36896 | tf_op jit(solution)/shard_map/ppermute | solution.py:38
  36.5 1.2 %collective-permute-done.8.refs_2_ = bf16[16,1152]{1,0:T(8,128)(2,1)S(1)} collective-permute-done((bf16[16,1152]{1,0:T(8,128)(2,1)S(1)}, bf16[16,1152]{1,0:T(8,128)(2,1)S(1)}, u32[]{:S(2)}, u32[]{:S(2)}) %collective-permute-start.8) | collective-permute-done | bytes 36896 | tf_op jit(solution)/shard_map/ppermute | solution.py:38
  37.6 0.2 collective-permute-done.9.refs_3_
  37.8 0.9 %project.1 = (f32[16,3584]{1,0:T(8,128)S(1)}, bf16[16,3584]{1,0:T(8,128)(2,1)S(1)}) custom-call(f32[16,1152]{1,0:T(8,128)S(1)} %get-tuple-element.19.refs_0_, bf16[16,1152]{1,0:T(8,128)(2,1)S(1)} %collective-permute-done.7.refs_1_, bf16[16,1152]{1,0:T(8,128)(2,1)S(1)} %collective-permute-done.8.refs_2_, bf16[16,1152]{1,0:T(8,128)(2,1)S(1)} %collective-permute-done.9.refs_3_, ...), custom_call_target="tpu_custom_call" | custom-call | bytes 4460544 | tf_op jit(solution)/shard_map/project/pallas_call | solution.py:47
  38.7 0.0 collective-permute-start.10
  38.7 1.3 %collective-permute-done.10 = bf16[16,3584]{1,0:T(8,128)(2,1)S(1)} collective-permute-done((bf16[16,3584]{1,0:T(8,128)(2,1)S(1)}, bf16[16,3584]{1,0:T(8,128)(2,1)S(1)}, u32[]{:S(2)}, u32[]{:S(2)}) %collective-permute-start.10) | collective-permute-done | bytes 114720 | tf_op jit(solution)/shard_map/ppermute | solution.py:38
  40.1 1.2 %collective-permute-start.11 = (bf16[16,1792]{1,0:T(8,128)(2,1)S(1)}, bf16[16,1792]{1,0:T(8,128)(2,1)S(1)}, u32[]{:S(2)}, u32[]{:S(2)}) collective-permute-start(bf16[16,1792]{1,0:T(8,128)(2,1)S(1)} %slice.15), channel_id=1, source_target_pairs={{0,3},{1,2},{2,1},{3,0},{4,7},{5,6},{6,5},{7,4},{8,11},{9,10},{10,... | collective-permute-start | bytes 172040 | tf_op jit(solution)/shard_map/ppermute | solution.py:38
  41.3 2.7 %collective-permute-done.11 = bf16[16,1792]{1,0:T(8,128)(2,1)S(1)} collective-permute-done((bf16[16,1792]{1,0:T(8,128)(2,1)S(1)}, bf16[16,1792]{1,0:T(8,128)(2,1)S(1)}, u32[]{:S(2)}, u32[]{:S(2)}) %collective-permute-start.11) | collective-permute-done | bytes 57376 | tf_op jit(solution)/shard_map/ppermute | solution.py:38
  44.0 2.2 %collective-permute-start.14 = (bf16[16,1792]{1,0:T(8,128)(2,1)S(1)}, bf16[16,1792]{1,0:T(8,128)(2,1)S(1)}, u32[]{:S(2)}, u32[]{:S(2)}) collective-permute-start(bf16[16,1792]{1,0:T(8,128)(2,1)S(1)} %fusion), channel_id=1, source_target_pairs={{0,12},{1,13},{2,14},{3,15},{4,8},{5,9},{6,10},{7,11},{8,4},{9,5},... | collective-permute-start | bytes 172040 | tf_op jit(solution)/shard_map/ppermute | solution.py:38
  46.3 0.7 %collective-permute-start.13 = (bf16[16,1792]{1,0:T(8,128)(2,1)S(1)}, bf16[16,1792]{1,0:T(8,128)(2,1)S(1)}, u32[]{:S(2)}, u32[]{:S(2)}) collective-permute-start(bf16[16,1792]{1,0:T(8,128)(2,1)S(1)} %fusion), channel_id=1, source_target_pairs={{0,8},{1,9},{2,10},{3,11},{4,12},{5,13},{6,14},{7,15},{8,0},{9,1},... | collective-permute-start | bytes 172040 | tf_op jit(solution)/shard_map/ppermute | solution.py:38
  47.0 1.5 %collective-permute-start.12 = (bf16[16,1792]{1,0:T(8,128)(2,1)S(1)}, bf16[16,1792]{1,0:T(8,128)(2,1)S(1)}, u32[]{:S(2)}, u32[]{:S(2)}) collective-permute-start(bf16[16,1792]{1,0:T(8,128)(2,1)S(1)} %fusion), channel_id=1, source_target_pairs={{0,4},{1,5},{2,6},{3,7},{4,0},{5,1},{6,2},{7,3},{8,12},{9,13},{10,... | collective-permute-start | bytes 172040 | tf_op jit(solution)/shard_map/ppermute | solution.py:38
  48.5 2.2 %collective-permute-done.14 = bf16[16,1792]{1,0:T(8,128)(2,1)S(1)} collective-permute-done((bf16[16,1792]{1,0:T(8,128)(2,1)S(1)}, bf16[16,1792]{1,0:T(8,128)(2,1)S(1)}, u32[]{:S(2)}, u32[]{:S(2)}) %collective-permute-start.14) | collective-permute-done | bytes 57376 | tf_op jit(solution)/shard_map/ppermute | solution.py:38
  50.7 2.1 %collective-permute-done.13 = bf16[16,1792]{1,0:T(8,128)(2,1)S(1)} collective-permute-done((bf16[16,1792]{1,0:T(8,128)(2,1)S(1)}, bf16[16,1792]{1,0:T(8,128)(2,1)S(1)}, u32[]{:S(2)}, u32[]{:S(2)}) %collective-permute-start.13) | collective-permute-done | bytes 57376 | tf_op jit(solution)/shard_map/ppermute | solution.py:38
  52.8 0.0 collective-permute-done.12
  52.8 0.9 %collective-permute-start.15 = (bf16[16,1792]{1,0:T(8,128)(2,1)S(1)}, bf16[16,1792]{1,0:T(8,128)(2,1)S(1)}, u32[]{:S(2)}, u32[]{:S(2)}) collective-permute-start(bf16[16,1792]{1,0:T(8,128)(2,1)S(1)} %add_convert_fusion), channel_id=1, source_target_pairs={{0,3},{1,2},{2,1},{3,0},{4,7},{5,6},{6,5},{7,4},{8,11},{9,10},{10,... | collective-permute-start | bytes 172040 | tf_op jit(solution)/shard_map/ppermute | solution.py:38
  53.8 3.3 %collective-permute-done.15 = bf16[16,1792]{1,0:T(8,128)(2,1)S(1)} collective-permute-done((bf16[16,1792]{1,0:T(8,128)(2,1)S(1)}, bf16[16,1792]{1,0:T(8,128)(2,1)S(1)}, u32[]{:S(2)}, u32[]{:S(2)}) %collective-permute-start.15) | collective-permute-done | bytes 57376 | tf_op jit(solution)/shard_map/ppermute | solution.py:38
  57.1 0.2 collective-permute-start.16
  57.3 1.2 %collective-permute-done.16.refs_1_ = bf16[16,3584]{1,0:T(8,128)(2,1)S(1)} collective-permute-done((bf16[16,3584]{1,0:T(8,128)(2,1)S(1)}, bf16[16,3584]{1,0:T(8,128)(2,1)S(1)}, u32[]{:S(2)}, u32[]{:S(2)}) %collective-permute-start.16) | collective-permute-done | bytes 114720 | tf_op jit(solution)/shard_map/ppermute | solution.py:38
  58.5 0.7 %place.1 = bf16[16,7168]{1,0:T(8,128)(2,1)} custom-call(bf16[16,3584]{1,0:T(8,128)(2,1)S(1)} %pad_maximum_fusion.1.refs_0_, bf16[16,3584]{1,0:T(8,128)(2,1)S(1)} %collective-permute-done.16.refs_1_), custom_call_target="tpu_custom_call" | custom-call | tf_op jit(solution)/shard_map/place/pallas_call | solution.py:379
  (20 shorter events, 0.2 us)
Async XLA Ops:
  0.0 0.9 %copy-start.4 = (bf16[2,128,512]{2,1,0:T(8,128)(2,1)S(1)}, bf16[2,128,512]{2,1,0:T(8,128)(2,1)}, u32[]{:S(2)}) copy-start(bf16[2,128,512]{2,1,0:T(8,128)(2,1)} %key_ref.1) | copy-start | bytes 786436
  0.0 1.1 %copy-start.2 = (bf16[1536,128]{1,0:T(8,128)(2,1)S(1)}, bf16[1536,128]{1,0:T(8,128)(2,1)}, u32[]{:S(2)}) copy-start(bf16[1536,128]{1,0:T(8,128)(2,1)} %rope_ref.1) | copy-start | bytes 1179652
  0.0 1.3 %copy-start.1 = (bf16[1536,256]{1,0:T(8,128)(2,1)S(1)}, bf16[1536,256]{1,0:T(8,128)(2,1)}, u32[]{:S(2)}) copy-start(bf16[1536,256]{1,0:T(8,128)(2,1)} %nope_ref.1) | copy-start | bytes 2359300
  0.0 1.3 %copy-start.6 = (bf16[1536]{0:T(1024)(128)(2,1)S(1)}, bf16[1536]{0:T(1024)(128)(2,1)}, u32[]{:S(2)}) copy-start(bf16[1536]{0:T(1024)(128)(2,1)} %gain_ref.1) | copy-start | bytes 9220
  0.0 1.3 %copy-start.5 = (bf16[16,1536]{1,0:T(8,128)(2,1)S(1)}, bf16[16,1536]{1,0:T(8,128)(2,1)}, u32[]{:S(2)}) copy-start(bf16[16,1536]{1,0:T(8,128)(2,1)} %x_ref.1) | copy-start | bytes 147460
  1.9 17.1 %copy-start.7 = (bf16[2,2048,512]{2,1,0:T(8,128)(2,1)S(1)}, bf16[2,2048,512]{2,1,0:T(8,128)(2,1)}, u32[]{:S(2)}) copy-start(bf16[2,2048,512]{2,1,0:T(8,128)(2,1)} %refs_4_.2) | copy-start | bytes 12582916
  1.9 17.1 %copy-start.8 = (bf16[2,64,2048]{2,1,0:T(8,128)(2,1)S(1)}, bf16[2,64,2048]{2,1,0:T(8,128)(2,1)}, u32[]{:S(2)}) copy-start(bf16[2,64,2048]{2,1,0:T(8,128)(2,1)} %refs_5_.2) | copy-start | bytes 1572868
  1.9 17.1 %copy-start.9 = (s32[2]{0:T(128)S(1)}, s32[2]{0:T(128)}, u32[]{:S(2)}) copy-start(s32[2]{0:T(128)} %refs_0_.1) | copy-start | bytes 28
  1.9 6.4 %collective-permute-start.2 = (bf16[16,1152]{1,0:T(8,128)(2,1)S(1)}, bf16[16,1152]{1,0:T(8,128)(2,1)S(1)}, u32[]{:S(2)}, u32[]{:S(2)}) collective-permute-start(bf16[16,1152]{1,0:T(8,128)(2,1)S(1)} %query.1.refs_0_), channel_id=1, source_target_pairs={{0,13},{1,12},{2,15},{3,14},{4,9},{5,8},{6,11},{7,10},{8,5},{9,4},... | collective-permute-start | bytes 110600 | tf_op jit(solution)/shard_map/ppermute | solution.py:38
  6.5 4.5 %collective-permute-start.1 = (bf16[16,1152]{1,0:T(8,128)(2,1)S(1)}, bf16[16,1152]{1,0:T(8,128)(2,1)S(1)}, u32[]{:S(2)}, u32[]{:S(2)}) collective-permute-start(bf16[16,1152]{1,0:T(8,128)(2,1)S(1)} %query.1.refs_0_), channel_id=1, source_target_pairs={{0,9},{1,8},{2,11},{3,10},{4,13},{5,12},{6,15},{7,14},{8,1},{9,0},... | collective-permute-start | bytes 110600 | tf_op jit(solution)/shard_map/ppermute | solution.py:38
  6.5 4.5 %collective-permute-start = (bf16[16,1152]{1,0:T(8,128)(2,1)S(1)}, bf16[16,1152]{1,0:T(8,128)(2,1)S(1)}, u32[]{:S(2)}, u32[]{:S(2)}) collective-permute-start(bf16[16,1152]{1,0:T(8,128)(2,1)S(1)} %query.1.refs_0_), channel_id=1, source_target_pairs={{0,4},{1,5},{2,6},{3,7},{4,0},{5,1},{6,2},{7,3},{8,12},{9,13},{10,... | collective-permute-start | bytes 110600 | tf_op jit(solution)/shard_map/ppermute | solution.py:38
  11.0 6.3 %collective-permute-start.3 = (bf16[64,1152]{1,0:T(8,128)(2,1)S(1)}, bf16[64,1152]{1,0:T(8,128)(2,1)S(1)}, u32[]{:S(2)}, u32[]{:S(2)}) collective-permute-start(bf16[64,1152]{1,0:T(8,128)(2,1)S(1)} %join.1), channel_id=1, source_target_pairs={{0,2},{1,3},{2,0},{3,1},{4,6},{5,7},{6,4},{7,5},{8,10},{9,11},{10,... | collective-permute-start | bytes 442376 | tf_op jit(solution)/shard_map/ppermute | solution.py:38
  17.3 20.5 %copy-start = (bf16[256,7168]{1,0:T(8,128)(2,1)S(1)}, bf16[256,7168]{1,0:T(8,128)(2,1)}, u32[]{:S(2)}) copy-start(bf16[256,7168]{1,0:T(8,128)(2,1)} %refs_5_.3) | copy-start | bytes 11010052
  17.3 20.5 %copy-start.3 = (bf16[2,512,128]{2,1,0:T(8,128)(2,1)S(1)}, bf16[2,512,128]{2,1,0:T(8,128)(2,1)}, u32[]{:S(2)}) copy-start(bf16[2,512,128]{2,1,0:T(8,128)(2,1)} %refs_4_.3) | copy-start | bytes 786436
  17.3 1.6 %collective-permute-start.4 = (bf16[128,1152]{1,0:T(8,128)(2,1)S(1)}, bf16[128,1152]{1,0:T(8,128)(2,1)S(1)}, u32[]{:S(2)}, u32[]{:S(2)}) collective-permute-start(bf16[128,1152]{1,0:T(8,128)(2,1)S(1)} %pad_maximum_fusion.refs_2_), channel_id=1, source_target_pairs={{0,1},{1,0},{2,3},{3,2},{4,5},{5,4},{6,7},{7,6},{8,9},{9,8},{10,11... | collective-permute-start | bytes 884744 | tf_op jit(solution)/shard_map/ppermute | solution.py:38
  22.9 1.6 %collective-permute-start.5 = (bf16[128,1152]{1,0:T(8,128)(2,1)S(1)}, bf16[128,1152]{1,0:T(8,128)(2,1)S(1)}, u32[]{:S(2)}, u32[]{:S(2)}) collective-permute-start(bf16[128,1152]{1,0:T(8,128)(2,1)S(1)} %get-tuple-element.16), channel_id=1, source_target_pairs={{0,1},{1,0},{2,3},{3,2},{4,5},{5,4},{6,7},{7,6},{8,9},{9,8},{10,11... | collective-permute-start | bytes 884744 | tf_op jit(solution)/shard_map/ppermute | solution.py:38
  24.9 6.0 %collective-permute-start.6 = (bf16[64,1152]{1,0:T(8,128)(2,1)S(1)}, bf16[64,1152]{1,0:T(8,128)(2,1)S(1)}, u32[]{:S(2)}, u32[]{:S(2)}) collective-permute-start(bf16[64,1152]{1,0:T(8,128)(2,1)S(1)} %get-tuple-element.18), channel_id=1, source_target_pairs={{0,2},{1,3},{2,0},{3,1},{4,6},{5,7},{6,4},{7,5},{8,10},{9,11},{10,... | collective-permute-start | bytes 442376 | tf_op jit(solution)/shard_map/ppermute | solution.py:38
  31.1 5.4 %collective-permute-start.7 = (bf16[16,1152]{1,0:T(8,128)(2,1)S(1)}, bf16[16,1152]{1,0:T(8,128)(2,1)S(1)}, u32[]{:S(2)}, u32[]{:S(2)}) collective-permute-start(bf16[16,1152]{1,0:T(8,128)(2,1)S(1)} %get-tuple-element.20), channel_id=1, source_target_pairs={{0,13},{1,12},{2,15},{3,14},{4,9},{5,8},{6,11},{7,10},{8,5},{9,4},... | collective-permute-start | bytes 110600 | tf_op jit(solution)/shard_map/ppermute | solution.py:38
  32.0 5.6 %collective-permute-start.8 = (bf16[16,1152]{1,0:T(8,128)(2,1)S(1)}, bf16[16,1152]{1,0:T(8,128)(2,1)S(1)}, u32[]{:S(2)}, u32[]{:S(2)}) collective-permute-start(bf16[16,1152]{1,0:T(8,128)(2,1)S(1)} %get-tuple-element.21), channel_id=1, source_target_pairs={{0,9},{1,8},{2,11},{3,10},{4,13},{5,12},{6,15},{7,14},{8,1},{9,0},... | collective-permute-start | bytes 110600 | tf_op jit(solution)/shard_map/ppermute | solution.py:38
  33.4 4.4 %collective-permute-start.9 = (bf16[16,1152]{1,0:T(8,128)(2,1)S(1)}, bf16[16,1152]{1,0:T(8,128)(2,1)S(1)}, u32[]{:S(2)}, u32[]{:S(2)}) collective-permute-start(bf16[16,1152]{1,0:T(8,128)(2,1)S(1)} %get-tuple-element.22), channel_id=1, source_target_pairs={{0,4},{1,5},{2,6},{3,7},{4,0},{5,1},{6,2},{7,3},{8,12},{9,13},{10,... | collective-permute-start | bytes 110600 | tf_op jit(solution)/shard_map/ppermute | solution.py:38
  38.7 1.4 %collective-permute-start.10 = (bf16[16,3584]{1,0:T(8,128)(2,1)S(1)}, bf16[16,3584]{1,0:T(8,128)(2,1)S(1)}, u32[]{:S(2)}, u32[]{:S(2)}) collective-permute-start(bf16[16,3584]{1,0:T(8,128)(2,1)S(1)} %get-tuple-element.24), channel_id=1, source_target_pairs={{0,1},{1,0},{2,3},{3,2},{4,5},{5,4},{6,7},{7,6},{8,9},{9,8},{10,11... | collective-permute-start | bytes 344072 | tf_op jit(solution)/shard_map/ppermute | solution.py:38
  40.1 3.9 %collective-permute-start.11 = (bf16[16,1792]{1,0:T(8,128)(2,1)S(1)}, bf16[16,1792]{1,0:T(8,128)(2,1)S(1)}, u32[]{:S(2)}, u32[]{:S(2)}) collective-permute-start(bf16[16,1792]{1,0:T(8,128)(2,1)S(1)} %slice.15), channel_id=1, source_target_pairs={{0,3},{1,2},{2,1},{3,0},{4,7},{5,6},{6,5},{7,4},{8,11},{9,10},{10,... | collective-permute-start | bytes 172040 | tf_op jit(solution)/shard_map/ppermute | solution.py:38
  44.0 6.6 %collective-permute-start.14 = (bf16[16,1792]{1,0:T(8,128)(2,1)S(1)}, bf16[16,1792]{1,0:T(8,128)(2,1)S(1)}, u32[]{:S(2)}, u32[]{:S(2)}) collective-permute-start(bf16[16,1792]{1,0:T(8,128)(2,1)S(1)} %fusion), channel_id=1, source_target_pairs={{0,12},{1,13},{2,14},{3,15},{4,8},{5,9},{6,10},{7,11},{8,4},{9,5},... | collective-permute-start | bytes 172040 | tf_op jit(solution)/shard_map/ppermute | solution.py:38
  46.3 6.5 %collective-permute-start.13 = (bf16[16,1792]{1,0:T(8,128)(2,1)S(1)}, bf16[16,1792]{1,0:T(8,128)(2,1)S(1)}, u32[]{:S(2)}, u32[]{:S(2)}) collective-permute-start(bf16[16,1792]{1,0:T(8,128)(2,1)S(1)} %fusion), channel_id=1, source_target_pairs={{0,8},{1,9},{2,10},{3,11},{4,12},{5,13},{6,14},{7,15},{8,0},{9,1},... | collective-permute-start | bytes 172040 | tf_op jit(solution)/shard_map/ppermute | solution.py:38
  47.0 5.8 %collective-permute-start.12 = (bf16[16,1792]{1,0:T(8,128)(2,1)S(1)}, bf16[16,1792]{1,0:T(8,128)(2,1)S(1)}, u32[]{:S(2)}, u32[]{:S(2)}) collective-permute-start(bf16[16,1792]{1,0:T(8,128)(2,1)S(1)} %fusion), channel_id=1, source_target_pairs={{0,4},{1,5},{2,6},{3,7},{4,0},{5,1},{6,2},{7,3},{8,12},{9,13},{10,... | collective-permute-start | bytes 172040 | tf_op jit(solution)/shard_map/ppermute | solution.py:38
  52.8 4.2 %collective-permute-start.15 = (bf16[16,1792]{1,0:T(8,128)(2,1)S(1)}, bf16[16,1792]{1,0:T(8,128)(2,1)S(1)}, u32[]{:S(2)}, u32[]{:S(2)}) collective-permute-start(bf16[16,1792]{1,0:T(8,128)(2,1)S(1)} %add_convert_fusion), channel_id=1, source_target_pairs={{0,3},{1,2},{2,1},{3,0},{4,7},{5,6},{6,5},{7,4},{8,11},{9,10},{10,... | collective-permute-start | bytes 172040 | tf_op jit(solution)/shard_map/ppermute | solution.py:38
  57.1 1.4 %collective-permute-start.16 = (bf16[16,3584]{1,0:T(8,128)(2,1)S(1)}, bf16[16,3584]{1,0:T(8,128)(2,1)S(1)}, u32[]{:S(2)}, u32[]{:S(2)}) collective-permute-start(bf16[16,3584]{1,0:T(8,128)(2,1)S(1)} %pad_maximum_fusion.1.refs_0_), channel_id=1, source_target_pairs={{0,1},{1,0},{2,3},{3,2},{4,5},{5,4},{6,7},{7,6},{8,9},{9,8},{10,11... | collective-permute-start | bytes 344072 | tf_op jit(solution)/shard_map/ppermute | solution.py:38

commit v5 on v3

v5 whole, which is shorter than its diff:
```python
import functools
import math

import jax
import jax.numpy as jnp
from jax import lax
from jax.experimental import pallas as pl
from jax.experimental.pallas import tpu as pltpu
from jax.sharding import PartitionSpec as P

mscale_yarn = 1.0 + 0.1 * math.log(40.0)
masked_score = -1e30
LOG2E = 1.4426950408889634
LANES = 128
F32 = jnp.float32
BF16 = jnp.bfloat16


def stage_list(count):
    stages, stride = [], 1
    while stride < count:
        left = count // stride
        radix = 2 if (stride < 4 or left < 4) else 4
        stages.append((stride, radix))
        stride *= radix
    return stages


def swap(x, count, mask):
    return lax.ppermute(x, "ctx", [(i, i ^ mask) for i in range(count)])


def call(body, outs, operands, *, flops=0, smem=(), name=None, limit=40 << 20):
    specs = [
        pl.BlockSpec(memory_space=pltpu.SMEM if i in smem else pltpu.VMEM)
        for i in range(len(operands))
    ]
    total = sum(o.size * o.dtype.itemsize for o in list(outs) + list(operands))
    return pl.pallas_call(
        body,
        out_shape=tuple(outs),
        in_specs=specs,
        out_specs=tuple(pl.BlockSpec(memory_space=pltpu.VMEM) for _ in outs),
        compiler_params=pltpu.CompilerParams(vmem_limit_bytes=limit),
        cost_estimate=pl.CostEstimate(flops=flops, bytes_accessed=total, transcendentals=0),
        name=name,
    )(*operands)


def spec(shape, dtype):
    return jax.ShapeDtypeStruct(shape, dtype)


def table_body(keys, table_ref):
    table_ref[...] = (
        lax.axis_index("ctx") * keys
        + lax.broadcasted_iota(jnp.int32, table_ref.shape, 1)
        - lax.broadcasted_iota(jnp.int32, table_ref.shape, 0)
    )


def query_body(heads, reqs, x_ref, gain_ref, nope_ref, rope_ref, key_ref, table_ref, out_ref):
    rows = x_ref.shape[0]
    stretch = rows // reqs
    nope_width, latent = key_ref.shape[1], key_ref.shape[2]
    rope_width = rope_ref.shape[1] // heads
    x = x_ref[...].astype(F32)
    mean = jnp.mean(x * x, axis=-1, keepdims=True)
    normed = (x * lax.rsqrt(mean + 1e-06) * gain_ref[...].astype(F32).reshape(1, -1)).astype(BF16)
    nope = jnp.dot(normed, nope_ref[...], preferred_element_type=F32).astype(BF16)
    rope = jnp.dot(normed, rope_ref[...], preferred_element_type=F32)
    lat = [
        jnp.dot(
            nope[:, h * nope_width : (h + 1) * nope_width], key_ref[h], preferred_element_type=F32
        )
        for h in range(heads)
    ]
    for b in range(reqs):
        part = slice(b * stretch, (b + 1) * stretch)
        rows_b = jnp.concatenate([lat[h][part] for h in range(heads)], axis=0)
        at = b * (latent + LANES)
        out_ref[:, at : at + latent] = rows_b.astype(BF16)
        rows_b = jnp.concatenate(
            [rope[part, h * rope_width : (h + 1) * rope_width] for h in range(heads)],
            axis=0,
        )
        rows_b = jnp.concatenate(
            [rows_b, jnp.zeros((heads * stretch, LANES - rope_width), F32)], axis=1
        )
        out_ref[:, at + latent : at + latent + LANES] = rows_b.astype(BF16)


def pack_stats(column):
    rows = column.shape[0]
    lane = lax.broadcasted_iota(jnp.int32, (rows, LANES), 1)
    high = column.astype(BF16).astype(F32)
    rest = column - high
    mid = rest.astype(BF16).astype(F32)
    out = jnp.zeros((rows, LANES), F32)
    for k, term in enumerate((high, mid, rest - mid)):
        out = jnp.where(lane == k, term, out)
    return out


def merge(parts):
    latent = parts[0].shape[1] - LANES
    lse = [
        (p[:, latent : latent + 1] + p[:, latent + 1 : latent + 2]) + p[:, latent + 2 : latent + 3]
        for p in parts
    ]
    top = functools.reduce(jnp.maximum, lse)
    weight = [jnp.exp(m - top) for m in lse]
    total = functools.reduce(jnp.add, weight)
    inverse = 1.0 / total
    pooled = functools.reduce(
        jnp.add, [p[:, :latent] * (w * inverse) for p, w in zip(parts, weight)]
    )
    return pooled, top + jnp.log(total)


def attend_body(b, latent, rope_width, stretch, scale, chunk, *refs):
    length_ref, table_ref, near_ref, far_ref = refs[:4]
    lat_ref, key_ref, keep_ref, send_ref, q_s, r_s, s_s, w_s = refs[4:]
    half = near_ref.shape[0]
    rows = 2 * half
    keys = lat_ref.shape[1]
    for at, q in ((0, near_ref), (half, far_ref)):
        q_s[at : at + half, :] = q[:, :latent]
        r_s[at : at + half, :] = q[:, latent : latent + rope_width]
    block = min(rows, 256)
    step = min(block, half)
    seen = length_ref[b]
    for r0 in range(0, rows, block):
        lhs = q_s[r0 : r0 + block, :]
        lhs_rope = r_s[r0 : r0 + block, :]
        peak = None
        for k0 in range(0, keys, chunk):
            s = lax.dot_general(
                lhs,
                lat_ref[b, k0 : k0 + chunk, :],
                (((1,), (1,)), ((), ())),
                preferred_element_type=F32,
            ) + jnp.dot(lhs_rope, key_ref[b, :, k0 : k0 + chunk], preferred_element_type=F32)
            visible = table_ref[...] + k0 <= seen
            s = jnp.where(
                visible[None], s.reshape(block // stretch, stretch, chunk), masked_score
            ).reshape(block, chunk)
            s_s[:, k0 : k0 + chunk] = s
            top = jnp.max(s, axis=1, keepdims=True)
            peak = top if peak is None else jnp.maximum(peak, top)
        total = None
        for k0 in range(0, keys, chunk):
            w = jnp.exp2((s_s[:, k0 : k0 + chunk] - peak) * (scale * LOG2E))
            part = jnp.sum(w, axis=1, keepdims=True)
            total = part if total is None else total + part
            w_s[:, k0 : k0 + chunk] = w.astype(BF16)
        pool = jnp.dot(w_s[...], lat_ref[b], preferred_element_type=F32) * (1.0 / total)
        packed = pack_stats(peak * scale + jnp.log(total))
        for lo in range(r0, r0 + block, step):
            part = slice(lo - r0, lo - r0 + step)
            if lo < half:
                keep_ref[lo : lo + step, :latent] = pool[part]
                keep_ref[lo : lo + step, latent:] = packed[part]
            else:
                send_ref[lo - half : lo - half + step, :latent] = pool[part].astype(BF16)
                send_ref[lo - half : lo - half + step, latent:] = packed[part].astype(BF16)


def read_groups(groups, width, refs):
    return [
        [refs[i][:, slot * width : (slot + 1) * width].astype(F32) for i, slot in group]
        for group in groups
    ]


def merge_body(n_in, groups, width, *refs):
    outs = refs[n_in:]
    size = outs[0].shape[0]
    for g, parts in enumerate(read_groups(groups, width, refs)):
        pooled, top = merge(parts)
        packed = pack_stats(top)
        at = g * width
        for j, out in enumerate(outs):
            rows = slice(j * size, (j + 1) * size)
            out[:, at : at + width - LANES] = pooled[rows].astype(out.dtype)
            out[:, at + width - LANES : at + width] = packed[rows].astype(out.dtype)


def project_body(n_in, groups, width, heads, parts_out, *refs):
    value_ref, weight_ref = refs[n_in], refs[n_in + 1]
    keep_ref, send_ref = refs[n_in + 2], refs[n_in + 3]
    pooled = [merge(parts)[0] for parts in read_groups(groups, width, refs)]
    stretch = pooled[0].shape[0] // heads
    values = []
    for h in range(heads):
        rows = jnp.concatenate([p[h * stretch : (h + 1) * stretch] for p in pooled], axis=0)
        values.append(
            jnp.dot(rows.astype(BF16), value_ref[h], preferred_element_type=F32).astype(BF16)
        )
    hidden = jnp.concatenate(values, axis=1)
    mine = lax.rem(lax.axis_index("ctx"), parts_out)
    columns = weight_ref.shape[1] // parts_out
    for e in range(parts_out):
        start = pl.multiple_of(jnp.bitwise_xor(mine, e) * columns, LANES)
        out = jnp.dot(hidden, weight_ref[:, pl.ds(start, columns)], preferred_element_type=F32)
        slot = slice((e // 2) * columns, (e // 2 + 1) * columns)
        if e % 2 == 0:
            keep_ref[:, slot] = out
        else:
            send_ref[:, slot] = out.astype(BF16)


def join_body(n_in, lanes, *refs):
    at = 0
    for r in refs[:n_in]:
        for out, cols in zip(refs[n_in:], lanes):
            out[at : at + r.shape[0], :] = r[:, cols]
        at += r.shape[0]


def place_body(parts_out, *refs):
    pieces, out_ref, sems = refs[:-2], refs[-2], refs[-1]
    copies = []
    mine = lax.rem(lax.axis_index("ctx"), parts_out)
    width = out_ref.shape[1] // parts_out
    e_order = (0, 2, 1, 3)
    at = 0
    for piece in pieces:
        for k in range(piece.shape[1] // width):
            start = pl.multiple_of(jnp.bitwise_xor(mine, e_order[at]) * width, LANES)
            copies.append(
                pltpu.make_async_copy(
                    piece.at[:, pl.ds(k * width, width)],
                    out_ref.at[:, pl.ds(start, width)],
                    sems.at[at],
                )
            )
            copies[-1].start()
            at += 1
    for copy in copies:
        copy.wait()


def local(count, query_input, query_gain, nope_weight, rope_weight, key_up, value_up, out_weight,
          cache_latent, cache_rope, cached_length):
    heads, nope_width, latent = key_up.shape
    reqs = cache_latent.shape[0]
    rope_width = cache_rope.shape[1]
    rows = query_input.shape[0]
    stretch = rows // reqs
    own = heads * stretch
    each = latent + LANES
    width = reqs * each
    stages = stage_list(count)
    scale = mscale_yarn * mscale_yarn / math.sqrt(nope_width + rope_width)

    chunk = 256
    (table,) = call(
        functools.partial(table_body, cache_latent.shape[1]),
        [spec((stretch, chunk), jnp.int32)],
        [],
        flops=2 << 30,
        limit=16 << 20,
        name="table",
    )
    (query,) = call(
        functools.partial(query_body, heads, reqs),
        [spec((own, width), BF16)],
        [query_input, query_gain, nope_weight, rope_weight, key_up, table],
        limit=16 << 20,
        name="query",
    )
    spans = [slice(b * each, (b + 1) * each) for b in range(reqs)]
    gathered = [query]
    for at, (stride, radix) in enumerate(reversed(stages[2:])):
        (held,) = gathered
        got = [swap(held, count, j * stride) for j in range(1, radix)]
        lanes = spans if at == len(stages) - 3 else [slice(0, width)]
        gathered = call(
            functools.partial(join_body, radix, lanes),
            [spec((radix * held.shape[0], c.stop - c.start), BF16) for c in lanes],
            [held] + got,
            flops=4 << 30,
            limit=16 << 20,
            name="join",
        )
    near, far = [], []
    for held in gathered:
        near.append(jnp.concatenate([held, swap(held, count, stages[1][0])], axis=0))
        far.append(swap(near[-1], count, stages[0][0]))

    half = near[0].shape[0]
    total = 2 * half
    block = min(total, 256)
    keys = cache_latent.shape[1]
    keeps, gots = [], []
    for b in range(reqs):
        operands = [cached_length, table, near[b], far[b], cache_latent, cache_rope]
        keep, send = pl.pallas_call(
            functools.partial(attend_body, b, latent, rope_width, stretch, scale, chunk),
            out_shape=(spec((half, each), F32), spec((half, each), BF16)),
            in_specs=[pl.BlockSpec(memory_space=pltpu.SMEM)]
            + [pl.BlockSpec(memory_space=pltpu.VMEM)] * (len(operands) - 1),
            out_specs=(pl.BlockSpec(memory_space=pltpu.VMEM),) * 2,
            scratch_shapes=[
                pltpu.VMEM((total, latent), BF16),
                pltpu.VMEM((total, rope_width), BF16),
                pltpu.VMEM((block, keys), F32),
                pltpu.VMEM((block, keys), BF16),
            ],
            compiler_params=pltpu.CompilerParams(vmem_limit_bytes=32 << 20),
            cost_estimate=pl.CostEstimate(
                flops=4 * total * keys * latent, bytes_accessed=4 << 20, transcendentals=0
            ),
            name="attend",
        )(*operands)
        keeps.append(keep)
        gots.append(swap(send, count, stages[0][0]))

    stride, radix = stages[1]
    size = half // radix
    for b in range(reqs):
        keeps[b], send = call(
            functools.partial(merge_body, 2, [[(0, 0), (1, 0)]], each),
            [spec((size, each), F32), spec((size, each), BF16)],
            [keeps[b], gots[b]],
            limit=16 << 20,
            name="merge",
        )
        gots[b] = swap(send, count, stride)
    operands = [x for b in range(reqs) for x in (keeps[b], gots[b])]
    groups = [[(2 * b, 0), (2 * b + 1, 0)] for b in range(reqs)]
    for stride, radix in stages[2:]:
        size //= radix
        pieces = call(
            functools.partial(merge_body, len(operands), groups, each),
            [spec((size, reqs * each), F32)] + [spec((size, reqs * each), BF16)] * (radix - 1),
            operands,
            limit=16 << 20,
            name="merge",
        )
        got = [swap(pieces[j], count, j * stride) for j in reversed(range(1, radix))]
        operands = [pieces[0]] + got
        groups = [[(i, b) for i in range(radix)] for b in range(reqs)]

    parts_out = 4
    model = out_weight.shape[1]
    quarter = model // parts_out
    keep, send = call(
        functools.partial(project_body, len(operands), groups, each, heads, parts_out),
        [spec((rows, 2 * quarter), F32), spec((rows, 2 * quarter), BF16)],
        operands + [value_up, out_weight],
        name="project",
    )
    kept = keep + swap(send, count, stages[0][0]).astype(F32)
    kept = kept[:, :quarter] + swap(kept[:, quarter:].astype(BF16), count, stages[1][0]).astype(F32)
    for stride, radix in stages[2:]:
        mine = kept.astype(BF16)
        terms = [mine.astype(F32)] + [
            swap(mine, count, j * stride).astype(F32) for j in range(1, radix)
        ]
        while len(terms) > 1:
            terms = [terms[i] + terms[i + 1] for i in range(0, len(terms), 2)]
        kept = terms[0]
    done = kept.astype(BF16)
    both = jnp.concatenate([done, swap(done, count, stages[1][0])], axis=1)
    other = swap(both, count, stages[0][0])
    return pl.pallas_call(
        functools.partial(place_body, parts_out),
        out_shape=spec((rows, model), BF16),
        in_specs=[pl.BlockSpec(memory_space=pltpu.VMEM)] * 2,
        out_specs=pl.BlockSpec(memory_space=pl.ANY),
        scratch_shapes=[pltpu.SemaphoreType.DMA((parts_out,))],
        compiler_params=pltpu.CompilerParams(vmem_limit_bytes=16 << 20),
        name="place",
    )(both, other)


def solution(mesh):
    placed = (
        P("groups", None),
        P(),
        P(None, "ctx"),
        P(None, "ctx"),
        P("ctx", None, None),
        P("ctx", None, None),
        P("ctx", None),
        P("groups", "ctx", None),
        P("groups", None, "ctx"),
        P("groups"),
    )
    return jax.shard_map(
        functools.partial(local, mesh.shape["ctx"]),
        mesh=mesh,
        in_specs=placed,
        out_specs=P("groups", None),
        check_vma=False,
    )
```

time: 59.1 us -> 59.6 us (level)
  waiting for transfers between devices: 29 us -> 28.1 us
  starting transfers between devices: 21.4 us -> 22.2 us
  Pallas kernels: 6.94 us -> 7.61 us
    ppermute x17 -> x21, waiting for transfers between devices: 29 us -> 28.1 us  [swap(): return lax.ppermute(x, 'ctx', [(i, i ^ mask) for i in range(count)])]
    ppermute x17 -> x21, starting transfers between devices: 21.4 us -> 22.2 us  [swap(): return lax.ppermute(x, 'ctx', [(i, i ^ mask) for i in range(count)])]
    pallas_call x1 -> x2, Pallas kernels: 4.2 us -> 4.68 us  [local(): pl.pallas_call(functools.partial(attend_body, b, latent, rope_width, stre...]
    pallas_call x6 -> x7, Pallas kernels: 2.02 us -> 2.22 us  [call(): pl.pallas_call(body, out_shape=tuple(outs), in_specs=specs, out_specs=tup...]
    unnamed x20 -> x22, local copies, waits for them, and re-layouts: 1.34 us -> 1.36 us
  transfers between devices with their start and end apart: 17 -> 21, of which waited for: 15 -> 14; matrix products, arithmetic and copies ran while one was open for 0% -> 0% of each run, Pallas kernels for 0% -> 9%
where the time goes in v5:
time: 59.6 us; the launch traced here: 59.5 us
  waiting for transfers between devices  28.1 us (47%)
  starting transfers between devices  22.2 us (37%)
  Pallas kernels  7.61 us (13%)
  local copies, waits for them, and re-layouts  1.4 us (2%)
    ppermute x21, waiting for transfers between devices, swap(): return lax.ppermute(x, 'ctx', [(i, i ^ mask) for i in range(count)])  28.1 us
    ppermute x21, starting transfers between devices, swap(): return lax.ppermute(x, 'ctx', [(i, i ^ mask) for i in range(count)])  22.2 us
    pallas_call x2, Pallas kernels, local(): pl.pallas_call(functools.partial(attend_body, b, latent, rope_width, stre...  4.68 us
    pallas_call x7, Pallas kernels, call(): pl.pallas_call(body, out_shape=tuple(outs), in_specs=specs, out_specs=tup...  2.22 us
    unnamed x22, local copies, waits for them, and re-layouts  1.36 us
  transfers between devices with their start and end apart: 21, of which 14 were waited for; matrix products, arithmetic and copies ran while one was open for 0% of the time, Pallas kernels for 9%

profile of v5, /device:TPU:0, one launch (start us, length us, event | category | flops | bytes accessed | tf_op | source)
XLA Modules:
  0.0 59.5 jit_solution(12733376836636272841)
XLA Ops:
  0.0 0.9 %copy-done.6 = bf16[2,128,512]{2,1,0:T(8,128)(2,1)S(1)} copy-done((bf16[2,128,512]{2,1,0:T(8,128)(2,1)S(1)}, bf16[2,128,512]{2,1,0:T(8,128)(2,1)}, u32[]{:S(2)}) %copy-start.6) | copy-done | bytes 262168
  1.0 0.1 copy-done.4
  1.1 0.3 copy-done.3
  1.3 0.5 query.1.refs_0_
  1.9 0.0 copy-start.9
  1.9 5.1 %collective-permute-start.2 = (bf16[16,1280]{1,0:T(8,128)(2,1)S(1)}, bf16[16,1280]{1,0:T(8,128)(2,1)S(1)}, u32[]{:S(2)}, u32[]{:S(2)}) collective-permute-start(bf16[16,1280]{1,0:T(8,128)(2,1)S(1)} %query.1.refs_0_), channel_id=1, source_target_pairs={{0,12},{1,13},{2,14},{3,15},{4,8},{5,9},{6,10},{7,11},{8,4},{9,5},... | collective-permute-start | bytes 122888 | tf_op jit(solution)/shard_map/ppermute | solution.py:30
  7.0 0.6 %collective-permute-start = (bf16[16,1280]{1,0:T(8,128)(2,1)S(1)}, bf16[16,1280]{1,0:T(8,128)(2,1)S(1)}, u32[]{:S(2)}, u32[]{:S(2)}) collective-permute-start(bf16[16,1280]{1,0:T(8,128)(2,1)S(1)} %query.1.refs_0_), channel_id=1, source_target_pairs={{0,4},{1,5},{2,6},{3,7},{4,0},{5,1},{6,2},{7,3},{8,12},{9,13},{10,... | collective-permute-start | bytes 122888 | tf_op jit(solution)/shard_map/ppermute | solution.py:30
  7.7 1.4 %collective-permute-done.2.refs_3_ = bf16[16,1280]{1,0:T(8,128)(2,1)S(1)} collective-permute-done((bf16[16,1280]{1,0:T(8,128)(2,1)S(1)}, bf16[16,1280]{1,0:T(8,128)(2,1)S(1)}, u32[]{:S(2)}, u32[]{:S(2)}) %collective-permute-start.2) | collective-permute-done | bytes 40992 | tf_op jit(solution)/shard_map/ppermute | solution.py:30
  9.0 2.9 %collective-permute-done.1.refs_2_ = bf16[16,1280]{1,0:T(8,128)(2,1)S(1)} collective-permute-done((bf16[16,1280]{1,0:T(8,128)(2,1)S(1)}, bf16[16,1280]{1,0:T(8,128)(2,1)S(1)}, u32[]{:S(2)}, u32[]{:S(2)}) %collective-permute-start.1) | collective-permute-done | bytes 40992 | tf_op jit(solution)/shard_map/ppermute | solution.py:30
  11.9 1.6 %collective-permute-start.3 = (bf16[64,640]{1,0:T(8,128)(2,1)S(1)}, bf16[64,640]{1,0:T(8,128)(2,1)S(1)}, u32[]{:S(2)}, u32[]{:S(2)}) collective-permute-start(bf16[64,640]{1,0:T(8,128)(2,1)S(1)} %get-tuple-element.21), channel_id=1, source_target_pairs={{0,2},{1,3},{2,0},{3,1},{4,6},{5,7},{6,4},{7,5},{8,10},{9,11},{10,... | collective-permute-start | bytes 245768 | tf_op jit(solution)/shard_map/ppermute | solution.py:30
  13.5 0.6 collective-permute-start.7
  14.1 3.9 %collective-permute-done.7 = bf16[64,640]{1,0:T(8,128)(2,1)S(1)} collective-permute-done((bf16[64,640]{1,0:T(8,128)(2,1)S(1)}, bf16[64,640]{1,0:T(8,128)(2,1)S(1)}, u32[]{:S(2)}, u32[]{:S(2)}) %collective-permute-start.7) | collective-permute-done | bytes 81952 | tf_op jit(solution)/shard_map/ppermute | solution.py:30
  18.1 0.1 collective-permute-start.8
  18.2 0.5 collective-permute-start.4
  18.7 0.8 %collective-permute-done.8.refs_3_ = bf16[128,640]{1,0:T(8,128)(2,1)S(1)} collective-permute-done((bf16[128,640]{1,0:T(8,128)(2,1)S(1)}, bf16[128,640]{1,0:T(8,128)(2,1)S(1)}, u32[]{:S(2)}, u32[]{:S(2)}) %collective-permute-start.8) | collective-permute-done | bytes 163872 | tf_op jit(solution)/shard_map/ppermute | solution.py:30
  19.5 2.3 %attend.3 = (f32[128,640]{1,0:T(8,128)S(1)}, bf16[128,640]{1,0:T(8,128)(2,1)S(1)}) custom-call(s32[2]{0:T(128)S(1)} %copy-done.9, s32[8,256]{1,0:T(8,128)S(1)} %table.1.table_ref.refs_1_, bf16[128,640]{1,0:T(8,128)(2,1)S(1)} %constant_dynamic-update-slice_fusion.2.refs_2_, bf16[128,640]{1,0:T(8,128)(2,1)S(1)} %collective-permute-done.8.refs_3_, ...), custom_call_target="tpu_custom_call" | custom-call | flops 1073741824 | bytes 4194304 | tf_op jit(solution)/shard_map/attend/pallas_call | solution.py:299
  21.9 0.0 copy-start.1
  21.9 0.0 copy-start.5
  21.9 0.2 collective-permute-start.9
  22.1 2.3 %attend.2 = (f32[128,640]{1,0:T(8,128)S(1)}, bf16[128,640]{1,0:T(8,128)(2,1)S(1)}) custom-call(s32[2]{0:T(128)S(1)} %copy-done.9, s32[8,256]{1,0:T(8,128)S(1)} %table.1.table_ref.refs_1_, bf16[128,640]{1,0:T(8,128)(2,1)S(1)} %constant_dynamic-update-slice_fusion.refs_2_, bf16[128,640]{1,0:T(8,128)(2,1)S(1)} %collective-permute-done.4.refs_3_, ...), custom_call_target="tpu_custom_call" | custom-call | flops 1073741824 | bytes 4194304 | tf_op jit(solution)/shard_map/attend/pallas_call | solution.py:299
  24.5 0.4 collective-permute-start.5
  24.9 0.3 merge.4
  25.2 0.9 %collective-permute-start.10 = (bf16[64,640]{1,0:T(8,128)(2,1)S(1)}, bf16[64,640]{1,0:T(8,128)(2,1)S(1)}, u32[]{:S(2)}, u32[]{:S(2)}) collective-permute-start(bf16[64,640]{1,0:T(8,128)(2,1)S(1)} %get-tuple-element.30), channel_id=1, source_target_pairs={{0,2},{1,3},{2,0},{3,1},{4,6},{5,7},{6,4},{7,5},{8,10},{9,11},{10,... | collective-permute-start | bytes 245768 | tf_op jit(solution)/shard_map/ppermute | solution.py:30
  26.1 0.3 merge.3
  26.3 1.3 %collective-permute-start.6 = (bf16[64,640]{1,0:T(8,128)(2,1)S(1)}, bf16[64,640]{1,0:T(8,128)(2,1)S(1)}, u32[]{:S(2)}, u32[]{:S(2)}) collective-permute-start(bf16[64,640]{1,0:T(8,128)(2,1)S(1)} %get-tuple-element.25), channel_id=1, source_target_pairs={{0,2},{1,3},{2,0},{3,1},{4,6},{5,7},{6,4},{7,5},{8,10},{9,11},{10,... | collective-permute-start | bytes 245768 | tf_op jit(solution)/shard_map/ppermute | solution.py:30
  27.6 2.7 %collective-permute-done.10.refs_3_ = bf16[64,640]{1,0:T(8,128)(2,1)S(1)} collective-permute-done((bf16[64,640]{1,0:T(8,128)(2,1)S(1)}, bf16[64,640]{1,0:T(8,128)(2,1)S(1)}, u32[]{:S(2)}, u32[]{:S(2)}) %collective-permute-start.10) | collective-permute-done | bytes 81952 | tf_op jit(solution)/shard_map/ppermute | solution.py:30
  30.3 1.2 %collective-permute-done.6.refs_1_ = bf16[64,640]{1,0:T(8,128)(2,1)S(1)} collective-permute-done((bf16[64,640]{1,0:T(8,128)(2,1)S(1)}, bf16[64,640]{1,0:T(8,128)(2,1)S(1)}, u32[]{:S(2)}, u32[]{:S(2)}) %collective-permute-start.6) | collective-permute-done | bytes 81952 | tf_op jit(solution)/shard_map/ppermute | solution.py:30
  31.5 0.2 merge.5
  31.7 1.7 %collective-permute-start.11 = (bf16[16,1280]{1,0:T(8,128)(2,1)S(1)}, bf16[16,1280]{1,0:T(8,128)(2,1)S(1)}, u32[]{:S(2)}, u32[]{:S(2)}) collective-permute-start(bf16[16,1280]{1,0:T(8,128)(2,1)S(1)} %get-tuple-element.32), channel_id=1, source_target_pairs={{0,12},{1,13},{2,14},{3,15},{4,8},{5,9},{6,10},{7,11},{8,4},{9,5},... | collective-permute-start | bytes 122888 | tf_op jit(solution)/shard_map/ppermute | solution.py:30
  33.4 0.5 collective-permute-start.12
  33.9 2.3 %collective-permute-start.13 = (bf16[16,1280]{1,0:T(8,128)(2,1)S(1)}, bf16[16,1280]{1,0:T(8,128)(2,1)S(1)}, u32[]{:S(2)}, u32[]{:S(2)}) collective-permute-start(bf16[16,1280]{1,0:T(8,128)(2,1)S(1)} %get-tuple-element.34), channel_id=1, source_target_pairs={{0,4},{1,5},{2,6},{3,7},{4,0},{5,1},{6,2},{7,3},{8,12},{9,13},{10,... | collective-permute-start | bytes 122888 | tf_op jit(solution)/shard_map/ppermute | solution.py:30
  36.2 1.7 %collective-permute-done.11.refs_1_ = bf16[16,1280]{1,0:T(8,128)(2,1)S(1)} collective-permute-done((bf16[16,1280]{1,0:T(8,128)(2,1)S(1)}, bf16[16,1280]{1,0:T(8,128)(2,1)S(1)}, u32[]{:S(2)}, u32[]{:S(2)}) %collective-permute-start.11) | collective-permute-done | bytes 40992 | tf_op jit(solution)/shard_map/ppermute | solution.py:30
  37.9 0.9 %collective-permute-done.12.refs_2_ = bf16[16,1280]{1,0:T(8,128)(2,1)S(1)} collective-permute-done((bf16[16,1280]{1,0:T(8,128)(2,1)S(1)}, bf16[16,1280]{1,0:T(8,128)(2,1)S(1)}, u32[]{:S(2)}, u32[]{:S(2)}) %collective-permute-start.12) | collective-permute-done | bytes 40992 | tf_op jit(solution)/shard_map/ppermute | solution.py:30
  38.8 0.9 %project.1 = (f32[16,3584]{1,0:T(8,128)S(1)}, bf16[16,3584]{1,0:T(8,128)(2,1)S(1)}) custom-call(f32[16,1280]{1,0:T(8,128)S(1)} %get-tuple-element.31.refs_0_, bf16[16,1280]{1,0:T(8,128)(2,1)S(1)} %collective-permute-done.11.refs_1_, bf16[16,1280]{1,0:T(8,128)(2,1)S(1)} %collective-permute-done.12.refs_2_, ...), custom_call_target="tpu_custom_call" | custom-call | bytes 4481024 | tf_op jit(solution)/shard_map/project/pallas_call | solution.py:39
  39.6 0.0 collective-permute-start.14
  39.7 1.3 %collective-permute-done.14 = bf16[16,3584]{1,0:T(8,128)(2,1)S(1)} collective-permute-done((bf16[16,3584]{1,0:T(8,128)(2,1)S(1)}, bf16[16,3584]{1,0:T(8,128)(2,1)S(1)}, u32[]{:S(2)}, u32[]{:S(2)}) %collective-permute-start.14) | collective-permute-done | bytes 114720 | tf_op jit(solution)/shard_map/ppermute | solution.py:30
  41.0 0.9 %collective-permute-start.15 = (bf16[16,1792]{1,0:T(8,128)(2,1)S(1)}, bf16[16,1792]{1,0:T(8,128)(2,1)S(1)}, u32[]{:S(2)}, u32[]{:S(2)}) collective-permute-start(bf16[16,1792]{1,0:T(8,128)(2,1)S(1)} %slice.15), channel_id=1, source_target_pairs={{0,2},{1,3},{2,0},{3,1},{4,6},{5,7},{6,4},{7,5},{8,10},{9,11},{10,... | collective-permute-start | bytes 172040 | tf_op jit(solution)/shard_map/ppermute | solution.py:30
  41.9 3.3 %collective-permute-done.15 = bf16[16,1792]{1,0:T(8,128)(2,1)S(1)} collective-permute-done((bf16[16,1792]{1,0:T(8,128)(2,1)S(1)}, bf16[16,1792]{1,0:T(8,128)(2,1)S(1)}, u32[]{:S(2)}, u32[]{:S(2)}) %collective-permute-start.15) | collective-permute-done | bytes 57376 | tf_op jit(solution)/shard_map/ppermute | solution.py:30
  45.3 2.3 %collective-permute-start.18 = (bf16[16,1792]{1,0:T(8,128)(2,1)S(1)}, bf16[16,1792]{1,0:T(8,128)(2,1)S(1)}, u32[]{:S(2)}, u32[]{:S(2)}) collective-permute-start(bf16[16,1792]{1,0:T(8,128)(2,1)S(1)} %fusion), channel_id=1, source_target_pairs={{0,12},{1,13},{2,14},{3,15},{4,8},{5,9},{6,10},{7,11},{8,4},{9,5},... | collective-permute-start | bytes 172040 | tf_op jit(solution)/shard_map/ppermute | solution.py:30
  47.6 0.7 %collective-permute-start.17 = (bf16[16,1792]{1,0:T(8,128)(2,1)S(1)}, bf16[16,1792]{1,0:T(8,128)(2,1)S(1)}, u32[]{:S(2)}, u32[]{:S(2)}) collective-permute-start(bf16[16,1792]{1,0:T(8,128)(2,1)S(1)} %fusion), channel_id=1, source_target_pairs={{0,8},{1,9},{2,10},{3,11},{4,12},{5,13},{6,14},{7,15},{8,0},{9,1},... | collective-permute-start | bytes 172040 | tf_op jit(solution)/shard_map/ppermute | solution.py:30
  48.3 1.5 %collective-permute-start.16 = (bf16[16,1792]{1,0:T(8,128)(2,1)S(1)}, bf16[16,1792]{1,0:T(8,128)(2,1)S(1)}, u32[]{:S(2)}, u32[]{:S(2)}) collective-permute-start(bf16[16,1792]{1,0:T(8,128)(2,1)S(1)} %fusion), channel_id=1, source_target_pairs={{0,4},{1,5},{2,6},{3,7},{4,0},{5,1},{6,2},{7,3},{8,12},{9,13},{10,... | collective-permute-start | bytes 172040 | tf_op jit(solution)/shard_map/ppermute | solution.py:30
  49.8 2.0 %collective-permute-done.18 = bf16[16,1792]{1,0:T(8,128)(2,1)S(1)} collective-permute-done((bf16[16,1792]{1,0:T(8,128)(2,1)S(1)}, bf16[16,1792]{1,0:T(8,128)(2,1)S(1)}, u32[]{:S(2)}, u32[]{:S(2)}) %collective-permute-start.18) | collective-permute-done | bytes 57376 | tf_op jit(solution)/shard_map/ppermute | solution.py:30
  51.7 1.4 %collective-permute-done.17 = bf16[16,1792]{1,0:T(8,128)(2,1)S(1)} collective-permute-done((bf16[16,1792]{1,0:T(8,128)(2,1)S(1)}, bf16[16,1792]{1,0:T(8,128)(2,1)S(1)}, u32[]{:S(2)}, u32[]{:S(2)}) %collective-permute-start.17) | collective-permute-done | bytes 57376 | tf_op jit(solution)/shard_map/ppermute | solution.py:30
  53.1 0.9 %collective-permute-start.19 = (bf16[16,1792]{1,0:T(8,128)(2,1)S(1)}, bf16[16,1792]{1,0:T(8,128)(2,1)S(1)}, u32[]{:S(2)}, u32[]{:S(2)}) collective-permute-start(bf16[16,1792]{1,0:T(8,128)(2,1)S(1)} %add_convert_fusion), channel_id=1, source_target_pairs={{0,2},{1,3},{2,0},{3,1},{4,6},{5,7},{6,4},{7,5},{8,10},{9,11},{10,... | collective-permute-start | bytes 172040 | tf_op jit(solution)/shard_map/ppermute | solution.py:30
  54.0 3.3 %collective-permute-done.19 = bf16[16,1792]{1,0:T(8,128)(2,1)S(1)} collective-permute-done((bf16[16,1792]{1,0:T(8,128)(2,1)S(1)}, bf16[16,1792]{1,0:T(8,128)(2,1)S(1)}, u32[]{:S(2)}, u32[]{:S(2)}) %collective-permute-start.19) | collective-permute-done | bytes 57376 | tf_op jit(solution)/shard_map/ppermute | solution.py:30
  57.4 0.1 collective-permute-start.20
  57.5 1.3 %collective-permute-done.20.refs_1_ = bf16[16,3584]{1,0:T(8,128)(2,1)S(1)} collective-permute-done((bf16[16,3584]{1,0:T(8,128)(2,1)S(1)}, bf16[16,3584]{1,0:T(8,128)(2,1)S(1)}, u32[]{:S(2)}, u32[]{:S(2)}) %collective-permute-start.20) | collective-permute-done | bytes 114720 | tf_op jit(solution)/shard_map/ppermute | solution.py:30
  58.8 0.7 %place.1 = bf16[16,7168]{1,0:T(8,128)(2,1)} custom-call(bf16[16,3584]{1,0:T(8,128)(2,1)S(1)} %pad_maximum_fusion.refs_0_, bf16[16,3584]{1,0:T(8,128)(2,1)S(1)} %collective-permute-done.20.refs_1_), custom_call_target="tpu_custom_call" | custom-call | tf_op jit(solution)/shard_map/place/pallas_call | solution.py:368
  (33 shorter events, 0.2 us)
Async XLA Ops:
  0.0 0.9 %copy-start.6 = (bf16[2,128,512]{2,1,0:T(8,128)(2,1)S(1)}, bf16[2,128,512]{2,1,0:T(8,128)(2,1)}, u32[]{:S(2)}) copy-start(bf16[2,128,512]{2,1,0:T(8,128)(2,1)} %key_ref.1) | copy-start | bytes 786436
  0.0 1.1 %copy-start.4 = (bf16[1536,128]{1,0:T(8,128)(2,1)S(1)}, bf16[1536,128]{1,0:T(8,128)(2,1)}, u32[]{:S(2)}) copy-start(bf16[1536,128]{1,0:T(8,128)(2,1)} %rope_ref.1) | copy-start | bytes 1179652
  0.0 1.3 %copy-start.3 = (bf16[1536,256]{1,0:T(8,128)(2,1)S(1)}, bf16[1536,256]{1,0:T(8,128)(2,1)}, u32[]{:S(2)}) copy-start(bf16[1536,256]{1,0:T(8,128)(2,1)} %nope_ref.1) | copy-start | bytes 2359300
  0.0 1.3 %copy-start.8 = (bf16[1536]{0:T(1024)(128)(2,1)S(1)}, bf16[1536]{0:T(1024)(128)(2,1)}, u32[]{:S(2)}) copy-start(bf16[1536]{0:T(1024)(128)(2,1)} %gain_ref.1) | copy-start | bytes 9220
  0.0 1.3 %copy-start.7 = (bf16[16,1536]{1,0:T(8,128)(2,1)S(1)}, bf16[16,1536]{1,0:T(8,128)(2,1)}, u32[]{:S(2)}) copy-start(bf16[16,1536]{1,0:T(8,128)(2,1)} %x_ref.1) | copy-start | bytes 147460
  1.9 17.6 %copy-start = (bf16[2,2048,512]{2,1,0:T(8,128)(2,1)S(1)}, bf16[2,2048,512]{2,1,0:T(8,128)(2,1)}, u32[]{:S(2)}) copy-start(bf16[2,2048,512]{2,1,0:T(8,128)(2,1)} %refs_4_.4) | copy-start | bytes 12582916
  1.9 17.6 %copy-start.2 = (bf16[2,64,2048]{2,1,0:T(8,128)(2,1)S(1)}, bf16[2,64,2048]{2,1,0:T(8,128)(2,1)}, u32[]{:S(2)}) copy-start(bf16[2,64,2048]{2,1,0:T(8,128)(2,1)} %refs_5_.4) | copy-start | bytes 1572868
  1.9 17.6 %copy-start.9 = (s32[2]{0:T(128)S(1)}, s32[2]{0:T(128)}, u32[]{:S(2)}) copy-start(s32[2]{0:T(128)} %refs_0_.3) | copy-start | bytes 28
  1.9 7.1 %collective-permute-start.2 = (bf16[16,1280]{1,0:T(8,128)(2,1)S(1)}, bf16[16,1280]{1,0:T(8,128)(2,1)S(1)}, u32[]{:S(2)}, u32[]{:S(2)}) collective-permute-start(bf16[16,1280]{1,0:T(8,128)(2,1)S(1)} %query.1.refs_0_), channel_id=1, source_target_pairs={{0,12},{1,13},{2,14},{3,15},{4,8},{5,9},{6,10},{7,11},{8,4},{9,5},... | collective-permute-start | bytes 122888 | tf_op jit(solution)/shard_map/ppermute | solution.py:30
  7.0 4.9 %collective-permute-start.1 = (bf16[16,1280]{1,0:T(8,128)(2,1)S(1)}, bf16[16,1280]{1,0:T(8,128)(2,1)S(1)}, u32[]{:S(2)}, u32[]{:S(2)}) collective-permute-start(bf16[16,1280]{1,0:T(8,128)(2,1)S(1)} %query.1.refs_0_), channel_id=1, source_target_pairs={{0,8},{1,9},{2,10},{3,11},{4,12},{5,13},{6,14},{7,15},{8,0},{9,1},... | collective-permute-start | bytes 122888 | tf_op jit(solution)/shard_map/ppermute | solution.py:30
  7.0 4.9 %collective-permute-start = (bf16[16,1280]{1,0:T(8,128)(2,1)S(1)}, bf16[16,1280]{1,0:T(8,128)(2,1)S(1)}, u32[]{:S(2)}, u32[]{:S(2)}) collective-permute-start(bf16[16,1280]{1,0:T(8,128)(2,1)S(1)} %query.1.refs_0_), channel_id=1, source_target_pairs={{0,4},{1,5},{2,6},{3,7},{4,0},{5,1},{6,2},{7,3},{8,12},{9,13},{10,... | collective-permute-start | bytes 122888 | tf_op jit(solution)/shard_map/ppermute | solution.py:30
  11.9 6.2 %collective-permute-start.3 = (bf16[64,640]{1,0:T(8,128)(2,1)S(1)}, bf16[64,640]{1,0:T(8,128)(2,1)S(1)}, u32[]{:S(2)}, u32[]{:S(2)}) collective-permute-start(bf16[64,640]{1,0:T(8,128)(2,1)S(1)} %get-tuple-element.21), channel_id=1, source_target_pairs={{0,2},{1,3},{2,0},{3,1},{4,6},{5,7},{6,4},{7,5},{8,10},{9,11},{10,... | collective-permute-start | bytes 245768 | tf_op jit(solution)/shard_map/ppermute | solution.py:30
  13.5 4.5 %collective-permute-start.7 = (bf16[64,640]{1,0:T(8,128)(2,1)S(1)}, bf16[64,640]{1,0:T(8,128)(2,1)S(1)}, u32[]{:S(2)}, u32[]{:S(2)}) collective-permute-start(bf16[64,640]{1,0:T(8,128)(2,1)S(1)} %get-tuple-element.26), channel_id=1, source_target_pairs={{0,2},{1,3},{2,0},{3,1},{4,6},{5,7},{6,4},{7,5},{8,10},{9,11},{10,... | collective-permute-start | bytes 245768 | tf_op jit(solution)/shard_map/ppermute | solution.py:30
  18.1 1.5 %collective-permute-start.8 = (bf16[128,640]{1,0:T(8,128)(2,1)S(1)}, bf16[128,640]{1,0:T(8,128)(2,1)S(1)}, u32[]{:S(2)}, u32[]{:S(2)}) collective-permute-start(bf16[128,640]{1,0:T(8,128)(2,1)S(1)} %constant_dynamic-update-slice_fusion.2.refs_2_), channel_id=1, source_target_pairs={{0,1},{1,0},{2,3},{3,2},{4,5},{5,4},{6,7},{7,6},{8,9},{9,8},{10,11... | collective-permute-start | bytes 491528 | tf_op jit(solution)/shard_map/ppermute | solution.py:30
  18.2 3.9 %collective-permute-start.4 = (bf16[128,640]{1,0:T(8,128)(2,1)S(1)}, bf16[128,640]{1,0:T(8,128)(2,1)S(1)}, u32[]{:S(2)}, u32[]{:S(2)}) collective-permute-start(bf16[128,640]{1,0:T(8,128)(2,1)S(1)} %constant_dynamic-update-slice_fusion.refs_2_), channel_id=1, source_target_pairs={{0,1},{1,0},{2,3},{3,2},{4,5},{5,4},{6,7},{7,6},{8,9},{9,8},{10,11... | collective-permute-start | bytes 491528 | tf_op jit(solution)/shard_map/ppermute | solution.py:30
  21.9 16.9 %copy-start.1 = (bf16[256,7168]{1,0:T(8,128)(2,1)S(1)}, bf16[256,7168]{1,0:T(8,128)(2,1)}, u32[]{:S(2)}) copy-start(bf16[256,7168]{1,0:T(8,128)(2,1)} %refs_5_.5) | copy-start | bytes 11010052
  21.9 16.9 %copy-start.5 = (bf16[2,512,128]{2,1,0:T(8,128)(2,1)S(1)}, bf16[2,512,128]{2,1,0:T(8,128)(2,1)}, u32[]{:S(2)}) copy-start(bf16[2,512,128]{2,1,0:T(8,128)(2,1)} %refs_4_.5) | copy-start | bytes 786436
  21.9 3.0 %collective-permute-start.9 = (bf16[128,640]{1,0:T(8,128)(2,1)S(1)}, bf16[128,640]{1,0:T(8,128)(2,1)S(1)}, u32[]{:S(2)}, u32[]{:S(2)}) collective-permute-start(bf16[128,640]{1,0:T(8,128)(2,1)S(1)} %get-tuple-element.28), channel_id=1, source_target_pairs={{0,1},{1,0},{2,3},{3,2},{4,5},{5,4},{6,7},{7,6},{8,9},{9,8},{10,11... | collective-permute-start | bytes 491528 | tf_op jit(solution)/shard_map/ppermute | solution.py:30
  24.5 1.6 %collective-permute-start.5 = (bf16[128,640]{1,0:T(8,128)(2,1)S(1)}, bf16[128,640]{1,0:T(8,128)(2,1)S(1)}, u32[]{:S(2)}, u32[]{:S(2)}) collective-permute-start(bf16[128,640]{1,0:T(8,128)(2,1)S(1)} %get-tuple-element.23), channel_id=1, source_target_pairs={{0,1},{1,0},{2,3},{3,2},{4,5},{5,4},{6,7},{7,6},{8,9},{9,8},{10,11... | collective-permute-start | bytes 491528 | tf_op jit(solution)/shard_map/ppermute | solution.py:30
  25.2 5.1 %collective-permute-start.10 = (bf16[64,640]{1,0:T(8,128)(2,1)S(1)}, bf16[64,640]{1,0:T(8,128)(2,1)S(1)}, u32[]{:S(2)}, u32[]{:S(2)}) collective-permute-start(bf16[64,640]{1,0:T(8,128)(2,1)S(1)} %get-tuple-element.30), channel_id=1, source_target_pairs={{0,2},{1,3},{2,0},{3,1},{4,6},{5,7},{6,4},{7,5},{8,10},{9,11},{10,... | collective-permute-start | bytes 245768 | tf_op jit(solution)/shard_map/ppermute | solution.py:30
  26.3 5.2 %collective-permute-start.6 = (bf16[64,640]{1,0:T(8,128)(2,1)S(1)}, bf16[64,640]{1,0:T(8,128)(2,1)S(1)}, u32[]{:S(2)}, u32[]{:S(2)}) collective-permute-start(bf16[64,640]{1,0:T(8,128)(2,1)S(1)} %get-tuple-element.25), channel_id=1, source_target_pairs={{0,2},{1,3},{2,0},{3,1},{4,6},{5,7},{6,4},{7,5},{8,10},{9,11},{10,... | collective-permute-start | bytes 245768 | tf_op jit(solution)/shard_map/ppermute | solution.py:30
  31.7 6.2 %collective-permute-start.11 = (bf16[16,1280]{1,0:T(8,128)(2,1)S(1)}, bf16[16,1280]{1,0:T(8,128)(2,1)S(1)}, u32[]{:S(2)}, u32[]{:S(2)}) collective-permute-start(bf16[16,1280]{1,0:T(8,128)(2,1)S(1)} %get-tuple-element.32), channel_id=1, source_target_pairs={{0,12},{1,13},{2,14},{3,15},{4,8},{5,9},{6,10},{7,11},{8,4},{9,5},... | collective-permute-start | bytes 122888 | tf_op jit(solution)/shard_map/ppermute | solution.py:30
  33.4 5.4 %collective-permute-start.12 = (bf16[16,1280]{1,0:T(8,128)(2,1)S(1)}, bf16[16,1280]{1,0:T(8,128)(2,1)S(1)}, u32[]{:S(2)}, u32[]{:S(2)}) collective-permute-start(bf16[16,1280]{1,0:T(8,128)(2,1)S(1)} %get-tuple-element.33), channel_id=1, source_target_pairs={{0,8},{1,9},{2,10},{3,11},{4,12},{5,13},{6,14},{7,15},{8,0},{9,1},... | collective-permute-start | bytes 122888 | tf_op jit(solution)/shard_map/ppermute | solution.py:30
  33.9 4.8 %collective-permute-start.13 = (bf16[16,1280]{1,0:T(8,128)(2,1)S(1)}, bf16[16,1280]{1,0:T(8,128)(2,1)S(1)}, u32[]{:S(2)}, u32[]{:S(2)}) collective-permute-start(bf16[16,1280]{1,0:T(8,128)(2,1)S(1)} %get-tuple-element.34), channel_id=1, source_target_pairs={{0,4},{1,5},{2,6},{3,7},{4,0},{5,1},{6,2},{7,3},{8,12},{9,13},{10,... | collective-permute-start | bytes 122888 | tf_op jit(solution)/shard_map/ppermute | solution.py:30
  39.6 1.4 %collective-permute-start.14 = (bf16[16,3584]{1,0:T(8,128)(2,1)S(1)}, bf16[16,3584]{1,0:T(8,128)(2,1)S(1)}, u32[]{:S(2)}, u32[]{:S(2)}) collective-permute-start(bf16[16,3584]{1,0:T(8,128)(2,1)S(1)} %get-tuple-element.36), channel_id=1, source_target_pairs={{0,1},{1,0},{2,3},{3,2},{4,5},{5,4},{6,7},{7,6},{8,9},{9,8},{10,11... | collective-permute-start | bytes 344072 | tf_op jit(solution)/shard_map/ppermute | solution.py:30
  41.0 4.2 %collective-permute-start.15 = (bf16[16,1792]{1,0:T(8,128)(2,1)S(1)}, bf16[16,1792]{1,0:T(8,128)(2,1)S(1)}, u32[]{:S(2)}, u32[]{:S(2)}) collective-permute-start(bf16[16,1792]{1,0:T(8,128)(2,1)S(1)} %slice.15), channel_id=1, source_target_pairs={{0,2},{1,3},{2,0},{3,1},{4,6},{5,7},{6,4},{7,5},{8,10},{9,11},{10,... | collective-permute-start | bytes 172040 | tf_op jit(solution)/shard_map/ppermute | solution.py:30
  45.3 6.4 %collective-permute-start.18 = (bf16[16,1792]{1,0:T(8,128)(2,1)S(1)}, bf16[16,1792]{1,0:T(8,128)(2,1)S(1)}, u32[]{:S(2)}, u32[]{:S(2)}) collective-permute-start(bf16[16,1792]{1,0:T(8,128)(2,1)S(1)} %fusion), channel_id=1, source_target_pairs={{0,12},{1,13},{2,14},{3,15},{4,8},{5,9},{6,10},{7,11},{8,4},{9,5},... | collective-permute-start | bytes 172040 | tf_op jit(solution)/shard_map/ppermute | solution.py:30
  47.6 5.5 %collective-permute-start.17 = (bf16[16,1792]{1,0:T(8,128)(2,1)S(1)}, bf16[16,1792]{1,0:T(8,128)(2,1)S(1)}, u32[]{:S(2)}, u32[]{:S(2)}) collective-permute-start(bf16[16,1792]{1,0:T(8,128)(2,1)S(1)} %fusion), channel_id=1, source_target_pairs={{0,8},{1,9},{2,10},{3,11},{4,12},{5,13},{6,14},{7,15},{8,0},{9,1},... | collective-permute-start | bytes 172040 | tf_op jit(solution)/shard_map/ppermute | solution.py:30
  48.3 4.8 %collective-permute-start.16 = (bf16[16,1792]{1,0:T(8,128)(2,1)S(1)}, bf16[16,1792]{1,0:T(8,128)(2,1)S(1)}, u32[]{:S(2)}, u32[]{:S(2)}) collective-permute-start(bf16[16,1792]{1,0:T(8,128)(2,1)S(1)} %fusion), channel_id=1, source_target_pairs={{0,4},{1,5},{2,6},{3,7},{4,0},{5,1},{6,2},{7,3},{8,12},{9,13},{10,... | collective-permute-start | bytes 172040 | tf_op jit(solution)/shard_map/ppermute | solution.py:30
  53.1 4.2 %collective-permute-start.19 = (bf16[16,1792]{1,0:T(8,128)(2,1)S(1)}, bf16[16,1792]{1,0:T(8,128)(2,1)S(1)}, u32[]{:S(2)}, u32[]{:S(2)}) collective-permute-start(bf16[16,1792]{1,0:T(8,128)(2,1)S(1)} %add_convert_fusion), channel_id=1, source_target_pairs={{0,2},{1,3},{2,0},{3,1},{4,6},{5,7},{6,4},{7,5},{8,10},{9,11},{10,... | collective-permute-start | bytes 172040 | tf_op jit(solution)/shard_map/ppermute | solution.py:30
  57.4 1.4 %collective-permute-start.20 = (bf16[16,3584]{1,0:T(8,128)(2,1)S(1)}, bf16[16,3584]{1,0:T(8,128)(2,1)S(1)}, u32[]{:S(2)}, u32[]{:S(2)}) collective-permute-start(bf16[16,3584]{1,0:T(8,128)(2,1)S(1)} %pad_maximum_fusion.refs_0_), channel_id=1, source_target_pairs={{0,1},{1,0},{2,3},{3,2},{4,5},{5,4},{6,7},{7,6},{8,9},{9,8},{10,11... | collective-permute-start | bytes 344072 | tf_op jit(solution)/shard_map/ppermute | solution.py:30

commit v6 on v4

--- a/solution.py
+++ b/solution.py
@@ -24,14 +24,6 @@
         stages.append((stride, radix))
         stride *= radix
     return stages
-
-
-def hop(j, stride):
-    return j * stride + (1 if j > 1 else 0)
-
-
-def beside_rel(e):
-    return (e & 1) ^ (3 if e & 2 else 0)
 
 
 def swap(x, count, mask):
@@ -206,20 +198,19 @@
 
 
 def merge_body(n_in, reqs, latent, *refs):
-    parts = [r[...].astype(F32) for r in refs[:n_in]]
     outs = refs[n_in:]
-    pooled, tops = merge(parts, reqs, latent)
-    packed = pack_stats(tops)
     size = outs[0].shape[0]
-    for j, out in enumerate(outs):
+    for j, out in enumerate(outs, 1):
         rows = slice(j * size, (j + 1) * size)
+        pooled, tops = merge([r[rows, :].astype(F32) for r in refs[:n_in]], reqs, latent)
         for b in range(reqs):
-            out[:, b * latent : (b + 1) * latent] = pooled[b][rows].astype(out.dtype)
-        out[:, reqs * latent :] = packed[rows].astype(out.dtype)
+            out[:, b * latent : (b + 1) * latent] = pooled[b].astype(out.dtype)
+        out[:, reqs * latent :] = pack_stats(tops).astype(out.dtype)
 
 
 def project_body(n_in, reqs, heads, latent, parts_out, *refs):
-    parts = [r[...].astype(F32) for r in refs[:n_in]]
+    own = heads * (refs[-1].shape[0] // reqs)
+    parts = [r[:own, :].astype(F32) for r in refs[:n_in]]
     value_ref, weight_ref = refs[n_in], refs[n_in + 1]
     keep_ref, send_ref = refs[n_in + 2], refs[n_in + 3]
     pooled, _ = merge(parts, reqs, latent)
@@ -234,7 +225,7 @@
     mine = lax.rem(lax.axis_index("ctx"), parts_out)
     width = weight_ref.shape[1] // parts_out
     for e in range(parts_out):
-        start = pl.multiple_of(jnp.bitwise_xor(mine, beside_rel(e)) * width, LANES)
+        start = pl.multiple_of(jnp.bitwise_xor(mine, e) * width, LANES)
         out = jnp.dot(hidden, weight_ref[:, pl.ds(start, width)], preferred_element_type=F32)
         slot = slice((e // 2) * width, (e // 2 + 1) * width)
         if e % 2 == 0:
@@ -259,7 +250,7 @@
     at = 0
     for piece in pieces:
         for k in range(piece.shape[1] // width):
-            start = pl.multiple_of(jnp.bitwise_xor(mine, beside_rel(e_order[at])) * width, LANES)
+            start = pl.multiple_of(jnp.bitwise_xor(mine, e_order[at]) * width, LANES)
             copies.append(
                 pltpu.make_async_copy(
                     piece.at[:, pl.ds(k * width, width)],
@@ -304,7 +295,7 @@
     join_flops = 4 << 30
     held = query
     for stride, radix in reversed(stages[2:]):
-        got = [swap(held, count, hop(j, stride)) for j in range(1, radix)]
+        got = [swap(held, count, j * stride) for j in range(1, radix)]
         parts = [held] + got
         (held,) = call(
             join_body,
@@ -342,29 +333,29 @@
         name="attend",
     )(*operands)
 
-    got = [swap(send, count, stages[0][0])]
+    parts = [keep, swap(send, count, stages[0][0])]
+    size = half
     for stride, radix in stages[1:]:
-        size = keep.shape[0] // radix
+        size //= radix
         pieces = call(
-            functools.partial(merge_body, 1 + len(got), reqs, latent),
-            [spec((size, width), F32)] + [spec((size, width), BF16)] * (radix - 1),
-            [keep] + got,
+            functools.partial(merge_body, len(parts), reqs, latent),
+            [spec((size, width), BF16)] * (radix - 1),
+            parts,
             name="merge",
         )
-        keep = pieces[0]
-        got = [swap(pieces[j], count, hop(j, stride)) for j in reversed(range(1, radix))]
+        parts += [swap(pieces[j - 1], count, j * stride) for j in reversed(range(1, radix))]
 
     parts_out = 4
     model = out_weight.shape[1]
     quarter = model // parts_out
     keep, send = call(
-        functools.partial(project_body, 1 + len(got), reqs, heads, latent, parts_out),
+        functools.partial(project_body, len(parts), reqs, heads, latent, parts_out),
         [spec((rows, 2 * quarter), F32), spec((rows, 2 * quarter), BF16)],
-        [keep] + got + [value_up, out_weight],
+        parts + [value_up, out_weight],
         name="project",
     )
     kept = keep + swap(send, count, stages[0][0]).astype(F32)
-    kept = kept[:, :quarter] + swap(kept[:, quarter:].astype(BF16), count, beside_rel(2)).astype(F32)
+    kept = kept[:, :quarter] + swap(kept[:, quarter:].astype(BF16), count, stages[1][0]).astype(F32)
     for stride, radix in stages[2:]:
         mine = kept.astype(BF16)
         terms = [mine.astype(F32)] + [
@@ -374,7 +365,7 @@
             terms = [terms[i] + terms[i + 1] for i in range(0, len(terms), 2)]
         kept = terms[0]
     done = kept.astype(BF16)
-    both = jnp.concatenate([done, swap(done, count, beside_rel(2))], axis=1)
+    both = jnp.concatenate([done, swap(done, count, stages[1][0])], axis=1)
     other = swap(both, count, stages[0][0])
     return pl.pallas_call(
         functools.partial(place_body, parts_out),

time: 59.3 us -> 58.6 us (0.988)
  waiting for transfers between devices: 31.4 us -> 29 us
  starting transfers between devices: 19.6 us -> 21.4 us
    ppermute x17, waiting for transfers between devices: 31.4 us -> 29 us  [swap(): return lax.ppermute(x, 'ctx', [(i, i ^ mask) for i in range(count)])]
    ppermute x17, starting transfers between devices: 19.6 us -> 21.4 us  [swap(): return lax.ppermute(x, 'ctx', [(i, i ^ mask) for i in range(count)])]
where the time goes in v6:
time: 58.6 us; the launch traced here: 58.5 us
  waiting for transfers between devices  29 us (49%)
  starting transfers between devices  21.4 us (37%)
  Pallas kernels  6.51 us (11%)
  local copies, waits for them, and re-layouts  1.35 us (2%)
    ppermute x17, waiting for transfers between devices, swap(): return lax.ppermute(x, 'ctx', [(i, i ^ mask) for i in range(count)])  29 us
    ppermute x17, starting transfers between devices, swap(): return lax.ppermute(x, 'ctx', [(i, i ^ mask) for i in range(count)])  21.4 us
    pallas_call x1, Pallas kernels, local(): pl.pallas_call(functools.partial(attend_body, 2, reqs, latent, rope_width...  3.87 us
    pallas_call x6, Pallas kernels, call(): pl.pallas_call(body, out_shape=tuple(outs), in_specs=specs, out_specs=tup...  1.93 us
    unnamed x20, local copies, waits for them, and re-layouts  1.34 us
  transfers between devices with their start and end apart: 17, of which 15 were waited for; matrix products, arithmetic and copies ran while one was open for 0% of the time, Pallas kernels for 0%

profile of v6, /device:TPU:0, one launch (start us, length us, event | category | flops | bytes accessed | tf_op | source)
XLA Modules:
  0.0 58.5 jit_solution(2355197565405515845)
XLA Ops:
  0.0 0.9 %copy-done.4 = bf16[2,128,512]{2,1,0:T(8,128)(2,1)S(1)} copy-done((bf16[2,128,512]{2,1,0:T(8,128)(2,1)S(1)}, bf16[2,128,512]{2,1,0:T(8,128)(2,1)}, u32[]{:S(2)}) %copy-start.4) | copy-done | bytes 262168
  1.0 0.1 copy-done.2
  1.1 0.3 copy-done.1
  1.3 0.0 copy-done.6
  1.3 0.0 copy-done.5
  1.3 0.5 query.1.refs_0_
  1.9 0.0 copy-start.9
  1.9 5.1 %collective-permute-start.2 = (bf16[16,1152]{1,0:T(8,128)(2,1)S(1)}, bf16[16,1152]{1,0:T(8,128)(2,1)S(1)}, u32[]{:S(2)}, u32[]{:S(2)}) collective-permute-start(bf16[16,1152]{1,0:T(8,128)(2,1)S(1)} %query.1.refs_0_), channel_id=1, source_target_pairs={{0,12},{1,13},{2,14},{3,15},{4,8},{5,9},{6,10},{7,11},{8,4},{9,5},... | collective-permute-start | bytes 110600 | tf_op jit(solution)/shard_map/ppermute | solution.py:30
  7.0 0.0 collective-permute-start.1
  7.0 0.6 %collective-permute-start = (bf16[16,1152]{1,0:T(8,128)(2,1)S(1)}, bf16[16,1152]{1,0:T(8,128)(2,1)S(1)}, u32[]{:S(2)}, u32[]{:S(2)}) collective-permute-start(bf16[16,1152]{1,0:T(8,128)(2,1)S(1)} %query.1.refs_0_), channel_id=1, source_target_pairs={{0,4},{1,5},{2,6},{3,7},{4,0},{5,1},{6,2},{7,3},{8,12},{9,13},{10,... | collective-permute-start | bytes 110600 | tf_op jit(solution)/shard_map/ppermute | solution.py:30
  7.7 1.3 %collective-permute-done.2.refs_3_ = bf16[16,1152]{1,0:T(8,128)(2,1)S(1)} collective-permute-done((bf16[16,1152]{1,0:T(8,128)(2,1)S(1)}, bf16[16,1152]{1,0:T(8,128)(2,1)S(1)}, u32[]{:S(2)}, u32[]{:S(2)}) %collective-permute-start.2) | collective-permute-done | bytes 36896 | tf_op jit(solution)/shard_map/ppermute | solution.py:30
  9.0 2.9 %collective-permute-done.1.refs_2_ = bf16[16,1152]{1,0:T(8,128)(2,1)S(1)} collective-permute-done((bf16[16,1152]{1,0:T(8,128)(2,1)S(1)}, bf16[16,1152]{1,0:T(8,128)(2,1)S(1)}, u32[]{:S(2)}, u32[]{:S(2)}) %collective-permute-start.1) | collective-permute-done | bytes 36896 | tf_op jit(solution)/shard_map/ppermute | solution.py:30
  11.9 0.0 collective-permute-done.refs_1_
  11.9 1.6 %collective-permute-start.3 = (bf16[64,1152]{1,0:T(8,128)(2,1)S(1)}, bf16[64,1152]{1,0:T(8,128)(2,1)S(1)}, u32[]{:S(2)}, u32[]{:S(2)}) collective-permute-start(bf16[64,1152]{1,0:T(8,128)(2,1)S(1)} %join.1), channel_id=1, source_target_pairs={{0,2},{1,3},{2,0},{3,1},{4,6},{5,7},{6,4},{7,5},{8,10},{9,11},{10,... | collective-permute-start | bytes 442376 | tf_op jit(solution)/shard_map/ppermute | solution.py:30
  13.5 3.6 %collective-permute-done.3 = bf16[64,1152]{1,0:T(8,128)(2,1)S(1)} collective-permute-done((bf16[64,1152]{1,0:T(8,128)(2,1)S(1)}, bf16[64,1152]{1,0:T(8,128)(2,1)S(1)}, u32[]{:S(2)}, u32[]{:S(2)}) %collective-permute-start.3) | collective-permute-done | bytes 147488 | tf_op jit(solution)/shard_map/ppermute | solution.py:30
  17.1 0.0 copy-start
  17.1 0.0 copy-start.3
  17.2 0.1 collective-permute-start.4
  17.2 1.6 %collective-permute-done.4.refs_3_ = bf16[128,1152]{1,0:T(8,128)(2,1)S(1)} collective-permute-done((bf16[128,1152]{1,0:T(8,128)(2,1)S(1)}, bf16[128,1152]{1,0:T(8,128)(2,1)S(1)}, u32[]{:S(2)}, u32[]{:S(2)}) %collective-permute-start.4) | collective-permute-done | bytes 294944 | tf_op jit(solution)/shard_map/ppermute | solution.py:30
  18.8 3.9 %attend.1 = (f32[128,1152]{1,0:T(8,128)S(1)}, bf16[128,1152]{1,0:T(8,128)(2,1)S(1)}) custom-call(s32[2]{0:T(128)S(1)} %copy-done.9, s32[8,256]{1,0:T(8,128)S(1)} %table.1.table_ref.refs_1_, bf16[128,1152]{1,0:T(8,128)(2,1)S(1)} %pad_maximum_fusion.refs_2_, bf16[128,1152]{1,0:T(8,128)(2,1)S(1)} %collective-permute-done.4.refs_3_, ...), custom_call_target="tpu_custom_call" | custom-call | flops 2147483648 | bytes 8388608 | tf_op jit(solution)/shard_map/attend/pallas_call | solution.py:316
  22.7 0.2 collective-permute-start.5
  22.9 1.5 %collective-permute-done.5.refs_1_ = bf16[128,1152]{1,0:T(8,128)(2,1)S(1)} collective-permute-done((bf16[128,1152]{1,0:T(8,128)(2,1)S(1)}, bf16[128,1152]{1,0:T(8,128)(2,1)S(1)}, u32[]{:S(2)}, u32[]{:S(2)}) %collective-permute-start.5) | collective-permute-done | bytes 294944 | tf_op jit(solution)/shard_map/ppermute | solution.py:30
  24.3 0.2 merge.2
  24.6 1.6 %collective-permute-start.6 = (bf16[64,1152]{1,0:T(8,128)(2,1)S(1)}, bf16[64,1152]{1,0:T(8,128)(2,1)S(1)}, u32[]{:S(2)}, u32[]{:S(2)}) collective-permute-start(bf16[64,1152]{1,0:T(8,128)(2,1)S(1)} %merge.2), channel_id=1, source_target_pairs={{0,2},{1,3},{2,0},{3,1},{4,6},{5,7},{6,4},{7,5},{8,10},{9,11},{10,... | collective-permute-start | bytes 442376 | tf_op jit(solution)/shard_map/ppermute | solution.py:30
  26.2 4.4 %collective-permute-done.6.refs_2_ = bf16[64,1152]{1,0:T(8,128)(2,1)S(1)} collective-permute-done((bf16[64,1152]{1,0:T(8,128)(2,1)S(1)}, bf16[64,1152]{1,0:T(8,128)(2,1)S(1)}, u32[]{:S(2)}, u32[]{:S(2)}) %collective-permute-start.6) | collective-permute-done | bytes 147488 | tf_op jit(solution)/shard_map/ppermute | solution.py:30
  30.5 0.2 merge.3
  30.8 1.5 %collective-permute-start.7 = (bf16[16,1152]{1,0:T(8,128)(2,1)S(1)}, bf16[16,1152]{1,0:T(8,128)(2,1)S(1)}, u32[]{:S(2)}, u32[]{:S(2)}) collective-permute-start(bf16[16,1152]{1,0:T(8,128)(2,1)S(1)} %get-tuple-element.14), channel_id=1, source_target_pairs={{0,12},{1,13},{2,14},{3,15},{4,8},{5,9},{6,10},{7,11},{8,4},{9,5},... | collective-permute-start | bytes 110600 | tf_op jit(solution)/shard_map/ppermute | solution.py:30
  32.3 0.6 %collective-permute-start.8 = (bf16[16,1152]{1,0:T(8,128)(2,1)S(1)}, bf16[16,1152]{1,0:T(8,128)(2,1)S(1)}, u32[]{:S(2)}, u32[]{:S(2)}) collective-permute-start(bf16[16,1152]{1,0:T(8,128)(2,1)S(1)} %get-tuple-element.15), channel_id=1, source_target_pairs={{0,8},{1,9},{2,10},{3,11},{4,12},{5,13},{6,14},{7,15},{8,0},{9,1},... | collective-permute-start | bytes 110600 | tf_op jit(solution)/shard_map/ppermute | solution.py:30
  33.0 2.3 %collective-permute-start.9 = (bf16[16,1152]{1,0:T(8,128)(2,1)S(1)}, bf16[16,1152]{1,0:T(8,128)(2,1)S(1)}, u32[]{:S(2)}, u32[]{:S(2)}) collective-permute-start(bf16[16,1152]{1,0:T(8,128)(2,1)S(1)} %get-tuple-element.16), channel_id=1, source_target_pairs={{0,4},{1,5},{2,6},{3,7},{4,0},{5,1},{6,2},{7,3},{8,12},{9,13},{10,... | collective-permute-start | bytes 110600 | tf_op jit(solution)/shard_map/ppermute | solution.py:30
  35.2 1.6 %collective-permute-done.7.refs_3_ = bf16[16,1152]{1,0:T(8,128)(2,1)S(1)} collective-permute-done((bf16[16,1152]{1,0:T(8,128)(2,1)S(1)}, bf16[16,1152]{1,0:T(8,128)(2,1)S(1)}, u32[]{:S(2)}, u32[]{:S(2)}) %collective-permute-start.7) | collective-permute-done | bytes 36896 | tf_op jit(solution)/shard_map/ppermute | solution.py:30
  36.8 0.4 collective-permute-done.8.refs_4_
  37.3 0.4 collective-permute-done.9.refs_5_
  37.6 0.9 %project.1 = (f32[16,3584]{1,0:T(8,128)S(1)}, bf16[16,3584]{1,0:T(8,128)(2,1)S(1)}) custom-call(f32[128,1152]{1,0:T(8,128)S(1)} %get-tuple-element.12.refs_0_, bf16[128,1152]{1,0:T(8,128)(2,1)S(1)} %collective-permute-done.5.refs_1_, bf16[64,1152]{1,0:T(8,128)(2,1)S(1)} %collective-permute-done.6.refs_2_, ...), custom_call_target="tpu_custom_call" | custom-call | bytes 5419008 | tf_op jit(solution)/shard_map/project/pallas_call | solution.py:39
  38.5 0.0 collective-permute-start.10
  38.5 1.3 %collective-permute-done.10 = bf16[16,3584]{1,0:T(8,128)(2,1)S(1)} collective-permute-done((bf16[16,3584]{1,0:T(8,128)(2,1)S(1)}, bf16[16,3584]{1,0:T(8,128)(2,1)S(1)}, u32[]{:S(2)}, u32[]{:S(2)}) %collective-permute-start.10) | collective-permute-done | bytes 114720 | tf_op jit(solution)/shard_map/ppermute | solution.py:30
  39.9 1.6 %collective-permute-start.11 = (bf16[16,1792]{1,0:T(8,128)(2,1)S(1)}, bf16[16,1792]{1,0:T(8,128)(2,1)S(1)}, u32[]{:S(2)}, u32[]{:S(2)}) collective-permute-start(bf16[16,1792]{1,0:T(8,128)(2,1)S(1)} %slice.15), channel_id=1, source_target_pairs={{0,2},{1,3},{2,0},{3,1},{4,6},{5,7},{6,4},{7,5},{8,10},{9,11},{10,... | collective-permute-start | bytes 172040 | tf_op jit(solution)/shard_map/ppermute | solution.py:30
  41.5 2.7 %collective-permute-done.11 = bf16[16,1792]{1,0:T(8,128)(2,1)S(1)} collective-permute-done((bf16[16,1792]{1,0:T(8,128)(2,1)S(1)}, bf16[16,1792]{1,0:T(8,128)(2,1)S(1)}, u32[]{:S(2)}, u32[]{:S(2)}) %collective-permute-start.11) | collective-permute-done | bytes 57376 | tf_op jit(solution)/shard_map/ppermute | solution.py:30
  44.2 2.4 %collective-permute-start.14 = (bf16[16,1792]{1,0:T(8,128)(2,1)S(1)}, bf16[16,1792]{1,0:T(8,128)(2,1)S(1)}, u32[]{:S(2)}, u32[]{:S(2)}) collective-permute-start(bf16[16,1792]{1,0:T(8,128)(2,1)S(1)} %fusion), channel_id=1, source_target_pairs={{0,12},{1,13},{2,14},{3,15},{4,8},{5,9},{6,10},{7,11},{8,4},{9,5},... | collective-permute-start | bytes 172040 | tf_op jit(solution)/shard_map/ppermute | solution.py:30
  46.5 0.7 %collective-permute-start.13 = (bf16[16,1792]{1,0:T(8,128)(2,1)S(1)}, bf16[16,1792]{1,0:T(8,128)(2,1)S(1)}, u32[]{:S(2)}, u32[]{:S(2)}) collective-permute-start(bf16[16,1792]{1,0:T(8,128)(2,1)S(1)} %fusion), channel_id=1, source_target_pairs={{0,8},{1,9},{2,10},{3,11},{4,12},{5,13},{6,14},{7,15},{8,0},{9,1},... | collective-permute-start | bytes 172040 | tf_op jit(solution)/shard_map/ppermute | solution.py:30
  47.3 1.3 %collective-permute-start.12 = (bf16[16,1792]{1,0:T(8,128)(2,1)S(1)}, bf16[16,1792]{1,0:T(8,128)(2,1)S(1)}, u32[]{:S(2)}, u32[]{:S(2)}) collective-permute-start(bf16[16,1792]{1,0:T(8,128)(2,1)S(1)} %fusion), channel_id=1, source_target_pairs={{0,4},{1,5},{2,6},{3,7},{4,0},{5,1},{6,2},{7,3},{8,12},{9,13},{10,... | collective-permute-start | bytes 172040 | tf_op jit(solution)/shard_map/ppermute | solution.py:30
  48.6 1.9 %collective-permute-done.14 = bf16[16,1792]{1,0:T(8,128)(2,1)S(1)} collective-permute-done((bf16[16,1792]{1,0:T(8,128)(2,1)S(1)}, bf16[16,1792]{1,0:T(8,128)(2,1)S(1)}, u32[]{:S(2)}, u32[]{:S(2)}) %collective-permute-start.14) | collective-permute-done | bytes 57376 | tf_op jit(solution)/shard_map/ppermute | solution.py:30
  50.5 1.5 %collective-permute-done.13 = bf16[16,1792]{1,0:T(8,128)(2,1)S(1)} collective-permute-done((bf16[16,1792]{1,0:T(8,128)(2,1)S(1)}, bf16[16,1792]{1,0:T(8,128)(2,1)S(1)}, u32[]{:S(2)}, u32[]{:S(2)}) %collective-permute-start.13) | collective-permute-done | bytes 57376 | tf_op jit(solution)/shard_map/ppermute | solution.py:30
  52.1 0.0 collective-permute-done.12
  52.1 1.6 %collective-permute-start.15 = (bf16[16,1792]{1,0:T(8,128)(2,1)S(1)}, bf16[16,1792]{1,0:T(8,128)(2,1)S(1)}, u32[]{:S(2)}, u32[]{:S(2)}) collective-permute-start(bf16[16,1792]{1,0:T(8,128)(2,1)S(1)} %add_convert_fusion), channel_id=1, source_target_pairs={{0,2},{1,3},{2,0},{3,1},{4,6},{5,7},{6,4},{7,5},{8,10},{9,11},{10,... | collective-permute-start | bytes 172040 | tf_op jit(solution)/shard_map/ppermute | solution.py:30
  53.7 2.7 %collective-permute-done.15 = bf16[16,1792]{1,0:T(8,128)(2,1)S(1)} collective-permute-done((bf16[16,1792]{1,0:T(8,128)(2,1)S(1)}, bf16[16,1792]{1,0:T(8,128)(2,1)S(1)}, u32[]{:S(2)}, u32[]{:S(2)}) %collective-permute-start.15) | collective-permute-done | bytes 57376 | tf_op jit(solution)/shard_map/ppermute | solution.py:30
  56.4 0.1 collective-permute-start.16
  56.4 1.3 %collective-permute-done.16.refs_1_ = bf16[16,3584]{1,0:T(8,128)(2,1)S(1)} collective-permute-done((bf16[16,3584]{1,0:T(8,128)(2,1)S(1)}, bf16[16,3584]{1,0:T(8,128)(2,1)S(1)}, u32[]{:S(2)}, u32[]{:S(2)}) %collective-permute-start.16) | collective-permute-done | bytes 114720 | tf_op jit(solution)/shard_map/ppermute | solution.py:30
  57.8 0.7 %place.1 = bf16[16,7168]{1,0:T(8,128)(2,1)} custom-call(bf16[16,3584]{1,0:T(8,128)(2,1)S(1)} %pad_maximum_fusion.1.refs_0_, bf16[16,3584]{1,0:T(8,128)(2,1)S(1)} %collective-permute-done.16.refs_1_), custom_call_target="tpu_custom_call" | custom-call | tf_op jit(solution)/shard_map/place/pallas_call | solution.py:370
  (20 shorter events, 0.2 us)
Async XLA Ops:
  0.0 0.9 %copy-start.4 = (bf16[2,128,512]{2,1,0:T(8,128)(2,1)S(1)}, bf16[2,128,512]{2,1,0:T(8,128)(2,1)}, u32[]{:S(2)}) copy-start(bf16[2,128,512]{2,1,0:T(8,128)(2,1)} %key_ref.1) | copy-start | bytes 786436
  0.0 1.1 %copy-start.2 = (bf16[1536,128]{1,0:T(8,128)(2,1)S(1)}, bf16[1536,128]{1,0:T(8,128)(2,1)}, u32[]{:S(2)}) copy-start(bf16[1536,128]{1,0:T(8,128)(2,1)} %rope_ref.1) | copy-start | bytes 1179652
  0.0 1.3 %copy-start.1 = (bf16[1536,256]{1,0:T(8,128)(2,1)S(1)}, bf16[1536,256]{1,0:T(8,128)(2,1)}, u32[]{:S(2)}) copy-start(bf16[1536,256]{1,0:T(8,128)(2,1)} %nope_ref.1) | copy-start | bytes 2359300
  0.0 1.3 %copy-start.6 = (bf16[1536]{0:T(1024)(128)(2,1)S(1)}, bf16[1536]{0:T(1024)(128)(2,1)}, u32[]{:S(2)}) copy-start(bf16[1536]{0:T(1024)(128)(2,1)} %gain_ref.1) | copy-start | bytes 9220
  0.0 1.3 %copy-start.5 = (bf16[16,1536]{1,0:T(8,128)(2,1)S(1)}, bf16[16,1536]{1,0:T(8,128)(2,1)}, u32[]{:S(2)}) copy-start(bf16[16,1536]{1,0:T(8,128)(2,1)} %x_ref.1) | copy-start | bytes 147460
  1.9 16.9 %copy-start.7 = (bf16[2,2048,512]{2,1,0:T(8,128)(2,1)S(1)}, bf16[2,2048,512]{2,1,0:T(8,128)(2,1)}, u32[]{:S(2)}) copy-start(bf16[2,2048,512]{2,1,0:T(8,128)(2,1)} %refs_4_.1) | copy-start | bytes 12582916
  1.9 16.9 %copy-start.8 = (bf16[2,64,2048]{2,1,0:T(8,128)(2,1)S(1)}, bf16[2,64,2048]{2,1,0:T(8,128)(2,1)}, u32[]{:S(2)}) copy-start(bf16[2,64,2048]{2,1,0:T(8,128)(2,1)} %refs_5_.1) | copy-start | bytes 1572868
  1.9 16.9 %copy-start.9 = (s32[2]{0:T(128)S(1)}, s32[2]{0:T(128)}, u32[]{:S(2)}) copy-start(s32[2]{0:T(128)} %refs_0_.1) | copy-start | bytes 28
  1.9 7.1 %collective-permute-start.2 = (bf16[16,1152]{1,0:T(8,128)(2,1)S(1)}, bf16[16,1152]{1,0:T(8,128)(2,1)S(1)}, u32[]{:S(2)}, u32[]{:S(2)}) collective-permute-start(bf16[16,1152]{1,0:T(8,128)(2,1)S(1)} %query.1.refs_0_), channel_id=1, source_target_pairs={{0,12},{1,13},{2,14},{3,15},{4,8},{5,9},{6,10},{7,11},{8,4},{9,5},... | collective-permute-start | bytes 110600 | tf_op jit(solution)/shard_map/ppermute | solution.py:30
  7.0 4.9 %collective-permute-start.1 = (bf16[16,1152]{1,0:T(8,128)(2,1)S(1)}, bf16[16,1152]{1,0:T(8,128)(2,1)S(1)}, u32[]{:S(2)}, u32[]{:S(2)}) collective-permute-start(bf16[16,1152]{1,0:T(8,128)(2,1)S(1)} %query.1.refs_0_), channel_id=1, source_target_pairs={{0,8},{1,9},{2,10},{3,11},{4,12},{5,13},{6,14},{7,15},{8,0},{9,1},... | collective-permute-start | bytes 110600 | tf_op jit(solution)/shard_map/ppermute | solution.py:30
  7.0 4.9 %collective-permute-start = (bf16[16,1152]{1,0:T(8,128)(2,1)S(1)}, bf16[16,1152]{1,0:T(8,128)(2,1)S(1)}, u32[]{:S(2)}, u32[]{:S(2)}) collective-permute-start(bf16[16,1152]{1,0:T(8,128)(2,1)S(1)} %query.1.refs_0_), channel_id=1, source_target_pairs={{0,4},{1,5},{2,6},{3,7},{4,0},{5,1},{6,2},{7,3},{8,12},{9,13},{10,... | collective-permute-start | bytes 110600 | tf_op jit(solution)/shard_map/ppermute | solution.py:30
  11.9 5.2 %collective-permute-start.3 = (bf16[64,1152]{1,0:T(8,128)(2,1)S(1)}, bf16[64,1152]{1,0:T(8,128)(2,1)S(1)}, u32[]{:S(2)}, u32[]{:S(2)}) collective-permute-start(bf16[64,1152]{1,0:T(8,128)(2,1)S(1)} %join.1), channel_id=1, source_target_pairs={{0,2},{1,3},{2,0},{3,1},{4,6},{5,7},{6,4},{7,5},{8,10},{9,11},{10,... | collective-permute-start | bytes 442376 | tf_op jit(solution)/shard_map/ppermute | solution.py:30
  17.1 20.5 %copy-start = (bf16[256,7168]{1,0:T(8,128)(2,1)S(1)}, bf16[256,7168]{1,0:T(8,128)(2,1)}, u32[]{:S(2)}) copy-start(bf16[256,7168]{1,0:T(8,128)(2,1)} %refs_7_.1) | copy-start | bytes 11010052
  17.1 20.5 %copy-start.3 = (bf16[2,512,128]{2,1,0:T(8,128)(2,1)S(1)}, bf16[2,512,128]{2,1,0:T(8,128)(2,1)}, u32[]{:S(2)}) copy-start(bf16[2,512,128]{2,1,0:T(8,128)(2,1)} %refs_6_.1) | copy-start | bytes 786436
  17.2 1.6 %collective-permute-start.4 = (bf16[128,1152]{1,0:T(8,128)(2,1)S(1)}, bf16[128,1152]{1,0:T(8,128)(2,1)S(1)}, u32[]{:S(2)}, u32[]{:S(2)}) collective-permute-start(bf16[128,1152]{1,0:T(8,128)(2,1)S(1)} %pad_maximum_fusion.refs_2_), channel_id=1, source_target_pairs={{0,1},{1,0},{2,3},{3,2},{4,5},{5,4},{6,7},{7,6},{8,9},{9,8},{10,11... | collective-permute-start | bytes 884744 | tf_op jit(solution)/shard_map/ppermute | solution.py:30
  22.7 1.6 %collective-permute-start.5 = (bf16[128,1152]{1,0:T(8,128)(2,1)S(1)}, bf16[128,1152]{1,0:T(8,128)(2,1)S(1)}, u32[]{:S(2)}, u32[]{:S(2)}) collective-permute-start(bf16[128,1152]{1,0:T(8,128)(2,1)S(1)} %get-tuple-element.13), channel_id=1, source_target_pairs={{0,1},{1,0},{2,3},{3,2},{4,5},{5,4},{6,7},{7,6},{8,9},{9,8},{10,11... | collective-permute-start | bytes 884744 | tf_op jit(solution)/shard_map/ppermute | solution.py:30
  24.6 6.0 %collective-permute-start.6 = (bf16[64,1152]{1,0:T(8,128)(2,1)S(1)}, bf16[64,1152]{1,0:T(8,128)(2,1)S(1)}, u32[]{:S(2)}, u32[]{:S(2)}) collective-permute-start(bf16[64,1152]{1,0:T(8,128)(2,1)S(1)} %merge.2), channel_id=1, source_target_pairs={{0,2},{1,3},{2,0},{3,1},{4,6},{5,7},{6,4},{7,5},{8,10},{9,11},{10,... | collective-permute-start | bytes 442376 | tf_op jit(solution)/shard_map/ppermute | solution.py:30
  30.8 6.0 %collective-permute-start.7 = (bf16[16,1152]{1,0:T(8,128)(2,1)S(1)}, bf16[16,1152]{1,0:T(8,128)(2,1)S(1)}, u32[]{:S(2)}, u32[]{:S(2)}) collective-permute-start(bf16[16,1152]{1,0:T(8,128)(2,1)S(1)} %get-tuple-element.14), channel_id=1, source_target_pairs={{0,12},{1,13},{2,14},{3,15},{4,8},{5,9},{6,10},{7,11},{8,4},{9,5},... | collective-permute-start | bytes 110600 | tf_op jit(solution)/shard_map/ppermute | solution.py:30
  32.3 4.9 %collective-permute-start.8 = (bf16[16,1152]{1,0:T(8,128)(2,1)S(1)}, bf16[16,1152]{1,0:T(8,128)(2,1)S(1)}, u32[]{:S(2)}, u32[]{:S(2)}) collective-permute-start(bf16[16,1152]{1,0:T(8,128)(2,1)S(1)} %get-tuple-element.15), channel_id=1, source_target_pairs={{0,8},{1,9},{2,10},{3,11},{4,12},{5,13},{6,14},{7,15},{8,0},{9,1},... | collective-permute-start | bytes 110600 | tf_op jit(solution)/shard_map/ppermute | solution.py:30
  33.0 4.6 %collective-permute-start.9 = (bf16[16,1152]{1,0:T(8,128)(2,1)S(1)}, bf16[16,1152]{1,0:T(8,128)(2,1)S(1)}, u32[]{:S(2)}, u32[]{:S(2)}) collective-permute-start(bf16[16,1152]{1,0:T(8,128)(2,1)S(1)} %get-tuple-element.16), channel_id=1, source_target_pairs={{0,4},{1,5},{2,6},{3,7},{4,0},{5,1},{6,2},{7,3},{8,12},{9,13},{10,... | collective-permute-start | bytes 110600 | tf_op jit(solution)/shard_map/ppermute | solution.py:30
  38.5 1.4 %collective-permute-start.10 = (bf16[16,3584]{1,0:T(8,128)(2,1)S(1)}, bf16[16,3584]{1,0:T(8,128)(2,1)S(1)}, u32[]{:S(2)}, u32[]{:S(2)}) collective-permute-start(bf16[16,3584]{1,0:T(8,128)(2,1)S(1)} %get-tuple-element.18), channel_id=1, source_target_pairs={{0,1},{1,0},{2,3},{3,2},{4,5},{5,4},{6,7},{7,6},{8,9},{9,8},{10,11... | collective-permute-start | bytes 344072 | tf_op jit(solution)/shard_map/ppermute | solution.py:30
  39.9 4.2 %collective-permute-start.11 = (bf16[16,1792]{1,0:T(8,128)(2,1)S(1)}, bf16[16,1792]{1,0:T(8,128)(2,1)S(1)}, u32[]{:S(2)}, u32[]{:S(2)}) collective-permute-start(bf16[16,1792]{1,0:T(8,128)(2,1)S(1)} %slice.15), channel_id=1, source_target_pairs={{0,2},{1,3},{2,0},{3,1},{4,6},{5,7},{6,4},{7,5},{8,10},{9,11},{10,... | collective-permute-start | bytes 172040 | tf_op jit(solution)/shard_map/ppermute | solution.py:30
  44.2 6.4 %collective-permute-start.14 = (bf16[16,1792]{1,0:T(8,128)(2,1)S(1)}, bf16[16,1792]{1,0:T(8,128)(2,1)S(1)}, u32[]{:S(2)}, u32[]{:S(2)}) collective-permute-start(bf16[16,1792]{1,0:T(8,128)(2,1)S(1)} %fusion), channel_id=1, source_target_pairs={{0,12},{1,13},{2,14},{3,15},{4,8},{5,9},{6,10},{7,11},{8,4},{9,5},... | collective-permute-start | bytes 172040 | tf_op jit(solution)/shard_map/ppermute | solution.py:30
  46.5 5.5 %collective-permute-start.13 = (bf16[16,1792]{1,0:T(8,128)(2,1)S(1)}, bf16[16,1792]{1,0:T(8,128)(2,1)S(1)}, u32[]{:S(2)}, u32[]{:S(2)}) collective-permute-start(bf16[16,1792]{1,0:T(8,128)(2,1)S(1)} %fusion), channel_id=1, source_target_pairs={{0,8},{1,9},{2,10},{3,11},{4,12},{5,13},{6,14},{7,15},{8,0},{9,1},... | collective-permute-start | bytes 172040 | tf_op jit(solution)/shard_map/ppermute | solution.py:30
  47.3 4.8 %collective-permute-start.12 = (bf16[16,1792]{1,0:T(8,128)(2,1)S(1)}, bf16[16,1792]{1,0:T(8,128)(2,1)S(1)}, u32[]{:S(2)}, u32[]{:S(2)}) collective-permute-start(bf16[16,1792]{1,0:T(8,128)(2,1)S(1)} %fusion), channel_id=1, source_target_pairs={{0,4},{1,5},{2,6},{3,7},{4,0},{5,1},{6,2},{7,3},{8,12},{9,13},{10,... | collective-permute-start | bytes 172040 | tf_op jit(solution)/shard_map/ppermute | solution.py:30
  52.1 4.2 %collective-permute-start.15 = (bf16[16,1792]{1,0:T(8,128)(2,1)S(1)}, bf16[16,1792]{1,0:T(8,128)(2,1)S(1)}, u32[]{:S(2)}, u32[]{:S(2)}) collective-permute-start(bf16[16,1792]{1,0:T(8,128)(2,1)S(1)} %add_convert_fusion), channel_id=1, source_target_pairs={{0,2},{1,3},{2,0},{3,1},{4,6},{5,7},{6,4},{7,5},{8,10},{9,11},{10,... | collective-permute-start | bytes 172040 | tf_op jit(solution)/shard_map/ppermute | solution.py:30
  56.4 1.4 %collective-permute-start.16 = (bf16[16,3584]{1,0:T(8,128)(2,1)S(1)}, bf16[16,3584]{1,0:T(8,128)(2,1)S(1)}, u32[]{:S(2)}, u32[]{:S(2)}) collective-permute-start(bf16[16,3584]{1,0:T(8,128)(2,1)S(1)} %pad_maximum_fusion.1.refs_0_), channel_id=1, source_target_pairs={{0,1},{1,0},{2,3},{3,2},{4,5},{5,4},{6,7},{7,6},{8,9},{9,8},{10,11... | collective-permute-start | bytes 344072 | tf_op jit(solution)/shard_map/ppermute | solution.py:30

commit v7 on v6

--- a/solution.py
+++ b/solution.py
@@ -197,12 +197,26 @@
                 send_ref[lo - half : lo - half + size, reqs * latent :] = piece.astype(BF16)
 
 
-def merge_body(n_in, reqs, latent, *refs):
+def part_rows(ref, spread, place, own, lo, size):
+    if not spread:
+        return ref[lo : lo + size, :].astype(F32)
+    blocks = [
+        ref[(2 * k + place) * own : (2 * k + place + 1) * own, :]
+        for k in range(lo // own, (lo + size) // own)
+    ]
+    return jnp.concatenate([b.astype(F32) for b in blocks], axis=0)
+
+
+def merge_body(n_in, reqs, latent, own, beside, *refs):
     outs = refs[n_in:]
     size = outs[0].shape[0]
     for j, out in enumerate(outs, 1):
-        rows = slice(j * size, (j + 1) * size)
-        pooled, tops = merge([r[rows, :].astype(F32) for r in refs[:n_in]], reqs, latent)
+        lo = 0 if beside else j * size
+        parts = [
+            part_rows(r, i < 2, 1 if beside else 0, own, lo, size)
+            for i, r in enumerate(refs[:n_in])
+        ]
+        pooled, tops = merge(parts, reqs, latent)
         for b in range(reqs):
             out[:, b * latent : (b + 1) * latent] = pooled[b].astype(out.dtype)
         out[:, reqs * latent :] = pack_stats(tops).astype(out.dtype)
@@ -212,7 +226,7 @@
     own = heads * (refs[-1].shape[0] // reqs)
     parts = [r[:own, :].astype(F32) for r in refs[:n_in]]
     value_ref, weight_ref = refs[n_in], refs[n_in + 1]
-    keep_ref, send_ref = refs[n_in + 2], refs[n_in + 3]
+    hidden_ref, send_ref = refs[n_in + 2], refs[n_in + 3]
     pooled, _ = merge(parts, reqs, latent)
     stretch = pooled[0].shape[0] // heads
     values = []
@@ -222,16 +236,21 @@
             jnp.dot(rows.astype(BF16), value_ref[h], preferred_element_type=F32).astype(BF16)
         )
     hidden = jnp.concatenate(values, axis=1)
+    hidden_ref[...] = hidden
+    project_half(1, parts_out, hidden, weight_ref, send_ref)
+
+
+def project_half(odd, parts_out, hidden, weight_ref, out_ref):
     mine = lax.rem(lax.axis_index("ctx"), parts_out)
     width = weight_ref.shape[1] // parts_out
-    for e in range(parts_out):
+    for e in range(odd, parts_out, 2):
         start = pl.multiple_of(jnp.bitwise_xor(mine, e) * width, LANES)
         out = jnp.dot(hidden, weight_ref[:, pl.ds(start, width)], preferred_element_type=F32)
-        slot = slice((e // 2) * width, (e // 2 + 1) * width)
-        if e % 2 == 0:
-            keep_ref[:, slot] = out
-        else:
-            send_ref[:, slot] = out.astype(BF16)
+        out_ref[:, (e // 2) * width : (e // 2 + 1) * width] = out.astype(out_ref.dtype)
+
+
+def rest_body(parts_out, hidden_ref, weight_ref, keep_ref):
+    project_half(0, parts_out, hidden_ref[...], weight_ref, keep_ref)
 
 
 def join_body(*refs):
@@ -292,21 +311,18 @@
         limit=16 << 20,
         name="query",
     )
-    join_flops = 4 << 30
-    held = query
+    held = jnp.concatenate([query, swap(query, count, stages[1][0])], axis=0)
     for stride, radix in reversed(stages[2:]):
         got = [swap(held, count, j * stride) for j in range(1, radix)]
-        parts = [held] + got
         (held,) = call(
             join_body,
             [spec((radix * held.shape[0], width), BF16)],
-            parts,
-            flops=join_flops,
+            [held] + got,
+            flops=4 << 30,
             limit=16 << 20,
             name="join",
         )
-    beside = swap(held, count, stages[1][0])
-    near = jnp.concatenate([held, beside], axis=0)
+    near = held
     far = swap(near, count, stages[0][0])
 
     half = near.shape[0]
@@ -335,10 +351,10 @@
 
     parts = [keep, swap(send, count, stages[0][0])]
     size = half
-    for stride, radix in stages[1:]:
+    for at, (stride, radix) in enumerate(stages[1:]):
         size //= radix
         pieces = call(
-            functools.partial(merge_body, len(parts), reqs, latent),
+            functools.partial(merge_body, len(parts), reqs, latent, own, at == 0),
             [spec((size, width), BF16)] * (radix - 1),
             parts,
             name="merge",
@@ -348,13 +364,23 @@
     parts_out = 4
     model = out_weight.shape[1]
     quarter = model // parts_out
-    keep, send = call(
+    hidden, send = call(
         functools.partial(project_body, len(parts), reqs, heads, latent, parts_out),
-        [spec((rows, 2 * quarter), F32), spec((rows, 2 * quarter), BF16)],
+        [spec((rows, out_weight.shape[0]), BF16), spec((rows, 2 * quarter), BF16)],
         parts + [value_up, out_weight],
+        limit=24 << 20,
         name="project",
     )
-    kept = keep + swap(send, count, stages[0][0]).astype(F32)
+    received = swap(send, count, stages[0][0])
+    (keep,) = call(
+        functools.partial(rest_body, parts_out),
+        [spec((rows, 2 * quarter), F32)],
+        [hidden, out_weight],
+        flops=2 * rows * out_weight.size // 2,
+        limit=24 << 20,
+        name="rest",
+    )
+    kept = keep + received.astype(F32)
     kept = kept[:, :quarter] + swap(kept[:, quarter:].astype(BF16), count, stages[1][0]).astype(F32)
     for stride, radix in stages[2:]:
         mine = kept.astype(BF16)

time: 58.6 us -> 58.3 us (level)
  waiting for transfers between devices: 29 us -> 28.1 us
    ppermute x17, waiting for transfers between devices: 29 us -> 28.1 us  [swap(): return lax.ppermute(x, 'ctx', [(i, i ^ mask) for i in range(count)])]
    pallas_call x6 -> x7, Pallas kernels: 1.93 us -> 2.06 us  [call(): pl.pallas_call(body, out_shape=tuple(outs), in_specs=specs, out_specs=tup...]
  transfers between devices with their start and end apart: 17 -> 17, of which waited for: 15 -> 14; matrix products, arithmetic and copies ran while one was open for 0% -> 0% of each run, Pallas kernels for 0% -> 1%
where the time goes in v7:
time: 58.3 us; the launch traced here: 58.2 us
  waiting for transfers between devices  28.1 us (48%)
  starting transfers between devices  21.9 us (38%)
  Pallas kernels  6.64 us (11%)
  local copies, waits for them, and re-layouts  1.35 us (2%)
    ppermute x17, waiting for transfers between devices, swap(): return lax.ppermute(x, 'ctx', [(i, i ^ mask) for i in range(count)])  28.1 us
    ppermute x17, starting transfers between devices, swap(): return lax.ppermute(x, 'ctx', [(i, i ^ mask) for i in range(count)])  21.9 us
    pallas_call x1, Pallas kernels, local(): pl.pallas_call(functools.partial(attend_body, 2, reqs, latent, rope_width...  3.87 us
    pallas_call x7, Pallas kernels, call(): pl.pallas_call(body, out_shape=tuple(outs), in_specs=specs, out_specs=tup...  2.06 us
    unnamed x20, local copies, waits for them, and re-layouts  1.34 us
  transfers between devices with their start and end apart: 17, of which 14 were waited for; matrix products, arithmetic and copies ran while one was open for 0% of the time, Pallas kernels for 1%

profile of v7, /device:TPU:0, one launch (start us, length us, event | category | flops | bytes accessed | tf_op | source)
XLA Modules:
  0.0 58.2 jit_solution(570308029220523150)
XLA Ops:
  0.0 0.9 %copy-done.4 = bf16[2,128,512]{2,1,0:T(8,128)(2,1)S(1)} copy-done((bf16[2,128,512]{2,1,0:T(8,128)(2,1)S(1)}, bf16[2,128,512]{2,1,0:T(8,128)(2,1)}, u32[]{:S(2)}) %copy-start.4) | copy-done | bytes 262168
  1.0 0.1 copy-done.2
  1.1 0.3 copy-done.1
  1.3 0.5 query.1
  1.9 3.0 %collective-permute-start = (bf16[16,1152]{1,0:T(8,128)(2,1)S(1)}, bf16[16,1152]{1,0:T(8,128)(2,1)S(1)}, u32[]{:S(2)}, u32[]{:S(2)}) collective-permute-start(bf16[16,1152]{1,0:T(8,128)(2,1)S(1)} %query.1), channel_id=1, source_target_pairs={{0,2},{1,3},{2,0},{3,1},{4,6},{5,7},{6,4},{7,5},{8,10},{9,11},{10,... | collective-permute-start | bytes 110600 | tf_op jit(solution)/shard_map/ppermute | solution.py:30
  4.9 1.9 %collective-permute-done = bf16[16,1152]{1,0:T(8,128)(2,1)S(1)} collective-permute-done((bf16[16,1152]{1,0:T(8,128)(2,1)S(1)}, bf16[16,1152]{1,0:T(8,128)(2,1)S(1)}, u32[]{:S(2)}, u32[]{:S(2)}) %collective-permute-start) | collective-permute-done | bytes 36896 | tf_op jit(solution)/shard_map/ppermute | solution.py:30
  6.9 0.0 copy-start.8
  6.9 0.0 copy-start.9
  6.9 4.2 %collective-permute-start.3 = (bf16[32,1152]{1,0:T(8,128)(2,1)S(1)}, bf16[32,1152]{1,0:T(8,128)(2,1)S(1)}, u32[]{:S(2)}, u32[]{:S(2)}) collective-permute-start(bf16[32,1152]{1,0:T(8,128)(2,1)S(1)} %pad_maximum_fusion.1.refs_0_), channel_id=1, source_target_pairs={{0,12},{1,13},{2,14},{3,15},{4,8},{5,9},{6,10},{7,11},{8,4},{9,5},... | collective-permute-start | bytes 221192 | tf_op jit(solution)/shard_map/ppermute | solution.py:30
  11.0 0.0 collective-permute-start.2
  11.1 0.6 %collective-permute-start.1 = (bf16[32,1152]{1,0:T(8,128)(2,1)S(1)}, bf16[32,1152]{1,0:T(8,128)(2,1)S(1)}, u32[]{:S(2)}, u32[]{:S(2)}) collective-permute-start(bf16[32,1152]{1,0:T(8,128)(2,1)S(1)} %pad_maximum_fusion.1.refs_0_), channel_id=1, source_target_pairs={{0,4},{1,5},{2,6},{3,7},{4,0},{5,1},{6,2},{7,3},{8,12},{9,13},{10,... | collective-permute-start | bytes 221192 | tf_op jit(solution)/shard_map/ppermute | solution.py:30
  11.7 1.9 %collective-permute-done.3.refs_3_ = bf16[32,1152]{1,0:T(8,128)(2,1)S(1)} collective-permute-done((bf16[32,1152]{1,0:T(8,128)(2,1)S(1)}, bf16[32,1152]{1,0:T(8,128)(2,1)S(1)}, u32[]{:S(2)}, u32[]{:S(2)}) %collective-permute-start.3) | collective-permute-done | bytes 73760 | tf_op jit(solution)/shard_map/ppermute | solution.py:30
  13.6 3.0 %collective-permute-done.2.refs_2_ = bf16[32,1152]{1,0:T(8,128)(2,1)S(1)} collective-permute-done((bf16[32,1152]{1,0:T(8,128)(2,1)S(1)}, bf16[32,1152]{1,0:T(8,128)(2,1)S(1)}, u32[]{:S(2)}, u32[]{:S(2)}) %collective-permute-start.2) | collective-permute-done | bytes 73760 | tf_op jit(solution)/shard_map/ppermute | solution.py:30
  16.7 0.0 collective-permute-done.1.refs_1_
  16.7 0.0 copy-start
  16.7 0.0 copy-start.3
  16.7 0.1 collective-permute-start.4
  16.8 1.6 %collective-permute-done.4.refs_3_ = bf16[128,1152]{1,0:T(8,128)(2,1)S(1)} collective-permute-done((bf16[128,1152]{1,0:T(8,128)(2,1)S(1)}, bf16[128,1152]{1,0:T(8,128)(2,1)S(1)}, u32[]{:S(2)}, u32[]{:S(2)}) %collective-permute-start.4) | collective-permute-done | bytes 294944 | tf_op jit(solution)/shard_map/ppermute | solution.py:30
  18.4 3.9 %attend.1 = (f32[128,1152]{1,0:T(8,128)S(1)}, bf16[128,1152]{1,0:T(8,128)(2,1)S(1)}) custom-call(s32[2]{0:T(128)S(1)} %copy-done.9, s32[8,256]{1,0:T(8,128)S(1)} %table.1.table_ref.refs_1_, bf16[128,1152]{1,0:T(8,128)(2,1)S(1)} %join.1.refs_2_, bf16[128,1152]{1,0:T(8,128)(2,1)S(1)} %collective-permute-done.4.refs_3_, bf16[2,2048,512]{2,1,0:T(8,128)(2,1)S(1)} %copy-done.7, ...), custom_call_target="tpu_custom_call" | custom-call | flops 2147483648 | bytes 8388608 | tf_op jit(solution)/shard_map/attend/pallas_call | solution.py:332
  22.3 0.2 collective-permute-start.5
  22.5 1.5 %collective-permute-done.5.refs_1_ = bf16[128,1152]{1,0:T(8,128)(2,1)S(1)} collective-permute-done((bf16[128,1152]{1,0:T(8,128)(2,1)S(1)}, bf16[128,1152]{1,0:T(8,128)(2,1)S(1)}, u32[]{:S(2)}, u32[]{:S(2)}) %collective-permute-start.5) | collective-permute-done | bytes 294944 | tf_op jit(solution)/shard_map/ppermute | solution.py:30
  23.9 0.2 merge.2
  24.2 1.6 %collective-permute-start.6 = (bf16[64,1152]{1,0:T(8,128)(2,1)S(1)}, bf16[64,1152]{1,0:T(8,128)(2,1)S(1)}, u32[]{:S(2)}, u32[]{:S(2)}) collective-permute-start(bf16[64,1152]{1,0:T(8,128)(2,1)S(1)} %merge.2), channel_id=1, source_target_pairs={{0,2},{1,3},{2,0},{3,1},{4,6},{5,7},{6,4},{7,5},{8,10},{9,11},{10,... | collective-permute-start | bytes 442376 | tf_op jit(solution)/shard_map/ppermute | solution.py:30
  25.7 4.4 %collective-permute-done.6.refs_2_ = bf16[64,1152]{1,0:T(8,128)(2,1)S(1)} collective-permute-done((bf16[64,1152]{1,0:T(8,128)(2,1)S(1)}, bf16[64,1152]{1,0:T(8,128)(2,1)S(1)}, u32[]{:S(2)}, u32[]{:S(2)}) %collective-permute-start.6) | collective-permute-done | bytes 147488 | tf_op jit(solution)/shard_map/ppermute | solution.py:30
  30.1 0.2 merge.3
  30.4 2.3 %collective-permute-start.7 = (bf16[16,1152]{1,0:T(8,128)(2,1)S(1)}, bf16[16,1152]{1,0:T(8,128)(2,1)S(1)}, u32[]{:S(2)}, u32[]{:S(2)}) collective-permute-start(bf16[16,1152]{1,0:T(8,128)(2,1)S(1)} %get-tuple-element.14), channel_id=1, source_target_pairs={{0,12},{1,13},{2,14},{3,15},{4,8},{5,9},{6,10},{7,11},{8,4},{9,5},... | collective-permute-start | bytes 110600 | tf_op jit(solution)/shard_map/ppermute | solution.py:30
  32.6 0.0 collective-permute-start.8
  32.6 2.2 %collective-permute-start.9 = (bf16[16,1152]{1,0:T(8,128)(2,1)S(1)}, bf16[16,1152]{1,0:T(8,128)(2,1)S(1)}, u32[]{:S(2)}, u32[]{:S(2)}) collective-permute-start(bf16[16,1152]{1,0:T(8,128)(2,1)S(1)} %get-tuple-element.16), channel_id=1, source_target_pairs={{0,4},{1,5},{2,6},{3,7},{4,0},{5,1},{6,2},{7,3},{8,12},{9,13},{10,... | collective-permute-start | bytes 110600 | tf_op jit(solution)/shard_map/ppermute | solution.py:30
  34.8 1.4 %collective-permute-done.7.refs_3_ = bf16[16,1152]{1,0:T(8,128)(2,1)S(1)} collective-permute-done((bf16[16,1152]{1,0:T(8,128)(2,1)S(1)}, bf16[16,1152]{1,0:T(8,128)(2,1)S(1)}, u32[]{:S(2)}, u32[]{:S(2)}) %collective-permute-start.7) | collective-permute-done | bytes 36896 | tf_op jit(solution)/shard_map/ppermute | solution.py:30
  36.2 1.3 %collective-permute-done.8.refs_4_ = bf16[16,1152]{1,0:T(8,128)(2,1)S(1)} collective-permute-done((bf16[16,1152]{1,0:T(8,128)(2,1)S(1)}, bf16[16,1152]{1,0:T(8,128)(2,1)S(1)}, u32[]{:S(2)}, u32[]{:S(2)}) %collective-permute-start.8) | collective-permute-done | bytes 36896 | tf_op jit(solution)/shard_map/ppermute | solution.py:30
  37.5 0.0 collective-permute-done.9.refs_5_
  37.5 0.6 %project.1 = (bf16[16,256]{1,0:T(8,128)(2,1)S(1)}, bf16[16,3584]{1,0:T(8,128)(2,1)S(1)}) custom-call(f32[128,1152]{1,0:T(8,128)S(1)} %get-tuple-element.12.refs_0_, bf16[128,1152]{1,0:T(8,128)(2,1)S(1)} %collective-permute-done.5.refs_1_, bf16[64,1152]{1,0:T(8,128)(2,1)S(1)} %collective-permute-done.6.refs_2_, ...), custom_call_target="tpu_custom_call" | custom-call | bytes 5197824 | tf_op jit(solution)/shard_map/project/pallas_call | solution.py:39
  38.2 0.0 collective-permute-start.10
  38.2 0.4 rest.1
  38.6 1.0 %collective-permute-done.10 = bf16[16,3584]{1,0:T(8,128)(2,1)S(1)} collective-permute-done((bf16[16,3584]{1,0:T(8,128)(2,1)S(1)}, bf16[16,3584]{1,0:T(8,128)(2,1)S(1)}, u32[]{:S(2)}, u32[]{:S(2)}) %collective-permute-start.10) | collective-permute-done | bytes 114720 | tf_op jit(solution)/shard_map/ppermute | solution.py:30
  39.6 1.6 %collective-permute-start.11 = (bf16[16,1792]{1,0:T(8,128)(2,1)S(1)}, bf16[16,1792]{1,0:T(8,128)(2,1)S(1)}, u32[]{:S(2)}, u32[]{:S(2)}) collective-permute-start(bf16[16,1792]{1,0:T(8,128)(2,1)S(1)} %slice.15), channel_id=1, source_target_pairs={{0,2},{1,3},{2,0},{3,1},{4,6},{5,7},{6,4},{7,5},{8,10},{9,11},{10,... | collective-permute-start | bytes 172040 | tf_op jit(solution)/shard_map/ppermute | solution.py:30
  41.1 2.7 %collective-permute-done.11 = bf16[16,1792]{1,0:T(8,128)(2,1)S(1)} collective-permute-done((bf16[16,1792]{1,0:T(8,128)(2,1)S(1)}, bf16[16,1792]{1,0:T(8,128)(2,1)S(1)}, u32[]{:S(2)}, u32[]{:S(2)}) %collective-permute-start.11) | collective-permute-done | bytes 57376 | tf_op jit(solution)/shard_map/ppermute | solution.py:30
  43.8 2.1 %collective-permute-start.14 = (bf16[16,1792]{1,0:T(8,128)(2,1)S(1)}, bf16[16,1792]{1,0:T(8,128)(2,1)S(1)}, u32[]{:S(2)}, u32[]{:S(2)}) collective-permute-start(bf16[16,1792]{1,0:T(8,128)(2,1)S(1)} %fusion), channel_id=1, source_target_pairs={{0,12},{1,13},{2,14},{3,15},{4,8},{5,9},{6,10},{7,11},{8,4},{9,5},... | collective-permute-start | bytes 172040 | tf_op jit(solution)/shard_map/ppermute | solution.py:30
  45.9 0.7 %collective-permute-start.13 = (bf16[16,1792]{1,0:T(8,128)(2,1)S(1)}, bf16[16,1792]{1,0:T(8,128)(2,1)S(1)}, u32[]{:S(2)}, u32[]{:S(2)}) collective-permute-start(bf16[16,1792]{1,0:T(8,128)(2,1)S(1)} %fusion), channel_id=1, source_target_pairs={{0,8},{1,9},{2,10},{3,11},{4,12},{5,13},{6,14},{7,15},{8,0},{9,1},... | collective-permute-start | bytes 172040 | tf_op jit(solution)/shard_map/ppermute | solution.py:30
  46.6 1.7 %collective-permute-start.12 = (bf16[16,1792]{1,0:T(8,128)(2,1)S(1)}, bf16[16,1792]{1,0:T(8,128)(2,1)S(1)}, u32[]{:S(2)}, u32[]{:S(2)}) collective-permute-start(bf16[16,1792]{1,0:T(8,128)(2,1)S(1)} %fusion), channel_id=1, source_target_pairs={{0,4},{1,5},{2,6},{3,7},{4,0},{5,1},{6,2},{7,3},{8,12},{9,13},{10,... | collective-permute-start | bytes 172040 | tf_op jit(solution)/shard_map/ppermute | solution.py:30
  48.3 2.1 %collective-permute-done.14 = bf16[16,1792]{1,0:T(8,128)(2,1)S(1)} collective-permute-done((bf16[16,1792]{1,0:T(8,128)(2,1)S(1)}, bf16[16,1792]{1,0:T(8,128)(2,1)S(1)}, u32[]{:S(2)}, u32[]{:S(2)}) %collective-permute-start.14) | collective-permute-done | bytes 57376 | tf_op jit(solution)/shard_map/ppermute | solution.py:30
  50.4 1.4 %collective-permute-done.13 = bf16[16,1792]{1,0:T(8,128)(2,1)S(1)} collective-permute-done((bf16[16,1792]{1,0:T(8,128)(2,1)S(1)}, bf16[16,1792]{1,0:T(8,128)(2,1)S(1)}, u32[]{:S(2)}, u32[]{:S(2)}) %collective-permute-start.13) | collective-permute-done | bytes 57376 | tf_op jit(solution)/shard_map/ppermute | solution.py:30
  51.8 0.0 collective-permute-done.12
  51.8 1.6 %collective-permute-start.15 = (bf16[16,1792]{1,0:T(8,128)(2,1)S(1)}, bf16[16,1792]{1,0:T(8,128)(2,1)S(1)}, u32[]{:S(2)}, u32[]{:S(2)}) collective-permute-start(bf16[16,1792]{1,0:T(8,128)(2,1)S(1)} %add_convert_fusion), channel_id=1, source_target_pairs={{0,2},{1,3},{2,0},{3,1},{4,6},{5,7},{6,4},{7,5},{8,10},{9,11},{10,... | collective-permute-start | bytes 172040 | tf_op jit(solution)/shard_map/ppermute | solution.py:30
  53.4 2.7 %collective-permute-done.15 = bf16[16,1792]{1,0:T(8,128)(2,1)S(1)} collective-permute-done((bf16[16,1792]{1,0:T(8,128)(2,1)S(1)}, bf16[16,1792]{1,0:T(8,128)(2,1)S(1)}, u32[]{:S(2)}, u32[]{:S(2)}) %collective-permute-start.15) | collective-permute-done | bytes 57376 | tf_op jit(solution)/shard_map/ppermute | solution.py:30
  56.1 0.1 collective-permute-start.16
  56.1 1.3 %collective-permute-done.16.refs_1_ = bf16[16,3584]{1,0:T(8,128)(2,1)S(1)} collective-permute-done((bf16[16,3584]{1,0:T(8,128)(2,1)S(1)}, bf16[16,3584]{1,0:T(8,128)(2,1)S(1)}, u32[]{:S(2)}, u32[]{:S(2)}) %collective-permute-start.16) | collective-permute-done | bytes 114720 | tf_op jit(solution)/shard_map/ppermute | solution.py:30
  57.5 0.7 %place.1 = bf16[16,7168]{1,0:T(8,128)(2,1)} custom-call(bf16[16,3584]{1,0:T(8,128)(2,1)S(1)} %pad_maximum_fusion.refs_0_, bf16[16,3584]{1,0:T(8,128)(2,1)S(1)} %collective-permute-done.16.refs_1_), custom_call_target="tpu_custom_call" | custom-call | tf_op jit(solution)/shard_map/place/pallas_call | solution.py:396
  (21 shorter events, 0.2 us)
Async XLA Ops:
  0.0 0.9 %copy-start.4 = (bf16[2,128,512]{2,1,0:T(8,128)(2,1)S(1)}, bf16[2,128,512]{2,1,0:T(8,128)(2,1)}, u32[]{:S(2)}) copy-start(bf16[2,128,512]{2,1,0:T(8,128)(2,1)} %key_ref.1) | copy-start | bytes 786436
  0.0 1.1 %copy-start.2 = (bf16[1536,128]{1,0:T(8,128)(2,1)S(1)}, bf16[1536,128]{1,0:T(8,128)(2,1)}, u32[]{:S(2)}) copy-start(bf16[1536,128]{1,0:T(8,128)(2,1)} %rope_ref.1) | copy-start | bytes 1179652
  0.0 1.3 %copy-start.1 = (bf16[1536,256]{1,0:T(8,128)(2,1)S(1)}, bf16[1536,256]{1,0:T(8,128)(2,1)}, u32[]{:S(2)}) copy-start(bf16[1536,256]{1,0:T(8,128)(2,1)} %nope_ref.1) | copy-start | bytes 2359300
  0.0 1.3 %copy-start.6 = (bf16[1536]{0:T(1024)(128)(2,1)S(1)}, bf16[1536]{0:T(1024)(128)(2,1)}, u32[]{:S(2)}) copy-start(bf16[1536]{0:T(1024)(128)(2,1)} %gain_ref.1) | copy-start | bytes 9220
  0.0 1.3 %copy-start.5 = (bf16[16,1536]{1,0:T(8,128)(2,1)S(1)}, bf16[16,1536]{1,0:T(8,128)(2,1)}, u32[]{:S(2)}) copy-start(bf16[16,1536]{1,0:T(8,128)(2,1)} %x_ref.1) | copy-start | bytes 147460
  1.9 5.0 %collective-permute-start = (bf16[16,1152]{1,0:T(8,128)(2,1)S(1)}, bf16[16,1152]{1,0:T(8,128)(2,1)S(1)}, u32[]{:S(2)}, u32[]{:S(2)}) collective-permute-start(bf16[16,1152]{1,0:T(8,128)(2,1)S(1)} %query.1), channel_id=1, source_target_pairs={{0,2},{1,3},{2,0},{3,1},{4,6},{5,7},{6,4},{7,5},{8,10},{9,11},{10,... | collective-permute-start | bytes 110600 | tf_op jit(solution)/shard_map/ppermute | solution.py:30
  6.8 11.5 %copy-start.7 = (bf16[2,2048,512]{2,1,0:T(8,128)(2,1)S(1)}, bf16[2,2048,512]{2,1,0:T(8,128)(2,1)}, u32[]{:S(2)}) copy-start(bf16[2,2048,512]{2,1,0:T(8,128)(2,1)} %refs_4_.1) | copy-start | bytes 12582916
  6.9 11.5 %copy-start.8 = (bf16[2,64,2048]{2,1,0:T(8,128)(2,1)S(1)}, bf16[2,64,2048]{2,1,0:T(8,128)(2,1)}, u32[]{:S(2)}) copy-start(bf16[2,64,2048]{2,1,0:T(8,128)(2,1)} %refs_5_.1) | copy-start | bytes 1572868
  6.9 11.5 %copy-start.9 = (s32[2]{0:T(128)S(1)}, s32[2]{0:T(128)}, u32[]{:S(2)}) copy-start(s32[2]{0:T(128)} %refs_0_.1) | copy-start | bytes 28
  6.9 6.8 %collective-permute-start.3 = (bf16[32,1152]{1,0:T(8,128)(2,1)S(1)}, bf16[32,1152]{1,0:T(8,128)(2,1)S(1)}, u32[]{:S(2)}, u32[]{:S(2)}) collective-permute-start(bf16[32,1152]{1,0:T(8,128)(2,1)S(1)} %pad_maximum_fusion.1.refs_0_), channel_id=1, source_target_pairs={{0,12},{1,13},{2,14},{3,15},{4,8},{5,9},{6,10},{7,11},{8,4},{9,5},... | collective-permute-start | bytes 221192 | tf_op jit(solution)/shard_map/ppermute | solution.py:30
  11.0 5.6 %collective-permute-start.2 = (bf16[32,1152]{1,0:T(8,128)(2,1)S(1)}, bf16[32,1152]{1,0:T(8,128)(2,1)S(1)}, u32[]{:S(2)}, u32[]{:S(2)}) collective-permute-start(bf16[32,1152]{1,0:T(8,128)(2,1)S(1)} %pad_maximum_fusion.1.refs_0_), channel_id=1, source_target_pairs={{0,8},{1,9},{2,10},{3,11},{4,12},{5,13},{6,14},{7,15},{8,0},{9,1},... | collective-permute-start | bytes 221192 | tf_op jit(solution)/shard_map/ppermute | solution.py:30
  11.1 5.6 %collective-permute-start.1 = (bf16[32,1152]{1,0:T(8,128)(2,1)S(1)}, bf16[32,1152]{1,0:T(8,128)(2,1)S(1)}, u32[]{:S(2)}, u32[]{:S(2)}) collective-permute-start(bf16[32,1152]{1,0:T(8,128)(2,1)S(1)} %pad_maximum_fusion.1.refs_0_), channel_id=1, source_target_pairs={{0,4},{1,5},{2,6},{3,7},{4,0},{5,1},{6,2},{7,3},{8,12},{9,13},{10,... | collective-permute-start | bytes 221192 | tf_op jit(solution)/shard_map/ppermute | solution.py:30
  16.7 20.8 %copy-start = (bf16[256,7168]{1,0:T(8,128)(2,1)S(1)}, bf16[256,7168]{1,0:T(8,128)(2,1)}, u32[]{:S(2)}) copy-start(bf16[256,7168]{1,0:T(8,128)(2,1)} %weight_ref.1) | copy-start | bytes 11010052
  16.7 20.8 %copy-start.3 = (bf16[2,512,128]{2,1,0:T(8,128)(2,1)S(1)}, bf16[2,512,128]{2,1,0:T(8,128)(2,1)}, u32[]{:S(2)}) copy-start(bf16[2,512,128]{2,1,0:T(8,128)(2,1)} %refs_6_.1) | copy-start | bytes 786436
  16.7 1.6 %collective-permute-start.4 = (bf16[128,1152]{1,0:T(8,128)(2,1)S(1)}, bf16[128,1152]{1,0:T(8,128)(2,1)S(1)}, u32[]{:S(2)}, u32[]{:S(2)}) collective-permute-start(bf16[128,1152]{1,0:T(8,128)(2,1)S(1)} %join.1.refs_2_), channel_id=1, source_target_pairs={{0,1},{1,0},{2,3},{3,2},{4,5},{5,4},{6,7},{7,6},{8,9},{9,8},{10,11... | collective-permute-start | bytes 884744 | tf_op jit(solution)/shard_map/ppermute | solution.py:30
  22.3 1.6 %collective-permute-start.5 = (bf16[128,1152]{1,0:T(8,128)(2,1)S(1)}, bf16[128,1152]{1,0:T(8,128)(2,1)S(1)}, u32[]{:S(2)}, u32[]{:S(2)}) collective-permute-start(bf16[128,1152]{1,0:T(8,128)(2,1)S(1)} %get-tuple-element.13), channel_id=1, source_target_pairs={{0,1},{1,0},{2,3},{3,2},{4,5},{5,4},{6,7},{7,6},{8,9},{9,8},{10,11... | collective-permute-start | bytes 884744 | tf_op jit(solution)/shard_map/ppermute | solution.py:30
  24.2 6.0 %collective-permute-start.6 = (bf16[64,1152]{1,0:T(8,128)(2,1)S(1)}, bf16[64,1152]{1,0:T(8,128)(2,1)S(1)}, u32[]{:S(2)}, u32[]{:S(2)}) collective-permute-start(bf16[64,1152]{1,0:T(8,128)(2,1)S(1)} %merge.2), channel_id=1, source_target_pairs={{0,2},{1,3},{2,0},{3,1},{4,6},{5,7},{6,4},{7,5},{8,10},{9,11},{10,... | collective-permute-start | bytes 442376 | tf_op jit(solution)/shard_map/ppermute | solution.py:30
  30.4 5.8 %collective-permute-start.7 = (bf16[16,1152]{1,0:T(8,128)(2,1)S(1)}, bf16[16,1152]{1,0:T(8,128)(2,1)S(1)}, u32[]{:S(2)}, u32[]{:S(2)}) collective-permute-start(bf16[16,1152]{1,0:T(8,128)(2,1)S(1)} %get-tuple-element.14), channel_id=1, source_target_pairs={{0,12},{1,13},{2,14},{3,15},{4,8},{5,9},{6,10},{7,11},{8,4},{9,5},... | collective-permute-start | bytes 110600 | tf_op jit(solution)/shard_map/ppermute | solution.py:30
  32.6 4.9 %collective-permute-start.8 = (bf16[16,1152]{1,0:T(8,128)(2,1)S(1)}, bf16[16,1152]{1,0:T(8,128)(2,1)S(1)}, u32[]{:S(2)}, u32[]{:S(2)}) collective-permute-start(bf16[16,1152]{1,0:T(8,128)(2,1)S(1)} %get-tuple-element.15), channel_id=1, source_target_pairs={{0,8},{1,9},{2,10},{3,11},{4,12},{5,13},{6,14},{7,15},{8,0},{9,1},... | collective-permute-start | bytes 110600 | tf_op jit(solution)/shard_map/ppermute | solution.py:30
  32.6 4.9 %collective-permute-start.9 = (bf16[16,1152]{1,0:T(8,128)(2,1)S(1)}, bf16[16,1152]{1,0:T(8,128)(2,1)S(1)}, u32[]{:S(2)}, u32[]{:S(2)}) collective-permute-start(bf16[16,1152]{1,0:T(8,128)(2,1)S(1)} %get-tuple-element.16), channel_id=1, source_target_pairs={{0,4},{1,5},{2,6},{3,7},{4,0},{5,1},{6,2},{7,3},{8,12},{9,13},{10,... | collective-permute-start | bytes 110600 | tf_op jit(solution)/shard_map/ppermute | solution.py:30
  38.2 1.4 %collective-permute-start.10 = (bf16[16,3584]{1,0:T(8,128)(2,1)S(1)}, bf16[16,3584]{1,0:T(8,128)(2,1)S(1)}, u32[]{:S(2)}, u32[]{:S(2)}) collective-permute-start(bf16[16,3584]{1,0:T(8,128)(2,1)S(1)} %get-tuple-element.18), channel_id=1, source_target_pairs={{0,1},{1,0},{2,3},{3,2},{4,5},{5,4},{6,7},{7,6},{8,9},{9,8},{10,11... | collective-permute-start | bytes 344072 | tf_op jit(solution)/shard_map/ppermute | solution.py:30
  39.6 4.2 %collective-permute-start.11 = (bf16[16,1792]{1,0:T(8,128)(2,1)S(1)}, bf16[16,1792]{1,0:T(8,128)(2,1)S(1)}, u32[]{:S(2)}, u32[]{:S(2)}) collective-permute-start(bf16[16,1792]{1,0:T(8,128)(2,1)S(1)} %slice.15), channel_id=1, source_target_pairs={{0,2},{1,3},{2,0},{3,1},{4,6},{5,7},{6,4},{7,5},{8,10},{9,11},{10,... | collective-permute-start | bytes 172040 | tf_op jit(solution)/shard_map/ppermute | solution.py:30
  43.8 6.6 %collective-permute-start.14 = (bf16[16,1792]{1,0:T(8,128)(2,1)S(1)}, bf16[16,1792]{1,0:T(8,128)(2,1)S(1)}, u32[]{:S(2)}, u32[]{:S(2)}) collective-permute-start(bf16[16,1792]{1,0:T(8,128)(2,1)S(1)} %fusion), channel_id=1, source_target_pairs={{0,12},{1,13},{2,14},{3,15},{4,8},{5,9},{6,10},{7,11},{8,4},{9,5},... | collective-permute-start | bytes 172040 | tf_op jit(solution)/shard_map/ppermute | solution.py:30
  45.9 5.9 %collective-permute-start.13 = (bf16[16,1792]{1,0:T(8,128)(2,1)S(1)}, bf16[16,1792]{1,0:T(8,128)(2,1)S(1)}, u32[]{:S(2)}, u32[]{:S(2)}) collective-permute-start(bf16[16,1792]{1,0:T(8,128)(2,1)S(1)} %fusion), channel_id=1, source_target_pairs={{0,8},{1,9},{2,10},{3,11},{4,12},{5,13},{6,14},{7,15},{8,0},{9,1},... | collective-permute-start | bytes 172040 | tf_op jit(solution)/shard_map/ppermute | solution.py:30
  46.6 5.2 %collective-permute-start.12 = (bf16[16,1792]{1,0:T(8,128)(2,1)S(1)}, bf16[16,1792]{1,0:T(8,128)(2,1)S(1)}, u32[]{:S(2)}, u32[]{:S(2)}) collective-permute-start(bf16[16,1792]{1,0:T(8,128)(2,1)S(1)} %fusion), channel_id=1, source_target_pairs={{0,4},{1,5},{2,6},{3,7},{4,0},{5,1},{6,2},{7,3},{8,12},{9,13},{10,... | collective-permute-start | bytes 172040 | tf_op jit(solution)/shard_map/ppermute | solution.py:30
  51.8 4.2 %collective-permute-start.15 = (bf16[16,1792]{1,0:T(8,128)(2,1)S(1)}, bf16[16,1792]{1,0:T(8,128)(2,1)S(1)}, u32[]{:S(2)}, u32[]{:S(2)}) collective-permute-start(bf16[16,1792]{1,0:T(8,128)(2,1)S(1)} %add_convert_fusion), channel_id=1, source_target_pairs={{0,2},{1,3},{2,0},{3,1},{4,6},{5,7},{6,4},{7,5},{8,10},{9,11},{10,... | collective-permute-start | bytes 172040 | tf_op jit(solution)/shard_map/ppermute | solution.py:30
  56.1 1.4 %collective-permute-start.16 = (bf16[16,3584]{1,0:T(8,128)(2,1)S(1)}, bf16[16,3584]{1,0:T(8,128)(2,1)S(1)}, u32[]{:S(2)}, u32[]{:S(2)}) collective-permute-start(bf16[16,3584]{1,0:T(8,128)(2,1)S(1)} %pad_maximum_fusion.refs_0_), channel_id=1, source_target_pairs={{0,1},{1,0},{2,3},{3,2},{4,5},{5,4},{6,7},{7,6},{8,9},{9,8},{10,11... | collective-permute-start | bytes 344072 | tf_op jit(solution)/shard_map/ppermute | solution.py:30

commit v8 on v7

--- a/solution.py
+++ b/solution.py
@@ -260,27 +260,40 @@
         at += r.shape[0]
 
 
-def place_body(parts_out, *refs):
-    pieces, out_ref, sems = refs[:-2], refs[-2], refs[-1]
-    copies = []
+def place_body(parts_out, order, piece, *refs):
+    out_ref, sems = refs[-2:]
     mine = lax.rem(lax.axis_index("ctx"), parts_out)
     width = out_ref.shape[1] // parts_out
-    e_order = (0, 2, 1, 3)
-    at = 0
-    for piece in pieces:
-        for k in range(piece.shape[1] // width):
-            start = pl.multiple_of(jnp.bitwise_xor(mine, e_order[at]) * width, LANES)
-            copies.append(
-                pltpu.make_async_copy(
-                    piece.at[:, pl.ds(k * width, width)],
-                    out_ref.at[:, pl.ds(start, width)],
-                    sems.at[at],
-                )
+    copies = []
+    for k, e in enumerate(order):
+        start = pl.multiple_of(jnp.bitwise_xor(mine, e) * width, LANES)
+        copies.append(
+            pltpu.make_async_copy(
+                piece.at[:, pl.ds(k * width, width)],
+                out_ref.at[:, pl.ds(start, width)],
+                sems.at[k],
             )
-            copies[-1].start()
-            at += 1
+        )
+        copies[-1].start()
     for copy in copies:
         copy.wait()
+
+
+def place(parts_out, order, piece, shape, into=()):
+    return pl.pallas_call(
+        functools.partial(place_body, parts_out, order),
+        out_shape=shape,
+        in_specs=[pl.BlockSpec(memory_space=pltpu.VMEM)]
+        + [pl.BlockSpec(memory_space=pl.ANY)] * len(into),
+        out_specs=pl.BlockSpec(memory_space=pl.ANY),
+        scratch_shapes=[pltpu.SemaphoreType.DMA((len(order),))],
+        input_output_aliases={1: 0} if into else {},
+        compiler_params=pltpu.CompilerParams(vmem_limit_bytes=16 << 20),
+        cost_estimate=pl.CostEstimate(
+            flops=0, bytes_accessed=2 * piece.size * 2, transcendentals=0
+        ),
+        name="place",
+    )(piece, *into)
 
 
 def local(count, query_input, query_gain, nope_weight, rope_weight, key_up, value_up, out_weight,
@@ -393,15 +406,9 @@
     done = kept.astype(BF16)
     both = jnp.concatenate([done, swap(done, count, stages[1][0])], axis=1)
     other = swap(both, count, stages[0][0])
-    return pl.pallas_call(
-        functools.partial(place_body, parts_out),
-        out_shape=spec((rows, model), BF16),
-        in_specs=[pl.BlockSpec(memory_space=pltpu.VMEM)] * 2,
-        out_specs=pl.BlockSpec(memory_space=pl.ANY),
-        scratch_shapes=[pltpu.SemaphoreType.DMA((parts_out,))],
-        compiler_params=pltpu.CompilerParams(vmem_limit_bytes=16 << 20),
-        name="place",
-    )(both, other)
+    shape = spec((rows, model), BF16)
+    first = place(parts_out, (0, 2), both, shape)
+    return place(parts_out, (1, 3), other, shape, (first,))
 
 
 def solution(mesh):

time: 58.3 us -> 58.3 us (level)
  waiting for transfers between devices: 28.1 us -> 27.4 us
  Pallas kernels: 6.64 us -> 7.25 us
    ppermute x17, waiting for transfers between devices: 28.1 us -> 27.4 us  [swap(): return lax.ppermute(x, 'ctx', [(i, i ^ mask) for i in range(count)])]
    pallas_call x1 -> x2, Pallas kernels: 0.71 us -> 1.33 us  [place(): pl.pallas_call(functools.partial(place_body, parts_out, order), out_shape...]
  transfers between devices with their start and end apart: 17 -> 17, of which waited for: 14 -> 14; matrix products, arithmetic and copies ran while one was open for 0% -> 0% of each run, Pallas kernels for 1% -> 2%
where the time goes in v8:
time: 58.3 us; the launch traced here: 58.1 us
  waiting for transfers between devices  27.4 us (47%)
  starting transfers between devices  21.9 us (38%)
  Pallas kernels  7.25 us (12%)
  local copies, waits for them, and re-layouts  1.35 us (2%)
    ppermute x17, waiting for transfers between devices, swap(): return lax.ppermute(x, 'ctx', [(i, i ^ mask) for i in range(count)])  27.4 us
    ppermute x17, starting transfers between devices, swap(): return lax.ppermute(x, 'ctx', [(i, i ^ mask) for i in range(count)])  21.9 us
    pallas_call x1, Pallas kernels, local(): pl.pallas_call(functools.partial(attend_body, 2, reqs, latent, rope_width...  3.87 us
    pallas_call x7, Pallas kernels, call(): pl.pallas_call(body, out_shape=tuple(outs), in_specs=specs, out_specs=tup...  2.06 us
    unnamed x20, local copies, waits for them, and re-layouts  1.34 us
    pallas_call x2, Pallas kernels, place(): pl.pallas_call(functools.partial(place_body, parts_out, order), out_shape...  1.33 us
  transfers between devices with their start and end apart: 17, of which 14 were waited for; matrix products, arithmetic and copies ran while one was open for 0% of the time, Pallas kernels for 2%

profile of v8, /device:TPU:0, one launch (start us, length us, event | category | flops | bytes accessed | tf_op | source)
XLA Modules:
  0.0 58.1 jit_solution(9786449094848524075)
XLA Ops:
  0.0 0.9 %copy-done.4 = bf16[2,128,512]{2,1,0:T(8,128)(2,1)S(1)} copy-done((bf16[2,128,512]{2,1,0:T(8,128)(2,1)S(1)}, bf16[2,128,512]{2,1,0:T(8,128)(2,1)}, u32[]{:S(2)}) %copy-start.4) | copy-done | bytes 262168
  1.0 0.1 copy-done.2
  1.1 0.3 copy-done.1
  1.3 0.5 query.1
  1.9 3.0 %collective-permute-start = (bf16[16,1152]{1,0:T(8,128)(2,1)S(1)}, bf16[16,1152]{1,0:T(8,128)(2,1)S(1)}, u32[]{:S(2)}, u32[]{:S(2)}) collective-permute-start(bf16[16,1152]{1,0:T(8,128)(2,1)S(1)} %query.1), channel_id=1, source_target_pairs={{0,2},{1,3},{2,0},{3,1},{4,6},{5,7},{6,4},{7,5},{8,10},{9,11},{10,... | collective-permute-start | bytes 110600 | tf_op jit(solution)/shard_map/ppermute | solution.py:30
  4.9 1.9 %collective-permute-done = bf16[16,1152]{1,0:T(8,128)(2,1)S(1)} collective-permute-done((bf16[16,1152]{1,0:T(8,128)(2,1)S(1)}, bf16[16,1152]{1,0:T(8,128)(2,1)S(1)}, u32[]{:S(2)}, u32[]{:S(2)}) %collective-permute-start) | collective-permute-done | bytes 36896 | tf_op jit(solution)/shard_map/ppermute | solution.py:30
  6.9 0.0 copy-start.8
  6.9 0.0 copy-start.9
  6.9 4.2 %collective-permute-start.3 = (bf16[32,1152]{1,0:T(8,128)(2,1)S(1)}, bf16[32,1152]{1,0:T(8,128)(2,1)S(1)}, u32[]{:S(2)}, u32[]{:S(2)}) collective-permute-start(bf16[32,1152]{1,0:T(8,128)(2,1)S(1)} %pad_maximum_fusion.1.refs_0_), channel_id=1, source_target_pairs={{0,12},{1,13},{2,14},{3,15},{4,8},{5,9},{6,10},{7,11},{8,4},{9,5},... | collective-permute-start | bytes 221192 | tf_op jit(solution)/shard_map/ppermute | solution.py:30
  11.0 0.0 collective-permute-start.2
  11.1 0.6 %collective-permute-start.1 = (bf16[32,1152]{1,0:T(8,128)(2,1)S(1)}, bf16[32,1152]{1,0:T(8,128)(2,1)S(1)}, u32[]{:S(2)}, u32[]{:S(2)}) collective-permute-start(bf16[32,1152]{1,0:T(8,128)(2,1)S(1)} %pad_maximum_fusion.1.refs_0_), channel_id=1, source_target_pairs={{0,4},{1,5},{2,6},{3,7},{4,0},{5,1},{6,2},{7,3},{8,12},{9,13},{10,... | collective-permute-start | bytes 221192 | tf_op jit(solution)/shard_map/ppermute | solution.py:30
  11.7 1.9 %collective-permute-done.3.refs_3_ = bf16[32,1152]{1,0:T(8,128)(2,1)S(1)} collective-permute-done((bf16[32,1152]{1,0:T(8,128)(2,1)S(1)}, bf16[32,1152]{1,0:T(8,128)(2,1)S(1)}, u32[]{:S(2)}, u32[]{:S(2)}) %collective-permute-start.3) | collective-permute-done | bytes 73760 | tf_op jit(solution)/shard_map/ppermute | solution.py:30
  13.6 3.0 %collective-permute-done.2.refs_2_ = bf16[32,1152]{1,0:T(8,128)(2,1)S(1)} collective-permute-done((bf16[32,1152]{1,0:T(8,128)(2,1)S(1)}, bf16[32,1152]{1,0:T(8,128)(2,1)S(1)}, u32[]{:S(2)}, u32[]{:S(2)}) %collective-permute-start.2) | collective-permute-done | bytes 73760 | tf_op jit(solution)/shard_map/ppermute | solution.py:30
  16.7 0.0 collective-permute-done.1.refs_1_
  16.7 0.0 copy-start
  16.7 0.0 copy-start.3
  16.7 0.1 collective-permute-start.4
  16.8 1.6 %collective-permute-done.4.refs_3_ = bf16[128,1152]{1,0:T(8,128)(2,1)S(1)} collective-permute-done((bf16[128,1152]{1,0:T(8,128)(2,1)S(1)}, bf16[128,1152]{1,0:T(8,128)(2,1)S(1)}, u32[]{:S(2)}, u32[]{:S(2)}) %collective-permute-start.4) | collective-permute-done | bytes 294944 | tf_op jit(solution)/shard_map/ppermute | solution.py:30
  18.4 3.9 %attend.1 = (f32[128,1152]{1,0:T(8,128)S(1)}, bf16[128,1152]{1,0:T(8,128)(2,1)S(1)}) custom-call(s32[2]{0:T(128)S(1)} %copy-done.9, s32[8,256]{1,0:T(8,128)S(1)} %table.1.table_ref.refs_1_, bf16[128,1152]{1,0:T(8,128)(2,1)S(1)} %join.1.refs_2_, bf16[128,1152]{1,0:T(8,128)(2,1)S(1)} %collective-permute-done.4.refs_3_, bf16[2,2048,512]{2,1,0:T(8,128)(2,1)S(1)} %copy-done.7, ...), custom_call_target="tpu_custom_call" | custom-call | flops 2147483648 | bytes 8388608 | tf_op jit(solution)/shard_map/attend/pallas_call | solution.py:345
  22.3 0.2 collective-permute-start.5
  22.5 1.5 %collective-permute-done.5.refs_1_ = bf16[128,1152]{1,0:T(8,128)(2,1)S(1)} collective-permute-done((bf16[128,1152]{1,0:T(8,128)(2,1)S(1)}, bf16[128,1152]{1,0:T(8,128)(2,1)S(1)}, u32[]{:S(2)}, u32[]{:S(2)}) %collective-permute-start.5) | collective-permute-done | bytes 294944 | tf_op jit(solution)/shard_map/ppermute | solution.py:30
  23.9 0.2 merge.2
  24.2 1.6 %collective-permute-start.6 = (bf16[64,1152]{1,0:T(8,128)(2,1)S(1)}, bf16[64,1152]{1,0:T(8,128)(2,1)S(1)}, u32[]{:S(2)}, u32[]{:S(2)}) collective-permute-start(bf16[64,1152]{1,0:T(8,128)(2,1)S(1)} %merge.2), channel_id=1, source_target_pairs={{0,2},{1,3},{2,0},{3,1},{4,6},{5,7},{6,4},{7,5},{8,10},{9,11},{10,... | collective-permute-start | bytes 442376 | tf_op jit(solution)/shard_map/ppermute | solution.py:30
  25.7 4.4 %collective-permute-done.6.refs_2_ = bf16[64,1152]{1,0:T(8,128)(2,1)S(1)} collective-permute-done((bf16[64,1152]{1,0:T(8,128)(2,1)S(1)}, bf16[64,1152]{1,0:T(8,128)(2,1)S(1)}, u32[]{:S(2)}, u32[]{:S(2)}) %collective-permute-start.6) | collective-permute-done | bytes 147488 | tf_op jit(solution)/shard_map/ppermute | solution.py:30
  30.1 0.2 merge.3
  30.4 2.3 %collective-permute-start.7 = (bf16[16,1152]{1,0:T(8,128)(2,1)S(1)}, bf16[16,1152]{1,0:T(8,128)(2,1)S(1)}, u32[]{:S(2)}, u32[]{:S(2)}) collective-permute-start(bf16[16,1152]{1,0:T(8,128)(2,1)S(1)} %get-tuple-element.14), channel_id=1, source_target_pairs={{0,12},{1,13},{2,14},{3,15},{4,8},{5,9},{6,10},{7,11},{8,4},{9,5},... | collective-permute-start | bytes 110600 | tf_op jit(solution)/shard_map/ppermute | solution.py:30
  32.6 2.2 %collective-permute-start.9 = (bf16[16,1152]{1,0:T(8,128)(2,1)S(1)}, bf16[16,1152]{1,0:T(8,128)(2,1)S(1)}, u32[]{:S(2)}, u32[]{:S(2)}) collective-permute-start(bf16[16,1152]{1,0:T(8,128)(2,1)S(1)} %get-tuple-element.16), channel_id=1, source_target_pairs={{0,4},{1,5},{2,6},{3,7},{4,0},{5,1},{6,2},{7,3},{8,12},{9,13},{10,... | collective-permute-start | bytes 110600 | tf_op jit(solution)/shard_map/ppermute | solution.py:30
  34.8 1.4 %collective-permute-done.7.refs_3_ = bf16[16,1152]{1,0:T(8,128)(2,1)S(1)} collective-permute-done((bf16[16,1152]{1,0:T(8,128)(2,1)S(1)}, bf16[16,1152]{1,0:T(8,128)(2,1)S(1)}, u32[]{:S(2)}, u32[]{:S(2)}) %collective-permute-start.7) | collective-permute-done | bytes 36896 | tf_op jit(solution)/shard_map/ppermute | solution.py:30
  36.2 1.3 %collective-permute-done.8.refs_4_ = bf16[16,1152]{1,0:T(8,128)(2,1)S(1)} collective-permute-done((bf16[16,1152]{1,0:T(8,128)(2,1)S(1)}, bf16[16,1152]{1,0:T(8,128)(2,1)S(1)}, u32[]{:S(2)}, u32[]{:S(2)}) %collective-permute-start.8) | collective-permute-done | bytes 36896 | tf_op jit(solution)/shard_map/ppermute | solution.py:30
  37.5 0.0 collective-permute-done.9.refs_5_
  37.5 0.6 %project.1 = (bf16[16,256]{1,0:T(8,128)(2,1)S(1)}, bf16[16,3584]{1,0:T(8,128)(2,1)S(1)}) custom-call(f32[128,1152]{1,0:T(8,128)S(1)} %get-tuple-element.12.refs_0_, bf16[128,1152]{1,0:T(8,128)(2,1)S(1)} %collective-permute-done.5.refs_1_, bf16[64,1152]{1,0:T(8,128)(2,1)S(1)} %collective-permute-done.6.refs_2_, ...), custom_call_target="tpu_custom_call" | custom-call | bytes 5197824 | tf_op jit(solution)/shard_map/project/pallas_call | solution.py:39
  38.2 0.0 collective-permute-start.10
  38.2 0.4 rest.1
  38.6 1.0 %collective-permute-done.10 = bf16[16,3584]{1,0:T(8,128)(2,1)S(1)} collective-permute-done((bf16[16,3584]{1,0:T(8,128)(2,1)S(1)}, bf16[16,3584]{1,0:T(8,128)(2,1)S(1)}, u32[]{:S(2)}, u32[]{:S(2)}) %collective-permute-start.10) | collective-permute-done | bytes 114720 | tf_op jit(solution)/shard_map/ppermute | solution.py:30
  39.6 1.6 %collective-permute-start.11 = (bf16[16,1792]{1,0:T(8,128)(2,1)S(1)}, bf16[16,1792]{1,0:T(8,128)(2,1)S(1)}, u32[]{:S(2)}, u32[]{:S(2)}) collective-permute-start(bf16[16,1792]{1,0:T(8,128)(2,1)S(1)} %slice.15), channel_id=1, source_target_pairs={{0,2},{1,3},{2,0},{3,1},{4,6},{5,7},{6,4},{7,5},{8,10},{9,11},{10,... | collective-permute-start | bytes 172040 | tf_op jit(solution)/shard_map/ppermute | solution.py:30
  41.1 2.7 %collective-permute-done.11 = bf16[16,1792]{1,0:T(8,128)(2,1)S(1)} collective-permute-done((bf16[16,1792]{1,0:T(8,128)(2,1)S(1)}, bf16[16,1792]{1,0:T(8,128)(2,1)S(1)}, u32[]{:S(2)}, u32[]{:S(2)}) %collective-permute-start.11) | collective-permute-done | bytes 57376 | tf_op jit(solution)/shard_map/ppermute | solution.py:30
  43.8 2.1 %collective-permute-start.14 = (bf16[16,1792]{1,0:T(8,128)(2,1)S(1)}, bf16[16,1792]{1,0:T(8,128)(2,1)S(1)}, u32[]{:S(2)}, u32[]{:S(2)}) collective-permute-start(bf16[16,1792]{1,0:T(8,128)(2,1)S(1)} %fusion), channel_id=1, source_target_pairs={{0,12},{1,13},{2,14},{3,15},{4,8},{5,9},{6,10},{7,11},{8,4},{9,5},... | collective-permute-start | bytes 172040 | tf_op jit(solution)/shard_map/ppermute | solution.py:30
  45.9 0.7 %collective-permute-start.13 = (bf16[16,1792]{1,0:T(8,128)(2,1)S(1)}, bf16[16,1792]{1,0:T(8,128)(2,1)S(1)}, u32[]{:S(2)}, u32[]{:S(2)}) collective-permute-start(bf16[16,1792]{1,0:T(8,128)(2,1)S(1)} %fusion), channel_id=1, source_target_pairs={{0,8},{1,9},{2,10},{3,11},{4,12},{5,13},{6,14},{7,15},{8,0},{9,1},... | collective-permute-start | bytes 172040 | tf_op jit(solution)/shard_map/ppermute | solution.py:30
  46.6 1.7 %collective-permute-start.12 = (bf16[16,1792]{1,0:T(8,128)(2,1)S(1)}, bf16[16,1792]{1,0:T(8,128)(2,1)S(1)}, u32[]{:S(2)}, u32[]{:S(2)}) collective-permute-start(bf16[16,1792]{1,0:T(8,128)(2,1)S(1)} %fusion), channel_id=1, source_target_pairs={{0,4},{1,5},{2,6},{3,7},{4,0},{5,1},{6,2},{7,3},{8,12},{9,13},{10,... | collective-permute-start | bytes 172040 | tf_op jit(solution)/shard_map/ppermute | solution.py:30
  48.3 2.1 %collective-permute-done.14 = bf16[16,1792]{1,0:T(8,128)(2,1)S(1)} collective-permute-done((bf16[16,1792]{1,0:T(8,128)(2,1)S(1)}, bf16[16,1792]{1,0:T(8,128)(2,1)S(1)}, u32[]{:S(2)}, u32[]{:S(2)}) %collective-permute-start.14) | collective-permute-done | bytes 57376 | tf_op jit(solution)/shard_map/ppermute | solution.py:30
  50.4 1.4 %collective-permute-done.13 = bf16[16,1792]{1,0:T(8,128)(2,1)S(1)} collective-permute-done((bf16[16,1792]{1,0:T(8,128)(2,1)S(1)}, bf16[16,1792]{1,0:T(8,128)(2,1)S(1)}, u32[]{:S(2)}, u32[]{:S(2)}) %collective-permute-start.13) | collective-permute-done | bytes 57376 | tf_op jit(solution)/shard_map/ppermute | solution.py:30
  51.8 0.0 collective-permute-done.12
  51.8 1.6 %collective-permute-start.15 = (bf16[16,1792]{1,0:T(8,128)(2,1)S(1)}, bf16[16,1792]{1,0:T(8,128)(2,1)S(1)}, u32[]{:S(2)}, u32[]{:S(2)}) collective-permute-start(bf16[16,1792]{1,0:T(8,128)(2,1)S(1)} %add_convert_fusion), channel_id=1, source_target_pairs={{0,2},{1,3},{2,0},{3,1},{4,6},{5,7},{6,4},{7,5},{8,10},{9,11},{10,... | collective-permute-start | bytes 172040 | tf_op jit(solution)/shard_map/ppermute | solution.py:30
  53.4 2.7 %collective-permute-done.15 = bf16[16,1792]{1,0:T(8,128)(2,1)S(1)} collective-permute-done((bf16[16,1792]{1,0:T(8,128)(2,1)S(1)}, bf16[16,1792]{1,0:T(8,128)(2,1)S(1)}, u32[]{:S(2)}, u32[]{:S(2)}) %collective-permute-start.15) | collective-permute-done | bytes 57376 | tf_op jit(solution)/shard_map/ppermute | solution.py:30
  56.1 0.1 collective-permute-start.16
  56.1 0.7 %place.2.refs_0_ = bf16[16,7168]{1,0:T(8,128)(2,1)} custom-call(bf16[16,3584]{1,0:T(8,128)(2,1)S(1)} %pad_maximum_fusion.piece), custom_call_target="tpu_custom_call" | custom-call | bytes 229376 | tf_op jit(solution)/shard_map/place/pallas_call | solution.py:283
  56.8 0.6 %collective-permute-done.16.piece = bf16[16,3584]{1,0:T(8,128)(2,1)S(1)} collective-permute-done((bf16[16,3584]{1,0:T(8,128)(2,1)S(1)}, bf16[16,3584]{1,0:T(8,128)(2,1)S(1)}, u32[]{:S(2)}, u32[]{:S(2)}) %collective-permute-start.16) | collective-permute-done | bytes 114720 | tf_op jit(solution)/shard_map/ppermute | solution.py:30
  57.5 0.7 %place.3 = bf16[16,7168]{1,0:T(8,128)(2,1)} custom-call(bf16[16,3584]{1,0:T(8,128)(2,1)S(1)} %collective-permute-done.16.piece, bf16[16,7168]{1,0:T(8,128)(2,1)} %place.2.refs_0_), custom_call_target="tpu_custom_call", output_to_operand_aliasing={{}: (1, {})} | custom-call | bytes 229376 | tf_op jit(solution)/shard_map/place/pallas_call | solution.py:283
  (22 shorter events, 0.2 us)
Async XLA Ops:
  0.0 0.9 %copy-start.4 = (bf16[2,128,512]{2,1,0:T(8,128)(2,1)S(1)}, bf16[2,128,512]{2,1,0:T(8,128)(2,1)}, u32[]{:S(2)}) copy-start(bf16[2,128,512]{2,1,0:T(8,128)(2,1)} %key_ref.1) | copy-start | bytes 786436
  0.0 1.1 %copy-start.2 = (bf16[1536,128]{1,0:T(8,128)(2,1)S(1)}, bf16[1536,128]{1,0:T(8,128)(2,1)}, u32[]{:S(2)}) copy-start(bf16[1536,128]{1,0:T(8,128)(2,1)} %rope_ref.1) | copy-start | bytes 1179652
  0.0 1.3 %copy-start.1 = (bf16[1536,256]{1,0:T(8,128)(2,1)S(1)}, bf16[1536,256]{1,0:T(8,128)(2,1)}, u32[]{:S(2)}) copy-start(bf16[1536,256]{1,0:T(8,128)(2,1)} %nope_ref.1) | copy-start | bytes 2359300
  0.0 1.3 %copy-start.6 = (bf16[1536]{0:T(1024)(128)(2,1)S(1)}, bf16[1536]{0:T(1024)(128)(2,1)}, u32[]{:S(2)}) copy-start(bf16[1536]{0:T(1024)(128)(2,1)} %gain_ref.1) | copy-start | bytes 9220
  0.0 1.3 %copy-start.5 = (bf16[16,1536]{1,0:T(8,128)(2,1)S(1)}, bf16[16,1536]{1,0:T(8,128)(2,1)}, u32[]{:S(2)}) copy-start(bf16[16,1536]{1,0:T(8,128)(2,1)} %x_ref.1) | copy-start | bytes 147460
  1.9 5.0 %collective-permute-start = (bf16[16,1152]{1,0:T(8,128)(2,1)S(1)}, bf16[16,1152]{1,0:T(8,128)(2,1)S(1)}, u32[]{:S(2)}, u32[]{:S(2)}) collective-permute-start(bf16[16,1152]{1,0:T(8,128)(2,1)S(1)} %query.1), channel_id=1, source_target_pairs={{0,2},{1,3},{2,0},{3,1},{4,6},{5,7},{6,4},{7,5},{8,10},{9,11},{10,... | collective-permute-start | bytes 110600 | tf_op jit(solution)/shard_map/ppermute | solution.py:30
  6.8 11.5 %copy-start.7 = (bf16[2,2048,512]{2,1,0:T(8,128)(2,1)S(1)}, bf16[2,2048,512]{2,1,0:T(8,128)(2,1)}, u32[]{:S(2)}) copy-start(bf16[2,2048,512]{2,1,0:T(8,128)(2,1)} %refs_4_.1) | copy-start | bytes 12582916
  6.9 11.5 %copy-start.8 = (bf16[2,64,2048]{2,1,0:T(8,128)(2,1)S(1)}, bf16[2,64,2048]{2,1,0:T(8,128)(2,1)}, u32[]{:S(2)}) copy-start(bf16[2,64,2048]{2,1,0:T(8,128)(2,1)} %refs_5_.1) | copy-start | bytes 1572868
  6.9 11.5 %copy-start.9 = (s32[2]{0:T(128)S(1)}, s32[2]{0:T(128)}, u32[]{:S(2)}) copy-start(s32[2]{0:T(128)} %refs_0_.1) | copy-start | bytes 28
  6.9 6.8 %collective-permute-start.3 = (bf16[32,1152]{1,0:T(8,128)(2,1)S(1)}, bf16[32,1152]{1,0:T(8,128)(2,1)S(1)}, u32[]{:S(2)}, u32[]{:S(2)}) collective-permute-start(bf16[32,1152]{1,0:T(8,128)(2,1)S(1)} %pad_maximum_fusion.1.refs_0_), channel_id=1, source_target_pairs={{0,12},{1,13},{2,14},{3,15},{4,8},{5,9},{6,10},{7,11},{8,4},{9,5},... | collective-permute-start | bytes 221192 | tf_op jit(solution)/shard_map/ppermute | solution.py:30
  11.0 5.6 %collective-permute-start.2 = (bf16[32,1152]{1,0:T(8,128)(2,1)S(1)}, bf16[32,1152]{1,0:T(8,128)(2,1)S(1)}, u32[]{:S(2)}, u32[]{:S(2)}) collective-permute-start(bf16[32,1152]{1,0:T(8,128)(2,1)S(1)} %pad_maximum_fusion.1.refs_0_), channel_id=1, source_target_pairs={{0,8},{1,9},{2,10},{3,11},{4,12},{5,13},{6,14},{7,15},{8,0},{9,1},... | collective-permute-start | bytes 221192 | tf_op jit(solution)/shard_map/ppermute | solution.py:30
  11.1 5.6 %collective-permute-start.1 = (bf16[32,1152]{1,0:T(8,128)(2,1)S(1)}, bf16[32,1152]{1,0:T(8,128)(2,1)S(1)}, u32[]{:S(2)}, u32[]{:S(2)}) collective-permute-start(bf16[32,1152]{1,0:T(8,128)(2,1)S(1)} %pad_maximum_fusion.1.refs_0_), channel_id=1, source_target_pairs={{0,4},{1,5},{2,6},{3,7},{4,0},{5,1},{6,2},{7,3},{8,12},{9,13},{10,... | collective-permute-start | bytes 221192 | tf_op jit(solution)/shard_map/ppermute | solution.py:30
  16.7 20.8 %copy-start = (bf16[256,7168]{1,0:T(8,128)(2,1)S(1)}, bf16[256,7168]{1,0:T(8,128)(2,1)}, u32[]{:S(2)}) copy-start(bf16[256,7168]{1,0:T(8,128)(2,1)} %weight_ref.1) | copy-start | bytes 11010052
  16.7 20.8 %copy-start.3 = (bf16[2,512,128]{2,1,0:T(8,128)(2,1)S(1)}, bf16[2,512,128]{2,1,0:T(8,128)(2,1)}, u32[]{:S(2)}) copy-start(bf16[2,512,128]{2,1,0:T(8,128)(2,1)} %refs_6_.1) | copy-start | bytes 786436
  16.7 1.6 %collective-permute-start.4 = (bf16[128,1152]{1,0:T(8,128)(2,1)S(1)}, bf16[128,1152]{1,0:T(8,128)(2,1)S(1)}, u32[]{:S(2)}, u32[]{:S(2)}) collective-permute-start(bf16[128,1152]{1,0:T(8,128)(2,1)S(1)} %join.1.refs_2_), channel_id=1, source_target_pairs={{0,1},{1,0},{2,3},{3,2},{4,5},{5,4},{6,7},{7,6},{8,9},{9,8},{10,11... | collective-permute-start | bytes 884744 | tf_op jit(solution)/shard_map/ppermute | solution.py:30
  22.3 1.6 %collective-permute-start.5 = (bf16[128,1152]{1,0:T(8,128)(2,1)S(1)}, bf16[128,1152]{1,0:T(8,128)(2,1)S(1)}, u32[]{:S(2)}, u32[]{:S(2)}) collective-permute-start(bf16[128,1152]{1,0:T(8,128)(2,1)S(1)} %get-tuple-element.13), channel_id=1, source_target_pairs={{0,1},{1,0},{2,3},{3,2},{4,5},{5,4},{6,7},{7,6},{8,9},{9,8},{10,11... | collective-permute-start | bytes 884744 | tf_op jit(solution)/shard_map/ppermute | solution.py:30
  24.2 6.0 %collective-permute-start.6 = (bf16[64,1152]{1,0:T(8,128)(2,1)S(1)}, bf16[64,1152]{1,0:T(8,128)(2,1)S(1)}, u32[]{:S(2)}, u32[]{:S(2)}) collective-permute-start(bf16[64,1152]{1,0:T(8,128)(2,1)S(1)} %merge.2), channel_id=1, source_target_pairs={{0,2},{1,3},{2,0},{3,1},{4,6},{5,7},{6,4},{7,5},{8,10},{9,11},{10,... | collective-permute-start | bytes 442376 | tf_op jit(solution)/shard_map/ppermute | solution.py:30
  30.4 5.8 %collective-permute-start.7 = (bf16[16,1152]{1,0:T(8,128)(2,1)S(1)}, bf16[16,1152]{1,0:T(8,128)(2,1)S(1)}, u32[]{:S(2)}, u32[]{:S(2)}) collective-permute-start(bf16[16,1152]{1,0:T(8,128)(2,1)S(1)} %get-tuple-element.14), channel_id=1, source_target_pairs={{0,12},{1,13},{2,14},{3,15},{4,8},{5,9},{6,10},{7,11},{8,4},{9,5},... | collective-permute-start | bytes 110600 | tf_op jit(solution)/shard_map/ppermute | solution.py:30
  32.6 4.9 %collective-permute-start.8 = (bf16[16,1152]{1,0:T(8,128)(2,1)S(1)}, bf16[16,1152]{1,0:T(8,128)(2,1)S(1)}, u32[]{:S(2)}, u32[]{:S(2)}) collective-permute-start(bf16[16,1152]{1,0:T(8,128)(2,1)S(1)} %get-tuple-element.15), channel_id=1, source_target_pairs={{0,8},{1,9},{2,10},{3,11},{4,12},{5,13},{6,14},{7,15},{8,0},{9,1},... | collective-permute-start | bytes 110600 | tf_op jit(solution)/shard_map/ppermute | solution.py:30
  32.6 4.9 %collective-permute-start.9 = (bf16[16,1152]{1,0:T(8,128)(2,1)S(1)}, bf16[16,1152]{1,0:T(8,128)(2,1)S(1)}, u32[]{:S(2)}, u32[]{:S(2)}) collective-permute-start(bf16[16,1152]{1,0:T(8,128)(2,1)S(1)} %get-tuple-element.16), channel_id=1, source_target_pairs={{0,4},{1,5},{2,6},{3,7},{4,0},{5,1},{6,2},{7,3},{8,12},{9,13},{10,... | collective-permute-start | bytes 110600 | tf_op jit(solution)/shard_map/ppermute | solution.py:30
  38.2 1.4 %collective-permute-start.10 = (bf16[16,3584]{1,0:T(8,128)(2,1)S(1)}, bf16[16,3584]{1,0:T(8,128)(2,1)S(1)}, u32[]{:S(2)}, u32[]{:S(2)}) collective-permute-start(bf16[16,3584]{1,0:T(8,128)(2,1)S(1)} %get-tuple-element.18), channel_id=1, source_target_pairs={{0,1},{1,0},{2,3},{3,2},{4,5},{5,4},{6,7},{7,6},{8,9},{9,8},{10,11... | collective-permute-start | bytes 344072 | tf_op jit(solution)/shard_map/ppermute | solution.py:30
  39.6 4.2 %collective-permute-start.11 = (bf16[16,1792]{1,0:T(8,128)(2,1)S(1)}, bf16[16,1792]{1,0:T(8,128)(2,1)S(1)}, u32[]{:S(2)}, u32[]{:S(2)}) collective-permute-start(bf16[16,1792]{1,0:T(8,128)(2,1)S(1)} %slice.15), channel_id=1, source_target_pairs={{0,2},{1,3},{2,0},{3,1},{4,6},{5,7},{6,4},{7,5},{8,10},{9,11},{10,... | collective-permute-start | bytes 172040 | tf_op jit(solution)/shard_map/ppermute | solution.py:30
  43.8 6.6 %collective-permute-start.14 = (bf16[16,1792]{1,0:T(8,128)(2,1)S(1)}, bf16[16,1792]{1,0:T(8,128)(2,1)S(1)}, u32[]{:S(2)}, u32[]{:S(2)}) collective-permute-start(bf16[16,1792]{1,0:T(8,128)(2,1)S(1)} %fusion), channel_id=1, source_target_pairs={{0,12},{1,13},{2,14},{3,15},{4,8},{5,9},{6,10},{7,11},{8,4},{9,5},... | collective-permute-start | bytes 172040 | tf_op jit(solution)/shard_map/ppermute | solution.py:30
  45.9 5.9 %collective-permute-start.13 = (bf16[16,1792]{1,0:T(8,128)(2,1)S(1)}, bf16[16,1792]{1,0:T(8,128)(2,1)S(1)}, u32[]{:S(2)}, u32[]{:S(2)}) collective-permute-start(bf16[16,1792]{1,0:T(8,128)(2,1)S(1)} %fusion), channel_id=1, source_target_pairs={{0,8},{1,9},{2,10},{3,11},{4,12},{5,13},{6,14},{7,15},{8,0},{9,1},... | collective-permute-start | bytes 172040 | tf_op jit(solution)/shard_map/ppermute | solution.py:30
  46.6 5.2 %collective-permute-start.12 = (bf16[16,1792]{1,0:T(8,128)(2,1)S(1)}, bf16[16,1792]{1,0:T(8,128)(2,1)S(1)}, u32[]{:S(2)}, u32[]{:S(2)}) collective-permute-start(bf16[16,1792]{1,0:T(8,128)(2,1)S(1)} %fusion), channel_id=1, source_target_pairs={{0,4},{1,5},{2,6},{3,7},{4,0},{5,1},{6,2},{7,3},{8,12},{9,13},{10,... | collective-permute-start | bytes 172040 | tf_op jit(solution)/shard_map/ppermute | solution.py:30
  51.8 4.2 %collective-permute-start.15 = (bf16[16,1792]{1,0:T(8,128)(2,1)S(1)}, bf16[16,1792]{1,0:T(8,128)(2,1)S(1)}, u32[]{:S(2)}, u32[]{:S(2)}) collective-permute-start(bf16[16,1792]{1,0:T(8,128)(2,1)S(1)} %add_convert_fusion), channel_id=1, source_target_pairs={{0,2},{1,3},{2,0},{3,1},{4,6},{5,7},{6,4},{7,5},{8,10},{9,11},{10,... | collective-permute-start | bytes 172040 | tf_op jit(solution)/shard_map/ppermute | solution.py:30
  56.1 1.4 %collective-permute-start.16 = (bf16[16,3584]{1,0:T(8,128)(2,1)S(1)}, bf16[16,3584]{1,0:T(8,128)(2,1)S(1)}, u32[]{:S(2)}, u32[]{:S(2)}) collective-permute-start(bf16[16,3584]{1,0:T(8,128)(2,1)S(1)} %pad_maximum_fusion.piece), channel_id=1, source_target_pairs={{0,1},{1,0},{2,3},{3,2},{4,5},{5,4},{6,7},{7,6},{8,9},{9,8},{10,11... | collective-permute-start | bytes 344072 | tf_op jit(solution)/shard_map/ppermute | solution.py:30
